TPU v7x, 512 devices: a whole 4x8x8 slice. The times are simulated.
512 devices in a mesh: dp: 64 (over z, y), rep: 8 (over x, core).
Axes of the slice: x: 4, y: 8, z: 8, core: 2. Of those that a mesh axis runs over, the one named last changes fastest.
Arguments:
- grads: float32 [64, 64, 256, 256], P('dp', None, 'rep'), may hold values from -5 to 5
- left_root: float32 [64, 2, 256, 256], P('dp', None, 'rep'), may hold values from -0.375 to 0.375
- right_root: float32 [64, 2, 256, 256], P('dp'), may hold values from -0.375 to 0.375
- momentum: float32 [64, 2, 256, 256], P('dp', None, 'rep'), may hold values from -6 to 6
- block_owner: int32 [64], replicated, may hold values from 0 to 63, as said below
- owner_counts: int32 [64], P('dp'), may hold values from 0 to 2, as said below
Outputs:
- update: float32 [64, 256, 256], P('dp', 'rep')
- new_momentum: float32 [64, 2, 256, 256], P('dp', None, 'rep')
Inputs may be any that keep to these rules, and one draw needn't show every extreme that they name: `block_owner`: no owner holds more than 2 blocks and some owner holds exactly 2. owner_counts[o] is the number of blocks b with block_owner[b] = o.
All inputs are finite; a program needn't handle non-finite values.
Results may differ from a plain program's by a relative error of at most 0.00007.
Values sent between devices are 32-bit elements; how exact they have to be, the bound alone decides.
No kernel may reach another device: no remote copies, remote signals or barrier semaphores. Data moves between devices by JAX's collectives and lax.ppermute only.
A program may use at most 64 MiB of HBM per device.

v0:
```python
import jax
import jax.numpy as jnp
from jax import lax
from jax.sharding import PartitionSpec as P

BETA = 0.9
EPS = 1e-06


def on_device(grads, left_root, right_root, momentum, block_owner, owner_counts):
    parts_local = grads[0]
    num_blocks = parts_local.shape[0]
    owners = lax.axis_size("dp")
    per_holder = num_blocks // owners
    slots = left_root.shape[1]
    order = left_root.shape[3]
    holder = lax.axis_index("dp")
    earlier = jnp.arange(num_blocks)[:, None] > jnp.arange(num_blocks)[None, :]
    same_owner = block_owner[:, None] == block_owner[None, :]
    slot_of = jnp.sum((earlier & same_owner).astype(jnp.int32), axis=1)
    owner_hot = (block_owner[:, None] == jnp.arange(owners)[None, :]).astype(jnp.float32)
    slot_hot = (slot_of[:, None] == jnp.arange(slots)[None, :]).astype(jnp.float32)
    mine = (block_owner == holder).astype(jnp.float32)
    chooser = (mine[:, None] * slot_hot).reshape(owners, per_holder, slots)
    summed = lax.psum_scatter(parts_local, "dp", scatter_dimension=0, tiled=True)
    local_owner = lax.dynamic_slice_in_dim(owner_hot, holder * per_holder, per_holder, 0)
    local_slot = lax.dynamic_slice_in_dim(slot_hot, holder * per_holder, per_holder, 0)
    outgoing = jnp.einsum(
        "jd,js,jxy->dsxy", local_owner, local_slot, summed, precision=lax.Precision.HIGHEST
    )
    arrived = lax.all_to_all(outgoing, "dp", split_axis=0, concat_axis=0, tiled=True)
    gradient = jnp.sum(arrived, axis=0)
    lefts = left_root[0]
    rights = right_root[0]
    right_part = jnp.einsum("sak,skc->sac", gradient, rights, precision=lax.Precision.HIGHEST)
    precond = jnp.einsum(
        "sak,skc->sac",
        lefts,
        lax.all_gather(right_part, "rep", axis=1, tiled=True),
        precision=lax.Precision.HIGHEST,
    )
    grad_square, pre_square = lax.psum(
        (jnp.sum(gradient * gradient, axis=(1, 2)), jnp.sum(precond * precond, axis=(1, 2))), "rep"
    )
    entries = order * order
    graft = jnp.sqrt(grad_square / entries) / jnp.sqrt(pre_square / entries + EPS)
    direction = graft[:, None, None] * precond
    moment = momentum[0]
    fresh = BETA * moment + direction
    update_owned = BETA * fresh + direction
    used = jnp.arange(slots) < owner_counts[0]
    new_moment = jnp.where(used[:, None, None], fresh, moment)
    outgoing_back = jnp.einsum(
        "hjs,sab->hjab", chooser, update_owned, precision=lax.Precision.HIGHEST
    )
    returned = lax.all_to_all(outgoing_back, "dp", split_axis=0, concat_axis=0, tiled=True)
    update = jnp.sum(returned, axis=0)
    return (update, new_moment[None])


def solution(mesh):
    in_specs = (
        P("dp", None, "rep", None),
        P("dp", None, "rep", None),
        P("dp", None, None, None),
        P("dp", None, "rep", None),
        P(),
        P("dp"),
    )
    out_specs = (P("dp", "rep", None), P("dp", None, "rep", None))
    return jax.shard_map(
        on_device, mesh=mesh, in_specs=in_specs, out_specs=out_specs, check_vma=False
    )
```

profile of v0, /device:TPU:103, one launch (start us, length us, event | category | flops | bytes accessed | tf_op | source)
XLA Modules:
  0.0 491.2 jit_solution(6341495661202593447)
XLA Ops:
  7.2 0.0 copy-start
  7.2 0.0 reduce-scatter.4.cloned.1.call-start
  7.2 0.7 reduce-scatter.4.cloned.1.call-update
  7.9 1.2 dynamic-slice.2
  9.2 0.9 convert_reduce_fusion
  10.1 0.1 iota_compare_fusion
  10.2 0.7 fusion.12
  10.8 0.1 broadcast_multiply_fusion
  10.9 243.1 %reduce-scatter.4.cloned.1.call-done = f32[1,32,256]{2,1,0:T(8,128)} async-done(((f32[64,32,256]{2,1,0:T(8,128)}), f32[1,32,256]{2,1,0:T(8,128)}) %reduce-scatter.4.cloned.1.call-update) | async-done | bytes 32784
  254.0 3.0 multiply_bitcast_fusion
  257.0 10.6 %all-to-all-start = ((f32[64,2,32,256]{3,2,1,0:T(8,128)}), f32[64,2,32,256]{3,2,1,0:T(8,128)}, u32[]{:S(2)}, u32[]{:S(2)}) async-start(f32[64,2,32,256]{3,2,1,0:T(8,128)} %multiply_bitcast_fusion), calls=%async_computation | async-start | bytes 8388608 | tf_op jit(solution)/shard_map/all_to_all | solution.py:31
  267.7 0.0 copy-start.2
  268.4 106.2 %all-to-all-done = f32[64,2,32,256]{3,2,1,0:T(8,128)} async-done(((f32[64,2,32,256]{3,2,1,0:T(8,128)}), f32[64,2,32,256]{3,2,1,0:T(8,128)}, u32[]{:S(2)}, u32[]{:S(2)}) %all-to-all-start) | async-done | bytes 4194336 | tf_op jit(solution)/shard_map/all_to_all | solution.py:31
  374.6 2.4 reduce_sum.48
  377.0 0.1 multiply_reduce_fusion.1
  377.1 0.4 fusion
  377.5 19.7 %all_gather.3 = f32[2,256,256]{2,1,0:T(8,128)S(1)} all-gather(f32[2,32,256]{2,1,0:T(8,128)S(1)} %fusion), channel_id=1, replica_groups=mesh['dp'=64,'rep'=8] {'rep'}, dimensions={1}, use_global_device_ids=true | all-gather | bytes 589824 | tf_op jit(solution)/shard_map/all_gather | solution.py:39
  397.2 0.5 multiply_reduce_fusion
  397.7 11.9 %all-reduce.1 = (f32[2]{0:T(128)S(1)}, f32[2]{0:T(128)S(1)}) all-reduce(f32[2]{0:T(128)S(1)} %get-tuple-element.6, f32[2]{0:T(128)S(1)} %multiply_reduce_fusion.1), channel_id=1, replica_groups=mesh['dp'=64,'rep'=8] {'rep'}, use_global_device_ids=true, to_apply=%region_6.0 | all-reduce | flops 4 | bytes 32 | tf_op jit(solution)/shard_map/psum | solution.py:42
  409.6 0.7 fusion.4
  410.3 1.8 convolution_bitcast_fusion
  412.2 1.2 copy.15
  413.4 70.2 %all_to_all.10 = f32[64,1,32,256]{3,2,1,0:T(8,128)S(1)} all-to-all(f32[64,1,32,256]{3,2,1,0:T(8,128)S(1)} %copy.15), channel_id=1, replica_groups=mesh['dp'=64,'rep'=8] {'dp'}, dimensions={0} | all-to-all | bytes 4194304 | tf_op jit(solution)/shard_map/all_to_all | solution.py:56
  483.6 0.8 reduce_sum.51
  (10 shorter events, 0.1 us)
Async XLA Ops:
  7.2 369.9 %copy-start = (f32[1,2,256,256]{3,2,1,0:T(8,128)S(1)}, f32[1,2,256,256]{3,2,1,0:T(8,128)}, u32[]{:S(2)}) copy-start(f32[1,2,256,256]{3,2,1,0:T(8,128)} %param.8) | copy-start | bytes 1572868
  7.2 246.8 %reduce-scatter.4.cloned.1.call-start = ((), (), s32[]{:S(2)}) async-start(), calls=%async_computation.3 | async-start | bytes 2129920
  257.0 11.3 %copy-start.3 = (s32[64]{0:T(128)S(1)}, s32[64]{0:T(128)}, u32[]{:S(2)}) copy-start(s32[64]{0:T(128)} %param.10) | copy-start | bytes 772
  257.0 117.5 %all-to-all-start = ((f32[64,2,32,256]{3,2,1,0:T(8,128)}), f32[64,2,32,256]{3,2,1,0:T(8,128)}, u32[]{:S(2)}, u32[]{:S(2)}) async-start(f32[64,2,32,256]{3,2,1,0:T(8,128)} %multiply_bitcast_fusion), calls=%async_computation | async-start | bytes 8388608 | tf_op jit(solution)/shard_map/all_to_all | solution.py:31
  267.6 129.6 %copy-start.1 = (f32[1,2,32,256]{3,2,1,0:T(8,128)S(1)}, f32[1,2,32,256]{3,2,1,0:T(8,128)}, u32[]{:S(2)}) copy-start(f32[1,2,32,256]{3,2,1,0:T(8,128)} %param.7) | copy-start | bytes 196612
  267.7 142.0 %copy-start.2 = (f32[1,2,32,256]{3,2,1,0:T(8,128)S(1)}, f32[1,2,32,256]{3,2,1,0:T(8,128)}, u32[]{:S(2)}) copy-start(f32[1,2,32,256]{3,2,1,0:T(8,128)} %param.9) | copy-start | bytes 196612
Sparse Core Ops, SparseCore 0:
  12.1 241.8 reduce-scatter.3
where the time goes:
time: 492 us; the launch traced here: 491 us
  waiting for transfers between devices  350 us (71%)
  blocking collectives  102 us (21%)
  between operations  14.8 us (3%)
  starting transfers between devices  10.6 us (2%)
  other arithmetic  8.78 us (2%)
    unnamed x2, waiting for transfers between devices  244 us
    all_to_all x1, waiting for transfers between devices, on_device(): lax.all_to_all(outgoing, 'dp', split_axis=0, concat_axis=0, tiled=True)  106 us
    all_to_all x1, blocking collectives, on_device(): lax.all_to_all(outgoing_back, 'dp', split_axis=0, concat_axis=0, tiled=True)  70.2 us
    all_gather x1, blocking collectives, on_device(): lax.all_gather(right_part, 'rep', axis=1, tiled=True)  19.7 us
    psum x1, blocking collectives, on_device(): lax.psum((jnp.sum(gradient * gradient, axis=(1, 2)), jnp.sum(precond * pr...  11.9 us
    all_to_all x1, starting transfers between devices, on_device(): lax.all_to_all(outgoing, 'dp', split_axis=0, concat_axis=0, tiled=True)  10.6 us
  transfers between devices with their start and end apart: 2, of which 2 were waited for; matrix products, arithmetic and copies ran while one was open for 1% of the time, Pallas kernels for 0%

commit v1 on v0

v1 whole, which is shorter than its diff:
```python
import jax
import jax.numpy as jnp
from jax import lax
from jax.sharding import Mesh, PartitionSpec as P

BETA = 0.9
EPS = 1e-06
AXES = ("z", "y", "x", "c")
HIGHEST = lax.Precision.HIGHEST


def device(z, y, x, c, sizes):
    return ((z * sizes[1] + y) * sizes[2] + x) * sizes[3] + c


def lines(sizes, along):
    groups = []
    for x in range(sizes[2]):
        for c in range(sizes[3]):
            for fixed in range(sizes[0]):
                if along[c] == "y":
                    groups.append([device(fixed, i, x, c, sizes) for i in range(sizes[1])])
                else:
                    groups.append([device(i, fixed, x, c, sizes) for i in range(sizes[0])])
    return groups


def make(sizes):
    side = sizes[0]
    reps = sizes[2] * sizes[3]
    first_lines = lines(sizes, ("y", "z"))
    second_lines = lines(sizes, ("z", "y"))

    def exchange(blocks, groups):
        return lax.all_to_all(blocks, AXES, 0, 0, tiled=True, axis_index_groups=groups)

    def on_device(grads, left_root, right_root, momentum, block_owner, owner_counts):
        parts = grads[0]
        nb, rows, order = parts.shape
        slots = left_root.shape[1]
        core = lax.axis_index("c")
        z, y = lax.axis_index("z"), lax.axis_index("y")
        flip = core == 1
        u = jnp.where(flip, z, y)
        w = jnp.where(flip, y, z)
        key = jnp.where(flip, (block_owner % side) * side + block_owner // side, block_owner)
        ids = jnp.arange(nb)
        less = key[None, :] < key[:, None]
        earlier = (key[None, :] == key[:, None]) & (ids[None, :] < ids[:, None])
        slot_of = jnp.sum(earlier.astype(jnp.int32), axis=1)
        rank = jnp.sum(less.astype(jnp.int32), axis=1) + slot_of
        hit = rank[None, :] == ids[:, None]
        block_at = jnp.sum(jnp.where(hit, ids[None, :], 0), axis=1)
        key_at = jnp.sum(jnp.where(hit, key[None, :], 0), axis=1)
        start = jnp.sum((key[None, :] < side * jnp.arange(side)[:, None]).astype(jnp.int32), axis=1)
        my_start = jnp.sum((key < w * side + u).astype(jnp.int32))
        first = (start - u + side - 1) // side

        send = jnp.take(parts, block_at.reshape(nb // side, side).T.reshape(nb), axis=0)
        got = exchange(send, first_lines)
        part = jnp.sum(got.reshape(side, nb // side, rows, order), axis=0)
        picks = jnp.clip(first[:, None] + jnp.arange(slots)[None, :], 0, nb // side - 1).reshape(-1)
        got = exchange(jnp.take(part, picks, axis=0), second_lines)
        held = jnp.sum(got.reshape(side, slots, rows, order), axis=0)
        at = jnp.clip(lax.dynamic_index_in_dim(first, w, 0, False) * side + u, 0, nb - 1)
        here = lax.dynamic_index_in_dim(key_at, at, 0, False) % side
        picks = (jnp.arange(side) != here).astype(jnp.int32)
        got = exchange(jnp.take(held, picks, axis=0), first_lines)
        gradient = jnp.take(got, (my_start + jnp.arange(slots)) % side, axis=0)

        lefts = lax.all_gather(left_root[0], ("x", "c"), axis=1, tiled=True)
        rights = right_root[0]
        whole = lax.all_gather(gradient, ("x", "c"), axis=1, tiled=True)
        right_part = jnp.einsum("sak,skc->sac", whole, rights, precision=HIGHEST)
        precond = jnp.einsum("sak,skc->sac", lefts, right_part, precision=HIGHEST)
        grad_square = jnp.sum(whole * whole, axis=(1, 2))
        pre_square = jnp.sum(precond * precond, axis=(1, 2))
        entries = order * order
        graft = jnp.sqrt(grad_square / entries) / jnp.sqrt(pre_square / entries + EPS)
        me = lax.axis_index(("x", "c"))
        direction = graft[:, None, None] * lax.dynamic_slice_in_dim(precond, me * rows, rows, 1)
        moment = momentum[0]
        fresh = BETA * moment + direction
        update_owned = BETA * fresh + direction
        used = jnp.arange(slots) < owner_counts[0]
        new_moment = jnp.where(used[:, None, None], fresh, moment)

        got = exchange(jnp.tile(update_owned, (side, 1, 1)), first_lines)
        others = jnp.where(flip, u * side + jnp.arange(side), jnp.arange(side) * side + u)
        picks = jnp.take((key % side) * slots + slot_of, others)
        got = exchange(jnp.take(got, picks, axis=0), second_lines)
        mine = z * side + y
        source = lax.dynamic_index_in_dim(key, mine, 0, False) // side
        update = lax.dynamic_index_in_dim(got, source, 0, True)
        return (update, new_moment[None])

    return on_device


def solution(mesh):
    sizes = (8, 8, 4, 2)
    fine = Mesh(mesh.devices.reshape(sizes), AXES)
    dp, rep = ("z", "y"), ("x", "c")
    in_specs = (
        P(dp, None, rep, None),
        P(dp, None, rep, None),
        P(dp, None, None, None),
        P(dp, None, rep, None),
        P(),
        P(dp),
    )
    out_specs = (P(dp, rep, None), P(dp, None, rep, None))
    return jax.shard_map(
        make(sizes), mesh=fine, in_specs=in_specs, out_specs=out_specs, check_vma=False
    )
```

time: 492 us -> 146 us (0.30)
  the two profiles are of different devices: /device:TPU:103 before, /device:TPU:2 now
where the time goes in v1:
time: 146 us; the launch traced here: 145 us
  waiting for transfers between devices  58.4 us (40%)
  starting transfers between devices  31.4 us (22%)
  blocking collectives  26.4 us (18%)
  other arithmetic  11.8 us (8%)
  local copies, waits for them, and re-layouts  8.6 us (6%)
  between operations  6.83 us (5%)
    all_to_all x5, waiting for transfers between devices, exchange(): lax.all_to_all(blocks, AXES, 0, 0, tiled=True, axis_index_groups=groups)  58.4 us
    all_to_all x5, starting transfers between devices, exchange(): lax.all_to_all(blocks, AXES, 0, 0, tiled=True, axis_index_groups=groups)  31.4 us
    all_gather x1, blocking collectives, on_device(): whole = lax.all_gather(gradient, ('x', 'c'), axis=1, tiled=True)  13.2 us
    all_gather x1, blocking collectives, on_device(): lefts = lax.all_gather(left_root[0], ('x', 'c'), axis=1, tiled=True)  13.2 us
    select_n x2, other arithmetic, on_device(): jnp.take(parts, block_at.reshape(nb // side, side).T.reshape(nb), axis=0)  3.1 us
  transfers between devices with their start and end apart: 5, of which 4 were waited for; matrix products, arithmetic and copies ran while one was open for 3% of the time, Pallas kernels for 0%

profile of v1, /device:TPU:2, one launch (start us, length us, event | category | flops | bytes accessed | tf_op | source)
XLA Modules:
  0.0 144.8 jit_solution(7358333378761921221)
XLA Ops:
  0.7 1.4 %fusion.10 = (s32[]{:T(128)}, s32[64]{0:T(128)S(1)}) fusion(s32[]{:T(128)S(6)} %add.314, s32[64]{0:T(128)} %param.10, pred[]{:T(512)S(6)} %eq.17), kind=kLoop, calls=%fused_computation.85 | loop fusion | flops 1599 | bytes 521 | tf_op jit(solution)/shard_map/reduce_sum | solution.py:56
  2.8 2.0 %gather_fusion.1 = f32[64,32,256]{2,1,0:T(8,128)} fusion(f32[64,32,256]{2,1,0:T(8,128)S(1)} %bitcast.56, s32[1024]{0:T(1024)S(1)} %pad_clamp_fusion.4), kind=kCustom, calls=%fused_computation.1 | custom fusion | bytes 4194560 | tf_op jit(solution)/shard_map/jit(_take)/gather | solution.py:59
  4.8 3.1 %broadcast_select_fusion = f32[64,32,256]{2,1,0:T(8,128)} fusion(f32[64,32,256]{2,1,0:T(8,128)} %gather_fusion.1, pred[64]{0:T(512)(128)(4,1)S(1)} %compare_and_fusion), kind=kLoop, calls=%fused_computation.6 | loop fusion | flops 524288 | bytes 4194368 | tf_op jit(solution)/shard_map/jit(_take)/select_n | solution.py:59
  7.9 7.1 %all-to-all-start = ((f32[64,32,256]{2,1,0:T(8,128)}), f32[64,32,256]{2,1,0:T(8,128)}, u32[]{:S(2)}, u32[]{:S(2)}) async-start(f32[64,32,256]{2,1,0:T(8,128)} %broadcast_select_fusion), calls=%async_computation | async-start | bytes 4194304 | tf_op jit(solution)/shard_map/all_to_all | solution.py:35
  15.4 29.9 %all-to-all-done = f32[64,32,256]{2,1,0:T(8,128)} async-done(((f32[64,32,256]{2,1,0:T(8,128)}), f32[64,32,256]{2,1,0:T(8,128)}, u32[]{:S(2)}, u32[]{:S(2)}) %all-to-all-start) | async-done | bytes 2097184 | tf_op jit(solution)/shard_map/all_to_all | solution.py:35
  45.3 1.8 %reduce_sum.96 = f32[8,32,256]{2,1,0:T(8,128)S(1)} reduce(f32[8,8,32,256]{3,2,1,0:T(8,128)} %bitcast.7, f32[]{:T(128)} %constant.201.clone.1), dimensions={0}, to_apply=%region_6.7 | reduce | flops 458752 | bytes 2359300 | tf_op jit(solution)/shard_map/reduce_sum | solution.py:61
  47.7 0.9 broadcast_select_fusion.1
  48.6 10.3 %all-to-all-start.1 = ((f32[16,32,256]{2,1,0:T(8,128)}), f32[16,32,256]{2,1,0:T(8,128)S(1)}, u32[]{:S(2)}, u32[]{:S(2)}) async-start(f32[16,32,256]{2,1,0:T(8,128)} %broadcast_select_fusion.1), calls=%async_computation.1 | async-start | bytes 1048576 | tf_op jit(solution)/shard_map/all_to_all | solution.py:35
  62.8 0.7 fusion.17
  63.5 8.7 %all-to-all-done.1 = f32[16,32,256]{2,1,0:T(8,128)S(1)} async-done(((f32[16,32,256]{2,1,0:T(8,128)}), f32[16,32,256]{2,1,0:T(8,128)S(1)}, u32[]{:S(2)}, u32[]{:S(2)}) %all-to-all-start.1) | async-done | bytes 524320 | tf_op jit(solution)/shard_map/all_to_all | solution.py:35
  72.8 0.8 broadcast_select_fusion.3
  73.6 3.4 %all-to-all-start.2 = ((f32[8,32,256]{2,1,0:T(8,128)}), f32[8,32,256]{2,1,0:T(8,128)S(1)}, u32[]{:S(2)}, u32[]{:S(2)}) async-start(f32[8,32,256]{2,1,0:T(8,128)} %broadcast_select_fusion.3), calls=%async_computation.2 | async-start | bytes 524288 | tf_op jit(solution)/shard_map/all_to_all | solution.py:35
  77.0 0.7 compare_and_fusion.3
  78.4 13.2 %all-gather = f32[1,2,256,256]{3,2,1,0:T(8,128)S(1)} all-gather(f32[1,2,32,256]{3,2,1,0:T(8,128)S(1)} %copy-done.2), channel_id=2, replica_groups=mesh['z'=8,'y'=8,'x'=4,'c'=2] {'x','c'}, dimensions={2}, use_global_device_ids=true | all-gather | bytes 589824 | tf_op jit(solution)/shard_map/all_gather | solution.py:71
  92.2 13.2 %all_gather.6 = f32[2,256,256]{2,1,0:T(8,128)S(1)} all-gather(f32[2,32,256]{2,1,0:T(8,128)S(1)} %broadcast_select_fusion.4), channel_id=1, replica_groups=mesh['z'=8,'y'=8,'x'=4,'c'=2] {'x','c'}, dimensions={1}, use_global_device_ids=true | all-gather | bytes 589824 | tf_op jit(solution)/shard_map/all_gather | solution.py:73
  105.6 0.7 fusion.2
  106.3 0.7 multiply_reduce_fusion
  107.0 0.7 fusion.4
  107.7 0.8 tile.4
  108.6 7.1 %all-to-all-start.3 = ((f32[16,32,256]{2,1,0:T(8,128)}), f32[16,32,256]{2,1,0:T(8,128)S(1)}, u32[]{:S(2)}, u32[]{:S(2)}) async-start(f32[16,32,256]{2,1,0:T(8,128)} %bitcast.15), calls=%async_computation.3 | async-start | bytes 1048576 | tf_op jit(solution)/shard_map/all_to_all | solution.py:35
  116.4 12.6 %all-to-all-done.3 = f32[16,32,256]{2,1,0:T(8,128)S(1)} async-done(((f32[16,32,256]{2,1,0:T(8,128)}), f32[16,32,256]{2,1,0:T(8,128)S(1)}, u32[]{:S(2)}, u32[]{:S(2)}) %all-to-all-start.3) | async-done | bytes 524320 | tf_op jit(solution)/shard_map/all_to_all | solution.py:35
  129.6 0.8 broadcast_select_fusion.2
  130.3 3.4 %all-to-all-start.4 = ((f32[8,32,256]{2,1,0:T(8,128)}), f32[8,32,256]{2,1,0:T(8,128)S(1)}, u32[]{:S(2)}, u32[]{:S(2)}) async-start(f32[8,32,256]{2,1,0:T(8,128)} %broadcast_select_fusion.2), calls=%async_computation.4 | async-start | bytes 524288 | tf_op jit(solution)/shard_map/all_to_all | solution.py:35
  137.0 7.2 %all-to-all-done.4 = f32[8,32,256]{2,1,0:T(8,128)S(1)} async-done(((f32[8,32,256]{2,1,0:T(8,128)}), f32[8,32,256]{2,1,0:T(8,128)S(1)}, u32[]{:S(2)}, u32[]{:S(2)}) %all-to-all-start.4) | async-done | bytes 262176 | tf_op jit(solution)/shard_map/all_to_all | solution.py:35
  (51 shorter events, 6.8 us)
Async XLA Ops:
  0.6 2.2 %copy-start = (f32[1,64,32,256]{3,2,1,0:T(8,128)S(1)}, f32[1,64,32,256]{3,2,1,0:T(8,128)}, u32[]{:S(2)}) copy-start(f32[1,64,32,256]{3,2,1,0:T(8,128)} %param.6) | copy-start | bytes 6291460
  7.9 37.5 %all-to-all-start = ((f32[64,32,256]{2,1,0:T(8,128)}), f32[64,32,256]{2,1,0:T(8,128)}, u32[]{:S(2)}, u32[]{:S(2)}) async-start(f32[64,32,256]{2,1,0:T(8,128)} %broadcast_select_fusion), calls=%async_computation | async-start | bytes 4194304 | tf_op jit(solution)/shard_map/all_to_all | solution.py:35
  47.7 30.7 %copy-start.2 = (f32[1,2,32,256]{3,2,1,0:T(8,128)S(1)}, f32[1,2,32,256]{3,2,1,0:T(8,128)}, u32[]{:S(2)}) copy-start(f32[1,2,32,256]{3,2,1,0:T(8,128)} %param.7) | copy-start | bytes 196612
  48.6 23.6 %all-to-all-start.1 = ((f32[16,32,256]{2,1,0:T(8,128)}), f32[16,32,256]{2,1,0:T(8,128)S(1)}, u32[]{:S(2)}, u32[]{:S(2)}) async-start(f32[16,32,256]{2,1,0:T(8,128)} %broadcast_select_fusion.1), calls=%async_computation.1 | async-start | bytes 1048576 | tf_op jit(solution)/shard_map/all_to_all | solution.py:35
  62.1 43.5 %copy-start.1 = (f32[1,2,256,256]{3,2,1,0:T(8,128)S(1)}, f32[1,2,256,256]{3,2,1,0:T(8,128)}, u32[]{:S(2)}) copy-start(f32[1,2,256,256]{3,2,1,0:T(8,128)} %param.8) | copy-start | bytes 1572868
  73.6 17.9 %all-to-all-start.2 = ((f32[8,32,256]{2,1,0:T(8,128)}), f32[8,32,256]{2,1,0:T(8,128)S(1)}, u32[]{:S(2)}, u32[]{:S(2)}) async-start(f32[8,32,256]{2,1,0:T(8,128)} %broadcast_select_fusion.3), calls=%async_computation.2 | async-start | bytes 524288 | tf_op jit(solution)/shard_map/all_to_all | solution.py:35
  92.2 14.8 %copy-start.3 = (f32[1,2,32,256]{3,2,1,0:T(8,128)S(1)}, f32[1,2,32,256]{3,2,1,0:T(8,128)}, u32[]{:S(2)}) copy-start(f32[1,2,32,256]{3,2,1,0:T(8,128)} %param.9) | copy-start | bytes 196612
  108.6 20.4 %all-to-all-start.3 = ((f32[16,32,256]{2,1,0:T(8,128)}), f32[16,32,256]{2,1,0:T(8,128)S(1)}, u32[]{:S(2)}, u32[]{:S(2)}) async-start(f32[16,32,256]{2,1,0:T(8,128)} %bitcast.15), calls=%async_computation.3 | async-start | bytes 1048576 | tf_op jit(solution)/shard_map/all_to_all | solution.py:35
  130.3 13.8 %all-to-all-start.4 = ((f32[8,32,256]{2,1,0:T(8,128)}), f32[8,32,256]{2,1,0:T(8,128)S(1)}, u32[]{:S(2)}, u32[]{:S(2)}) async-start(f32[8,32,256]{2,1,0:T(8,128)} %broadcast_select_fusion.2), calls=%async_computation.4 | async-start | bytes 524288 | tf_op jit(solution)/shard_map/all_to_all | solution.py:35

commit v2 on v1

--- a/solution.py
+++ b/solution.py
@@ -31,8 +31,26 @@
     first_lines = lines(sizes, ("y", "z"))
     second_lines = lines(sizes, ("z", "y"))
 
+    rep_lines = [
+        [device(z, y, x, c, sizes) for x in range(sizes[2]) for c in range(sizes[3])]
+        for z in range(sizes[0])
+        for y in range(sizes[1])
+    ]
+
+    def gather_any_order(rows):
+        other = lax.ppermute(rows, "c", [(0, 1), (1, 0)])
+        chip = jnp.concatenate([rows, other], axis=1)
+        away = [
+            lax.ppermute(chip, "x", [(i, (i + k) % sizes[2]) for i in range(sizes[2])])
+            for k in range(1, sizes[2])
+        ]
+        return jnp.concatenate([chip, *away], axis=1)
+
     def exchange(blocks, groups):
         return lax.all_to_all(blocks, AXES, 0, 0, tiled=True, axis_index_groups=groups)
+
+    def pick(blocks, index):
+        return blocks.at[index].get(mode="promise_in_bounds")
 
     def on_device(grads, left_root, right_root, momentum, block_owner, owner_counts):
         parts = grads[0]
@@ -56,29 +74,30 @@
         my_start = jnp.sum((key < w * side + u).astype(jnp.int32))
         first = (start - u + side - 1) // side
 
-        send = jnp.take(parts, block_at.reshape(nb // side, side).T.reshape(nb), axis=0)
+        send = pick(parts, block_at.reshape(nb // side, side).T.reshape(nb))
         got = exchange(send, first_lines)
+        lefts = gather_any_order(left_root[0])
+        got, lefts = lax.optimization_barrier((got, lefts))
         part = jnp.sum(got.reshape(side, nb // side, rows, order), axis=0)
         picks = jnp.clip(first[:, None] + jnp.arange(slots)[None, :], 0, nb // side - 1).reshape(-1)
-        got = exchange(jnp.take(part, picks, axis=0), second_lines)
+        got = exchange(pick(part, picks), second_lines)
         held = jnp.sum(got.reshape(side, slots, rows, order), axis=0)
         at = jnp.clip(lax.dynamic_index_in_dim(first, w, 0, False) * side + u, 0, nb - 1)
         here = lax.dynamic_index_in_dim(key_at, at, 0, False) % side
         picks = (jnp.arange(side) != here).astype(jnp.int32)
-        got = exchange(jnp.take(held, picks, axis=0), first_lines)
-        gradient = jnp.take(got, (my_start + jnp.arange(slots)) % side, axis=0)
+        got = exchange(pick(held, picks), first_lines)
+        gradient = pick(got, jnp.tile((my_start + jnp.arange(slots)) % side, reps))
 
-        lefts = lax.all_gather(left_root[0], ("x", "c"), axis=1, tiled=True)
         rights = right_root[0]
-        whole = lax.all_gather(gradient, ("x", "c"), axis=1, tiled=True)
+        got = exchange(gradient, rep_lines).reshape(reps, slots, rows, order)
+        whole = got.transpose(1, 0, 2, 3).reshape(slots, order, order)
         right_part = jnp.einsum("sak,skc->sac", whole, rights, precision=HIGHEST)
         precond = jnp.einsum("sak,skc->sac", lefts, right_part, precision=HIGHEST)
         grad_square = jnp.sum(whole * whole, axis=(1, 2))
         pre_square = jnp.sum(precond * precond, axis=(1, 2))
         entries = order * order
         graft = jnp.sqrt(grad_square / entries) / jnp.sqrt(pre_square / entries + EPS)
-        me = lax.axis_index(("x", "c"))
-        direction = graft[:, None, None] * lax.dynamic_slice_in_dim(precond, me * rows, rows, 1)
+        direction = graft[:, None, None] * precond[:, :rows]
         moment = momentum[0]
         fresh = BETA * moment + direction
         update_owned = BETA * fresh + direction
@@ -87,8 +106,8 @@
 
         got = exchange(jnp.tile(update_owned, (side, 1, 1)), first_lines)
         others = jnp.where(flip, u * side + jnp.arange(side), jnp.arange(side) * side + u)
-        picks = jnp.take((key % side) * slots + slot_of, others)
-        got = exchange(jnp.take(got, picks, axis=0), second_lines)
+        picks = pick((key % side) * slots + slot_of, others)
+        got = exchange(pick(got, picks), second_lines)
         mine = z * side + y
         source = lax.dynamic_index_in_dim(key, mine, 0, False) // side
         update = lax.dynamic_index_in_dim(got, source, 0, True)

time: 146 us -> 137 us (0.938)
  blocking collectives: 26.4 us -> 0 us
  starting transfers between devices: 31.4 us -> 47.8 us
  other arithmetic: 11.8 us -> 5.48 us
  waiting for transfers between devices: 58.4 us -> 61.7 us
  local copies, waits for them, and re-layouts: 8.6 us -> 11.6 us
    all_gather x2 -> x0, blocking collectives: 26.4 us -> none  [the longest x1 13.2 us: on_device(): whole = lax.all_gather(gradient, ('x', 'c'), axis=1, tiled=True)]
    ppermute x0 -> x4, starting transfers between devices: none -> 15.2 us  [the longest x3 10.5 us: gather_any_order(): lax.ppermute(chip, 'x', [(i, (i + k) % sizes[2]) for i in range(sizes[2])])]
    select_n x11 -> x7, other arithmetic: 6.32 us -> 0.71 us  [the longest x1 0.66 us: on_device(): gradient = pick(got, jnp.tile((my_start + jnp.arange(slots)) % side, reps))]
    ppermute x0 -> x4, waiting for transfers between devices: none -> 5 us  [the longest x3 4.53 us: gather_any_order(): lax.ppermute(chip, 'x', [(i, (i + k) % sizes[2]) for i in range(sizes[2])])]
    gather x6, local copies, waits for them, and re-layouts: 4.88 us -> 7.87 us  [pick(): return blocks.at[index].get(mode='promise_in_bounds')]
    all_to_all x5 -> x6, waiting for transfers between devices: 58.4 us -> 56.7 us  [exchange(): lax.all_to_all(blocks, AXES, 0, 0, tiled=True, axis_index_groups=groups)]
    all_to_all x5 -> x6, starting transfers between devices: 31.4 us -> 32.7 us  [exchange(): lax.all_to_all(blocks, AXES, 0, 0, tiled=True, axis_index_groups=groups)]
  transfers between devices with their start and end apart: 5 -> 10, of which waited for: 4 -> 9; matrix products, arithmetic and copies ran while one was open for 3% -> 3% of each run, Pallas kernels for 0% -> 0%
where the time goes in v2:
time: 137 us; the launch traced here: 136 us
  waiting for transfers between devices  61.7 us (45%)
  starting transfers between devices  47.8 us (35%)
  local copies, waits for them, and re-layouts  11.6 us (8%)
  between operations  6.77 us (5%)
  other arithmetic  5.48 us (4%)
  matrix products  2.45 us (2%)
    all_to_all x6, waiting for transfers between devices, exchange(): lax.all_to_all(blocks, AXES, 0, 0, tiled=True, axis_index_groups=groups)  56.7 us
    all_to_all x6, starting transfers between devices, exchange(): lax.all_to_all(blocks, AXES, 0, 0, tiled=True, axis_index_groups=groups)  32.7 us
    ppermute x3, starting transfers between devices, gather_any_order(): lax.ppermute(chip, 'x', [(i, (i + k) % sizes[2]) for i in range(sizes[2])])  10.5 us
    gather x6, local copies, waits for them, and re-layouts, pick(): return blocks.at[index].get(mode='promise_in_bounds')  7.87 us
    ppermute x1, starting transfers between devices, gather_any_order(): other = lax.ppermute(rows, 'c', [(0, 1), (1, 0)])  4.68 us
    ppermute x3, waiting for transfers between devices, gather_any_order(): lax.ppermute(chip, 'x', [(i, (i + k) % sizes[2]) for i in range(sizes[2])])  4.53 us
  transfers between devices with their start and end apart: 10, of which 9 were waited for; matrix products, arithmetic and copies ran while one was open for 3% of the time, Pallas kernels for 0%

profile of v2, /device:TPU:2, one launch (start us, length us, event | category | flops | bytes accessed | tf_op | source)
XLA Modules:
  0.0 135.9 jit_solution(12656184893131677338)
XLA Ops:
  0.7 1.4 %fusion.7 = (s32[]{:T(128)}, s32[64]{0:T(128)S(1)}) fusion(s32[]{:T(128)S(6)} %add.222, s32[64]{0:T(128)} %param.10, pred[]{:T(512)S(6)} %eq.13), kind=kLoop, calls=%fused_computation.64 | loop fusion | flops 1599 | bytes 521 | tf_op jit(solution)/shard_map/reduce_sum | solution.py:74
  2.7 2.0 %gather_fusion = f32[64,32,256]{2,1,0:T(8,128)} fusion(f32[64,32,256]{2,1,0:T(8,128)S(1)} %bitcast.49, s32[1024]{0:T(1024)S(1)} %pad_clamp_fusion.5), kind=kCustom, calls=%fused_computation | custom fusion | bytes 4194560 | tf_op jit(solution)/shard_map/gather | solution.py:53
  4.7 7.2 %all-to-all-start = ((f32[64,32,256]{2,1,0:T(8,128)}), f32[64,32,256]{2,1,0:T(8,128)}, u32[]{:S(2)}, u32[]{:S(2)}) async-start(f32[64,32,256]{2,1,0:T(8,128)} %gather_fusion), calls=%async_computation | async-start | bytes 4194304 | tf_op jit(solution)/shard_map/all_to_all | solution.py:50
  11.9 4.7 %collective-permute-start = (f32[2,32,256]{2,1,0:T(8,128)S(1)}, f32[2,32,256]{2,1,0:T(8,128)S(1)}, u32[]{:S(2)}, u32[]{:S(2)}) collective-permute-start(f32[2,32,256]{2,1,0:T(8,128)S(1)} %bitcast.54), channel_id=1, source_target_pairs={{0,1},{1,0},{2,3},{3,2},{4,5},{5,4},{6,7},{7,6},{8,9},{9,8},{10,11... | collective-permute-start | bytes 196616 | tf_op jit(solution)/shard_map/ppermute | solution.py:41
  17.5 3.4 %collective-permute-start.1 = (f32[2,64,256]{2,1,0:T(8,128)S(1)}, f32[2,64,256]{2,1,0:T(8,128)S(1)}, u32[]{:S(2)}, u32[]{:S(2)}) collective-permute-start(f32[2,64,256]{2,1,0:T(8,128)S(1)} %pad_maximum_fusion), channel_id=1, source_target_pairs={{0,2},{2,4},{4,6},{6,0},{1,3},{3,5},{5,7},{7,1},{8,10},{10,12},{12... | collective-permute-start | bytes 393224 | tf_op jit(solution)/shard_map/ppermute | solution.py:44
  20.9 3.2 %collective-permute-start.2 = (f32[2,64,256]{2,1,0:T(8,128)S(1)}, f32[2,64,256]{2,1,0:T(8,128)S(1)}, u32[]{:S(2)}, u32[]{:S(2)}) collective-permute-start(f32[2,64,256]{2,1,0:T(8,128)S(1)} %pad_maximum_fusion), channel_id=1, source_target_pairs={{0,4},{2,6},{4,0},{6,2},{1,5},{3,7},{5,1},{7,3},{8,12},{10,14},{12... | collective-permute-start | bytes 393224 | tf_op jit(solution)/shard_map/ppermute | solution.py:44
  24.1 3.9 %collective-permute-start.3 = (f32[2,64,256]{2,1,0:T(8,128)S(1)}, f32[2,64,256]{2,1,0:T(8,128)S(1)}, u32[]{:S(2)}, u32[]{:S(2)}) collective-permute-start(f32[2,64,256]{2,1,0:T(8,128)S(1)} %pad_maximum_fusion), channel_id=1, source_target_pairs={{0,6},{2,0},{4,2},{6,4},{1,7},{3,1},{5,3},{7,5},{8,14},{10,8},{12,... | collective-permute-start | bytes 393224 | tf_op jit(solution)/shard_map/ppermute | solution.py:44
  28.1 2.6 %collective-permute-done.2 = f32[2,64,256]{2,1,0:T(8,128)S(1)} collective-permute-done((f32[2,64,256]{2,1,0:T(8,128)S(1)}, f32[2,64,256]{2,1,0:T(8,128)S(1)}, u32[]{:S(2)}, u32[]{:S(2)}) %collective-permute-start.2) | collective-permute-done | bytes 131104 | tf_op jit(solution)/shard_map/ppermute | solution.py:44
  30.7 1.9 %collective-permute-done.3 = f32[2,64,256]{2,1,0:T(8,128)S(1)} collective-permute-done((f32[2,64,256]{2,1,0:T(8,128)S(1)}, f32[2,64,256]{2,1,0:T(8,128)S(1)}, u32[]{:S(2)}, u32[]{:S(2)}) %collective-permute-start.3) | collective-permute-done | bytes 131104 | tf_op jit(solution)/shard_map/ppermute | solution.py:44
  32.6 9.7 %all-to-all-done = f32[64,32,256]{2,1,0:T(8,128)} async-done(((f32[64,32,256]{2,1,0:T(8,128)}), f32[64,32,256]{2,1,0:T(8,128)}, u32[]{:S(2)}, u32[]{:S(2)}) %all-to-all-start) | async-done | bytes 2097184 | tf_op jit(solution)/shard_map/all_to_all | solution.py:50
  42.3 1.8 %reduce_sum.93 = f32[8,32,256]{2,1,0:T(8,128)S(1)} reduce(f32[8,8,32,256]{3,2,1,0:T(8,128)} %bitcast.5, f32[]{:T(128)} %constant.119.clone.1), dimensions={0}, to_apply=%region_3.4 | reduce | flops 458752 | bytes 2359300 | tf_op jit(solution)/shard_map/reduce_sum | solution.py:81
  44.1 1.4 %gather_fusion.1 = f32[16,32,256]{2,1,0:T(8,128)} fusion(f32[8,32,256]{2,1,0:T(8,128)S(1)} %reduce_sum.93, s32[1024]{0:T(1024)S(1)} %get-tuple-element.19), kind=kCustom, calls=%fused_computation.1 | custom fusion | bytes 1048640 | tf_op jit(solution)/shard_map/gather | solution.py:53
  45.4 10.3 %all-to-all-start.1 = ((f32[16,32,256]{2,1,0:T(8,128)}), f32[16,32,256]{2,1,0:T(8,128)S(1)}, u32[]{:S(2)}, u32[]{:S(2)}) async-start(f32[16,32,256]{2,1,0:T(8,128)} %gather_fusion.1), calls=%async_computation.1 | async-start | bytes 1048576 | tf_op jit(solution)/shard_map/all_to_all | solution.py:50
  59.6 9.5 %all-to-all-done.1 = f32[16,32,256]{2,1,0:T(8,128)S(1)} async-done(((f32[16,32,256]{2,1,0:T(8,128)}), f32[16,32,256]{2,1,0:T(8,128)S(1)}, u32[]{:S(2)}, u32[]{:S(2)}) %all-to-all-start.1) | async-done | bytes 524320 | tf_op jit(solution)/shard_map/all_to_all | solution.py:50
  70.3 3.4 %all-to-all-start.2 = ((f32[8,32,256]{2,1,0:T(8,128)}), f32[8,32,256]{2,1,0:T(8,128)S(1)}, u32[]{:S(2)}, u32[]{:S(2)}) async-start(f32[8,32,256]{2,1,0:T(8,128)} %gather_fusion.2), calls=%async_computation.2 | async-start | bytes 524288 | tf_op jit(solution)/shard_map/all_to_all | solution.py:50
  74.5 9.6 %all-to-all-done.2 = f32[8,32,256]{2,1,0:T(8,128)S(1)} async-done(((f32[8,32,256]{2,1,0:T(8,128)}), f32[8,32,256]{2,1,0:T(8,128)S(1)}, u32[]{:S(2)}, u32[]{:S(2)}) %all-to-all-start.2) | async-done | bytes 262176 | tf_op jit(solution)/shard_map/all_to_all | solution.py:50
  84.1 1.4 %gather_fusion.3 = f32[16,32,256]{2,1,0:T(8,128)} fusion(f32[8,32,256]{2,1,0:T(8,128)S(1)} %all-to-all-done.2, s32[1024]{0:T(1024)S(1)} %pad_clamp_fusion.2), kind=kCustom, calls=%fused_computation.3 | custom fusion | bytes 1048640 | tf_op jit(solution)/shard_map/gather | solution.py:53
  85.5 4.8 %all-to-all-start.3 = ((f32[16,32,256]{2,1,0:T(8,128)}), f32[16,32,256]{2,1,0:T(8,128)S(1)}, u32[]{:S(2)}, u32[]{:S(2)}) async-start(f32[16,32,256]{2,1,0:T(8,128)} %gather_fusion.3), calls=%async_computation.3 | async-start | bytes 1048576 | tf_op jit(solution)/shard_map/all_to_all | solution.py:50
  91.0 8.2 %all-to-all-done.3 = f32[16,32,256]{2,1,0:T(8,128)S(1)} async-done(((f32[16,32,256]{2,1,0:T(8,128)}), f32[16,32,256]{2,1,0:T(8,128)S(1)}, u32[]{:S(2)}, u32[]{:S(2)}) %all-to-all-start.3) | async-done | bytes 524320 | tf_op jit(solution)/shard_map/all_to_all | solution.py:50
  99.5 1.7 %fusion = f32[2,256,256]{2,1,0:T(8,128)S(1)} fusion(f32[2,256,256]{2,1,0:T(8,128)S(1)} %bitcast.52, f32[1,2,256,256]{3,2,1,0:T(8,128)} %param.8), kind=kOutput, calls=%fused_computation.6 | convolution fusion | flops 402653184 | bytes 1572864 | tf_op jit(solution)/shard_map/sak,skc->sac/dot_general | solution.py:94
  103.5 3.5 %all-to-all-start.4 = ((f32[16,32,256]{2,1,0:T(8,128)}), f32[16,32,256]{2,1,0:T(8,128)S(1)}, u32[]{:S(2)}, u32[]{:S(2)}) async-start(f32[16,32,256]{2,1,0:T(8,128)} %bitcast.17), calls=%async_computation.4 | async-start | bytes 1048576 | tf_op jit(solution)/shard_map/all_to_all | solution.py:50
  107.6 12.5 %all-to-all-done.4 = f32[16,32,256]{2,1,0:T(8,128)S(1)} async-done(((f32[16,32,256]{2,1,0:T(8,128)}), f32[16,32,256]{2,1,0:T(8,128)S(1)}, u32[]{:S(2)}, u32[]{:S(2)}) %all-to-all-start.4) | async-done | bytes 524320 | tf_op jit(solution)/shard_map/all_to_all | solution.py:50
  121.4 3.4 %all-to-all-start.5 = ((f32[8,32,256]{2,1,0:T(8,128)}), f32[8,32,256]{2,1,0:T(8,128)S(1)}, u32[]{:S(2)}, u32[]{:S(2)}) async-start(f32[8,32,256]{2,1,0:T(8,128)} %gather_fusion.5), calls=%async_computation.5 | async-start | bytes 524288 | tf_op jit(solution)/shard_map/all_to_all | solution.py:50
  128.1 7.2 %all-to-all-done.5 = f32[8,32,256]{2,1,0:T(8,128)S(1)} async-done(((f32[8,32,256]{2,1,0:T(8,128)}), f32[8,32,256]{2,1,0:T(8,128)S(1)}, u32[]{:S(2)}, u32[]{:S(2)}) %all-to-all-start.5) | async-done | bytes 262176 | tf_op jit(solution)/shard_map/all_to_all | solution.py:50
  (54 shorter events, 10.3 us)
Async XLA Ops:
  0.6 2.1 %copy-start = (f32[1,64,32,256]{3,2,1,0:T(8,128)S(1)}, f32[1,64,32,256]{3,2,1,0:T(8,128)}, u32[]{:S(2)}) copy-start(f32[1,64,32,256]{3,2,1,0:T(8,128)} %param.6) | copy-start | bytes 6291460
  4.7 7.2 %copy-start.1 = (f32[1,2,32,256]{3,2,1,0:T(8,128)S(1)}, f32[1,2,32,256]{3,2,1,0:T(8,128)}, u32[]{:S(2)}) copy-start(f32[1,2,32,256]{3,2,1,0:T(8,128)} %param.7) | copy-start | bytes 196612
  4.7 37.6 %all-to-all-start = ((f32[64,32,256]{2,1,0:T(8,128)}), f32[64,32,256]{2,1,0:T(8,128)}, u32[]{:S(2)}, u32[]{:S(2)}) async-start(f32[64,32,256]{2,1,0:T(8,128)} %gather_fusion), calls=%async_computation | async-start | bytes 4194304 | tf_op jit(solution)/shard_map/all_to_all | solution.py:50
  11.9 5.6 %collective-permute-start = (f32[2,32,256]{2,1,0:T(8,128)S(1)}, f32[2,32,256]{2,1,0:T(8,128)S(1)}, u32[]{:S(2)}, u32[]{:S(2)}) collective-permute-start(f32[2,32,256]{2,1,0:T(8,128)S(1)} %bitcast.54), channel_id=1, source_target_pairs={{0,1},{1,0},{2,3},{3,2},{4,5},{5,4},{6,7},{7,6},{8,9},{9,8},{10,11... | collective-permute-start | bytes 196616 | tf_op jit(solution)/shard_map/ppermute | solution.py:41
  17.5 10.5 %collective-permute-start.1 = (f32[2,64,256]{2,1,0:T(8,128)S(1)}, f32[2,64,256]{2,1,0:T(8,128)S(1)}, u32[]{:S(2)}, u32[]{:S(2)}) collective-permute-start(f32[2,64,256]{2,1,0:T(8,128)S(1)} %pad_maximum_fusion), channel_id=1, source_target_pairs={{0,2},{2,4},{4,6},{6,0},{1,3},{3,5},{5,7},{7,1},{8,10},{10,12},{12... | collective-permute-start | bytes 393224 | tf_op jit(solution)/shard_map/ppermute | solution.py:44
  20.9 9.8 %collective-permute-start.2 = (f32[2,64,256]{2,1,0:T(8,128)S(1)}, f32[2,64,256]{2,1,0:T(8,128)S(1)}, u32[]{:S(2)}, u32[]{:S(2)}) collective-permute-start(f32[2,64,256]{2,1,0:T(8,128)S(1)} %pad_maximum_fusion), channel_id=1, source_target_pairs={{0,4},{2,6},{4,0},{6,2},{1,5},{3,7},{5,1},{7,3},{8,12},{10,14},{12... | collective-permute-start | bytes 393224 | tf_op jit(solution)/shard_map/ppermute | solution.py:44
  24.1 8.4 %collective-permute-start.3 = (f32[2,64,256]{2,1,0:T(8,128)S(1)}, f32[2,64,256]{2,1,0:T(8,128)S(1)}, u32[]{:S(2)}, u32[]{:S(2)}) collective-permute-start(f32[2,64,256]{2,1,0:T(8,128)S(1)} %pad_maximum_fusion), channel_id=1, source_target_pairs={{0,6},{2,0},{4,2},{6,4},{1,7},{3,1},{5,3},{7,5},{8,14},{10,8},{12,... | collective-permute-start | bytes 393224 | tf_op jit(solution)/shard_map/ppermute | solution.py:44
  45.4 23.6 %all-to-all-start.1 = ((f32[16,32,256]{2,1,0:T(8,128)}), f32[16,32,256]{2,1,0:T(8,128)S(1)}, u32[]{:S(2)}, u32[]{:S(2)}) async-start(f32[16,32,256]{2,1,0:T(8,128)} %gather_fusion.1), calls=%async_computation.1 | async-start | bytes 1048576 | tf_op jit(solution)/shard_map/all_to_all | solution.py:50
  70.3 13.8 %all-to-all-start.2 = ((f32[8,32,256]{2,1,0:T(8,128)}), f32[8,32,256]{2,1,0:T(8,128)S(1)}, u32[]{:S(2)}, u32[]{:S(2)}) async-start(f32[8,32,256]{2,1,0:T(8,128)} %gather_fusion.2), calls=%async_computation.2 | async-start | bytes 524288 | tf_op jit(solution)/shard_map/all_to_all | solution.py:50
  85.5 13.7 %all-to-all-start.3 = ((f32[16,32,256]{2,1,0:T(8,128)}), f32[16,32,256]{2,1,0:T(8,128)S(1)}, u32[]{:S(2)}, u32[]{:S(2)}) async-start(f32[16,32,256]{2,1,0:T(8,128)} %gather_fusion.3), calls=%async_computation.3 | async-start | bytes 1048576 | tf_op jit(solution)/shard_map/all_to_all | solution.py:50
  99.3 2.7 %copy-start.2 = (f32[1,2,32,256]{3,2,1,0:T(8,128)S(1)}, f32[1,2,32,256]{3,2,1,0:T(8,128)}, u32[]{:S(2)}) copy-start(f32[1,2,32,256]{3,2,1,0:T(8,128)} %param.9) | copy-start | bytes 196612
  103.5 16.7 %all-to-all-start.4 = ((f32[16,32,256]{2,1,0:T(8,128)}), f32[16,32,256]{2,1,0:T(8,128)S(1)}, u32[]{:S(2)}, u32[]{:S(2)}) async-start(f32[16,32,256]{2,1,0:T(8,128)} %bitcast.17), calls=%async_computation.4 | async-start | bytes 1048576 | tf_op jit(solution)/shard_map/all_to_all | solution.py:50
  121.4 13.8 %all-to-all-start.5 = ((f32[8,32,256]{2,1,0:T(8,128)}), f32[8,32,256]{2,1,0:T(8,128)S(1)}, u32[]{:S(2)}, u32[]{:S(2)}) async-start(f32[8,32,256]{2,1,0:T(8,128)} %gather_fusion.5), calls=%async_computation.5 | async-start | bytes 524288 | tf_op jit(solution)/shard_map/all_to_all | solution.py:50

commit v3 on v2

--- a/solution.py
+++ b/solution.py
@@ -1,6 +1,8 @@
 import jax
 import jax.numpy as jnp
 from jax import lax
+from jax.experimental import pallas as pl
+from jax.experimental.pallas import tpu as pltpu
 from jax.sharding import Mesh, PartitionSpec as P
 
 BETA = 0.9
@@ -23,6 +25,83 @@
                 else:
                     groups.append([device(i, fixed, x, c, sizes) for i in range(sizes[0])])
     return groups
+
+
+VMEM = pl.BlockSpec(memory_space=pltpu.VMEM)
+SMEM = pl.BlockSpec(memory_space=pltpu.SMEM)
+
+
+def local_call(body, outs, ins, args):
+    return pl.pallas_call(
+        body,
+        out_shape=outs,
+        in_specs=ins,
+        out_specs=jax.tree.map(lambda _: VMEM, outs),
+        compiler_params=pltpu.CompilerParams(vmem_limit_bytes=24 * 2**20),
+    )(*args)
+
+
+def sum_and_pick(got, index, sources):
+    each, count = got.shape[0] // sources, index.shape[0]
+
+    def body(index_ref, got_ref, out_ref):
+        for i in range(count):
+            at = index_ref[i]
+            total = got_ref[at]
+            for s in range(1, sources):
+                total = total + got_ref[s * each + at]
+            out_ref[i] = total
+
+    out = jax.ShapeDtypeStruct((count, *got.shape[1:]), got.dtype)
+    return local_call(body, out, [SMEM, VMEM], (index, got))
+
+
+def pick_and_repeat(got, index, times):
+    count = index.shape[0]
+
+    def body(index_ref, got_ref, out_ref):
+        for i in range(count):
+            block = got_ref[index_ref[i]]
+            for t in range(times):
+                out_ref[t * count + i] = block
+
+    out = jax.ShapeDtypeStruct((times * count, *got.shape[1:]), got.dtype)
+    return local_call(body, out, [SMEM, VMEM], (index, got))
+
+
+def step(got, lefts, rights, moment, count, times):
+    slots, rows, order = moment.shape
+    reps = order // rows
+
+    def body(count_ref, got_ref, left_ref, right_ref, moment_ref, moment_out_ref, send_ref):
+        held = count_ref[0]
+        for s in range(slots):
+            whole = jnp.concatenate([got_ref[r * slots + s] for r in range(reps)], axis=0)
+            right_part = jnp.dot(
+                whole, right_ref[s], precision=HIGHEST, preferred_element_type=jnp.float32
+            )
+            precond = jnp.dot(
+                left_ref[s], right_part, precision=HIGHEST, preferred_element_type=jnp.float32
+            )
+            entries = order * order
+            grad_mean = jnp.sum(whole * whole, keepdims=True) / entries
+            pre_mean = jnp.sum(precond * precond, keepdims=True) / entries
+            graft = jnp.sqrt(grad_mean) / jnp.sqrt(pre_mean + EPS)
+            direction = graft * precond[:rows]
+            before = moment_ref[s]
+            fresh = BETA * before + direction
+            update = BETA * fresh + direction
+            moment_out_ref[s] = jnp.where(s < held, fresh, before)
+            for t in range(times):
+                send_ref[t * slots + s] = update
+
+    outs = (
+        jax.ShapeDtypeStruct(moment.shape, moment.dtype),
+        jax.ShapeDtypeStruct((times * slots, rows, order), moment.dtype),
+    )
+    return local_call(
+        body, outs, [SMEM, VMEM, VMEM, VMEM, VMEM], (count, got, lefts, rights, moment)
+    )
 
 
 def make(sizes):
@@ -74,42 +153,26 @@
         my_start = jnp.sum((key < w * side + u).astype(jnp.int32))
         first = (start - u + side - 1) // side
 
-        send = pick(parts, block_at.reshape(nb // side, side).T.reshape(nb))
-        got = exchange(send, first_lines)
-        lefts = gather_any_order(left_root[0])
-        got, lefts = lax.optimization_barrier((got, lefts))
-        part = jnp.sum(got.reshape(side, nb // side, rows, order), axis=0)
-        picks = jnp.clip(first[:, None] + jnp.arange(slots)[None, :], 0, nb // side - 1).reshape(-1)
-        got = exchange(pick(part, picks), second_lines)
-        held = jnp.sum(got.reshape(side, slots, rows, order), axis=0)
+        picks_two = jnp.clip(first[:, None] + jnp.arange(slots)[None, :], 0, nb // side - 1)
         at = jnp.clip(lax.dynamic_index_in_dim(first, w, 0, False) * side + u, 0, nb - 1)
         here = lax.dynamic_index_in_dim(key_at, at, 0, False) % side
-        picks = (jnp.arange(side) != here).astype(jnp.int32)
-        got = exchange(pick(held, picks), first_lines)
-        gradient = pick(got, jnp.tile((my_start + jnp.arange(slots)) % side, reps))
+        picks_three = (jnp.arange(side) != here).astype(jnp.int32)
+        picks_own = (my_start + jnp.arange(slots)) % side
+        others = jnp.where(flip, u * side + jnp.arange(side), jnp.arange(side) * side + u)
+        picks_back = pick((key % side) * slots + slot_of, others)
+        source = lax.dynamic_index_in_dim(key, z * side + y, 0, False) // side
+        tables = (picks_two.reshape(-1), picks_three, picks_own, picks_back, source)
 
-        rights = right_root[0]
-        got = exchange(gradient, rep_lines).reshape(reps, slots, rows, order)
-        whole = got.transpose(1, 0, 2, 3).reshape(slots, order, order)
-        right_part = jnp.einsum("sak,skc->sac", whole, rights, precision=HIGHEST)
-        precond = jnp.einsum("sak,skc->sac", lefts, right_part, precision=HIGHEST)
-        grad_square = jnp.sum(whole * whole, axis=(1, 2))
-        pre_square = jnp.sum(precond * precond, axis=(1, 2))
-        entries = order * order
-        graft = jnp.sqrt(grad_square / entries) / jnp.sqrt(pre_square / entries + EPS)
-        direction = graft[:, None, None] * precond[:, :rows]
-        moment = momentum[0]
-        fresh = BETA * moment + direction
-        update_owned = BETA * fresh + direction
-        used = jnp.arange(slots) < owner_counts[0]
-        new_moment = jnp.where(used[:, None, None], fresh, moment)
-
-        got = exchange(jnp.tile(update_owned, (side, 1, 1)), first_lines)
-        others = jnp.where(flip, u * side + jnp.arange(side), jnp.arange(side) * side + u)
-        picks = pick((key % side) * slots + slot_of, others)
-        got = exchange(pick(got, picks), second_lines)
-        mine = z * side + y
-        source = lax.dynamic_index_in_dim(key, mine, 0, False) // side
+        got = exchange(pick(parts, block_at.reshape(nb // side, side).T.reshape(nb)), first_lines)
+        lefts = gather_any_order(left_root[0])
+        got, lefts, tables = lax.optimization_barrier((got, lefts, tables))
+        picks_two, picks_three, picks_own, picks_back, source = tables
+        got = exchange(sum_and_pick(got, picks_two, side), second_lines)
+        got = exchange(sum_and_pick(got, picks_three, side), first_lines)
+        got = exchange(pick_and_repeat(got, picks_own, reps), rep_lines)
+        new_moment, send = step(got, lefts, right_root[0], momentum[0], owner_counts, side)
+        got = exchange(send, first_lines)
+        got = exchange(pick_and_repeat(got, picks_back, 1), second_lines)
         update = lax.dynamic_index_in_dim(got, source, 0, True)
         return (update, new_moment[None])
 

time: 137 us -> 132 us (0.964)
  blocking collectives: 0 us -> 52.2 us
  waiting for transfers between devices: 61.7 us -> 25 us
  starting transfers between devices: 47.8 us -> 30.5 us
  Pallas kernels: 0 us -> 7.34 us
  local copies, waits for them, and re-layouts: 11.6 us -> 6.42 us
  other arithmetic: 5.48 us -> 2.72 us
  matrix products: 2.45 us -> 0 us
    all_to_all x0 -> x3, blocking collectives: none -> 52.2 us  [exchange(): lax.all_to_all(blocks, AXES, 0, 0, tiled=True, axis_index_groups=groups)]
    all_to_all x6 -> x3, waiting for transfers between devices: 56.7 us -> 20.8 us  [exchange(): lax.all_to_all(blocks, AXES, 0, 0, tiled=True, axis_index_groups=groups)]
    all_to_all x6 -> x3, starting transfers between devices: 32.7 us -> 15.4 us  [exchange(): lax.all_to_all(blocks, AXES, 0, 0, tiled=True, axis_index_groups=groups)]
    pallas_call x0 -> x5, Pallas kernels: none -> 7.34 us  [local_call(): pl.pallas_call(body, out_shape=outs, in_specs=ins, out_specs=jax.tree.map...]
    gather x6 -> x2, local copies, waits for them, and re-layouts: 7.87 us -> 2.63 us  [pick(): return blocks.at[index].get(mode='promise_in_bounds')]
    dot_general x2 -> x0, matrix products: 2.45 us -> none  [the longest x1 1.7 us: on_device(): right_part = jnp.einsum('sak,skc->sac', whole, rights, precision=HIGHEST)]
    reduce_sum x3 -> x0, other arithmetic: 1.97 us -> none  [the longest x1 1.77 us: on_device(): part = jnp.sum(got.reshape(side, nb // side, rows, order), axis=0)]
  transfers between devices with their start and end apart: 10 -> 7, of which waited for: 9 -> 5; matrix products, arithmetic and copies ran while one was open for 3% -> 3% of each run, Pallas kernels for 0% -> 0%
where the time goes in v3:
time: 132 us; the launch traced here: 131 us
  blocking collectives  52.2 us (40%)
  starting transfers between devices  30.5 us (23%)
  waiting for transfers between devices  25 us (19%)
  Pallas kernels  7.34 us (6%)
  between operations  6.73 us (5%)
  local copies, waits for them, and re-layouts  6.42 us (5%)
  other arithmetic  2.72 us (2%)
    all_to_all x3, blocking collectives, exchange(): lax.all_to_all(blocks, AXES, 0, 0, tiled=True, axis_index_groups=groups)  52.2 us
    all_to_all x3, waiting for transfers between devices, exchange(): lax.all_to_all(blocks, AXES, 0, 0, tiled=True, axis_index_groups=groups)  20.8 us
    all_to_all x3, starting transfers between devices, exchange(): lax.all_to_all(blocks, AXES, 0, 0, tiled=True, axis_index_groups=groups)  15.4 us
    ppermute x3, starting transfers between devices, gather_any_order(): lax.ppermute(chip, 'x', [(i, (i + k) % sizes[2]) for i in range(sizes[2])])  10.5 us
    pallas_call x5, Pallas kernels, local_call(): pl.pallas_call(body, out_shape=outs, in_specs=ins, out_specs=jax.tree.map...  7.34 us
    ppermute x1, starting transfers between devices, gather_any_order(): other = lax.ppermute(rows, 'c', [(0, 1), (1, 0)])  4.68 us
    ppermute x3, waiting for transfers between devices, gather_any_order(): lax.ppermute(chip, 'x', [(i, (i + k) % sizes[2]) for i in range(sizes[2])])  4.19 us
  transfers between devices with their start and end apart: 7, of which 5 were waited for; matrix products, arithmetic and copies ran while one was open for 3% of the time, Pallas kernels for 0%

profile of v3, /device:TPU:2, one launch (start us, length us, event | category | flops | bytes accessed | tf_op | source)
XLA Modules:
  0.0 131.0 jit_solution(3114814119371701557)
XLA Ops:
  0.7 1.4 %fusion.3 = (s32[]{:T(128)}, s32[64]{0:T(128)S(1)}) fusion(s32[]{:T(128)S(6)} %add.152, s32[64]{0:T(128)} %param.10, pred[]{:T(512)S(6)} %eq.13), kind=kLoop, calls=%fused_computation.42 | loop fusion | flops 1599 | bytes 521 | tf_op jit(solution)/shard_map/reduce_sum | solution.py:153
  2.7 2.0 %gather_fusion = f32[64,32,256]{2,1,0:T(8,128)} fusion(f32[64,32,256]{2,1,0:T(8,128)S(1)} %bitcast.14, s32[1024]{0:T(1024)S(1)} %pad_clamp_fusion.1), kind=kCustom, calls=%fused_computation | custom fusion | bytes 4194560 | tf_op jit(solution)/shard_map/gather | solution.py:132
  4.7 7.2 %all-to-all-start = ((f32[64,32,256]{2,1,0:T(8,128)}), f32[64,32,256]{2,1,0:T(8,128)}, u32[]{:S(2)}, u32[]{:S(2)}) async-start(f32[64,32,256]{2,1,0:T(8,128)} %gather_fusion), calls=%async_computation | async-start | bytes 4194304 | tf_op jit(solution)/shard_map/all_to_all | solution.py:129
  11.9 4.7 %collective-permute-start = (f32[2,32,256]{2,1,0:T(8,128)S(1)}, f32[2,32,256]{2,1,0:T(8,128)S(1)}, u32[]{:S(2)}, u32[]{:S(2)}) collective-permute-start(f32[2,32,256]{2,1,0:T(8,128)S(1)} %bitcast.17), channel_id=1, source_target_pairs={{0,1},{1,0},{2,3},{3,2},{4,5},{5,4},{6,7},{7,6},{8,9},{9,8},{10,11... | collective-permute-start | bytes 196616 | tf_op jit(solution)/shard_map/ppermute | solution.py:120
  20.7 3.4 %collective-permute-start.1 = (f32[2,64,256]{2,1,0:T(8,128)S(1)}, f32[2,64,256]{2,1,0:T(8,128)S(1)}, u32[]{:S(2)}, u32[]{:S(2)}) collective-permute-start(f32[2,64,256]{2,1,0:T(8,128)S(1)} %pad_maximum_fusion), channel_id=1, source_target_pairs={{0,2},{2,4},{4,6},{6,0},{1,3},{3,5},{5,7},{7,1},{8,10},{10,12},{12... | collective-permute-start | bytes 393224 | tf_op jit(solution)/shard_map/ppermute | solution.py:123
  24.2 0.7 and_select_fusion.1.index_ref
  28.1 0.6 gather_fusion.1
  28.7 3.0 %collective-permute-start.2 = (f32[2,64,256]{2,1,0:T(8,128)S(1)}, f32[2,64,256]{2,1,0:T(8,128)S(1)}, u32[]{:S(2)}, u32[]{:S(2)}) collective-permute-start(f32[2,64,256]{2,1,0:T(8,128)S(1)} %pad_maximum_fusion), channel_id=1, source_target_pairs={{0,4},{2,6},{4,0},{6,2},{1,5},{3,7},{5,1},{7,3},{8,12},{10,14},{12... | collective-permute-start | bytes 393224 | tf_op jit(solution)/shard_map/ppermute | solution.py:123
  31.8 4.0 %collective-permute-start.3 = (f32[2,64,256]{2,1,0:T(8,128)S(1)}, f32[2,64,256]{2,1,0:T(8,128)S(1)}, u32[]{:S(2)}, u32[]{:S(2)}) collective-permute-start(f32[2,64,256]{2,1,0:T(8,128)S(1)} %pad_maximum_fusion), channel_id=1, source_target_pairs={{0,6},{2,0},{4,2},{6,4},{1,7},{3,1},{5,3},{7,5},{8,14},{10,8},{12,... | collective-permute-start | bytes 393224 | tf_op jit(solution)/shard_map/ppermute | solution.py:123
  35.9 2.3 %collective-permute-done.2 = f32[2,64,256]{2,1,0:T(8,128)S(1)} collective-permute-done((f32[2,64,256]{2,1,0:T(8,128)S(1)}, f32[2,64,256]{2,1,0:T(8,128)S(1)}, u32[]{:S(2)}, u32[]{:S(2)}) %collective-permute-start.2) | collective-permute-done | bytes 131104 | tf_op jit(solution)/shard_map/ppermute | solution.py:123
  38.2 1.9 %collective-permute-done.3 = f32[2,64,256]{2,1,0:T(8,128)S(1)} collective-permute-done((f32[2,64,256]{2,1,0:T(8,128)S(1)}, f32[2,64,256]{2,1,0:T(8,128)S(1)}, u32[]{:S(2)}, u32[]{:S(2)}) %collective-permute-start.3) | collective-permute-done | bytes 131104 | tf_op jit(solution)/shard_map/ppermute | solution.py:123
  40.1 2.2 %all-to-all-done.got_ref = f32[64,32,256]{2,1,0:T(8,128)} async-done(((f32[64,32,256]{2,1,0:T(8,128)}), f32[64,32,256]{2,1,0:T(8,128)}, u32[]{:S(2)}, u32[]{:S(2)}) %all-to-all-start) | async-done | bytes 2097184 | tf_op jit(solution)/shard_map/all_to_all | solution.py:129
  42.3 1.8 %shard_map.77 = f32[16,32,256]{2,1,0:T(8,128)S(1)} custom-call(s32[16]{0:T(128)S(1)} %min.16.index_ref, f32[64,32,256]{2,1,0:T(8,128)} %all-to-all-done.got_ref), custom_call_target="tpu_custom_call" | custom-call | tf_op jit(solution)/shard_map/pallas_call | solution.py:35
  44.1 23.5 %all_to_all.30.got_ref = f32[16,32,256]{2,1,0:T(8,128)S(1)} all-to-all(f32[16,32,256]{2,1,0:T(8,128)S(1)} %shard_map.77), channel_id=1, replica_groups={{0,64,128,192,256,320,384,448},{8,72,136,200,264,328,392,456},{16,80,14..., dimensions={0} | all-to-all | bytes 1048576 | tf_op jit(solution)/shard_map/all_to_all | solution.py:129
  68.3 13.0 %all_to_all.31.got_ref = f32[8,32,256]{2,1,0:T(8,128)S(1)} all-to-all(f32[8,32,256]{2,1,0:T(8,128)S(1)} %shard_map.78), channel_id=1, replica_groups={{0,8,16,24,32,40,48,56},{64,72,80,88,96,104,112,120},{128,136,144,152,1..., dimensions={0} | all-to-all | bytes 524288 | tf_op jit(solution)/shard_map/all_to_all | solution.py:129
  81.3 1.4 %shard_map.79 = f32[16,32,256]{2,1,0:T(8,128)} custom-call(s32[2]{0:T(128)S(1)} %and_select_fusion.1.index_ref, f32[8,32,256]{2,1,0:T(8,128)S(1)} %all_to_all.31.got_ref), custom_call_target="tpu_custom_call" | custom-call | tf_op jit(solution)/shard_map/pallas_call | solution.py:35
  82.7 4.7 %all-to-all-start.3 = ((f32[16,32,256]{2,1,0:T(8,128)}), f32[16,32,256]{2,1,0:T(8,128)S(1)}, u32[]{:S(2)}, u32[]{:S(2)}) async-start(f32[16,32,256]{2,1,0:T(8,128)} %shard_map.79), calls=%async_computation.3 | async-start | bytes 1048576 | tf_op jit(solution)/shard_map/all_to_all | solution.py:129
  88.0 8.2 %all-to-all-done.3.got_ref = f32[16,32,256]{2,1,0:T(8,128)S(1)} async-done(((f32[16,32,256]{2,1,0:T(8,128)}), f32[16,32,256]{2,1,0:T(8,128)S(1)}, u32[]{:S(2)}, u32[]{:S(2)}) %all-to-all-start.3) | async-done | bytes 524320 | tf_op jit(solution)/shard_map/all_to_all | solution.py:129
  96.3 1.0 copy-done.1
  97.3 2.3 %shard_map.80 = (f32[2,32,256]{2,1,0:T(8,128)}, f32[16,32,256]{2,1,0:T(8,128)S(1)}) custom-call(s32[1]{0:T(128)S(6)} %copy.15.count_ref, f32[16,32,256]{2,1,0:T(8,128)S(1)} %all-to-all-done.3.got_ref, f32[2,256,256]{2,1,0:T(8,128)S(1)} %constant_dynamic-update-slice_fusion.left_ref, f32[2,256,256]{2,1,0:T(8,128)S(1)} %bitcast.15, f32[2,32,256]{2,1,0:T(8,128)S(1)} %bitcast.16), custom_call_target="tpu_custom_call" | custom-call | tf_op jit(solution)/shard_map/pallas_call | solution.py:35
  99.6 15.7 %all_to_all.32.got_ref = f32[16,32,256]{2,1,0:T(8,128)S(1)} all-to-all(f32[16,32,256]{2,1,0:T(8,128)S(1)} %get-tuple-element.17), channel_id=1, replica_groups={{0,8,16,24,32,40,48,56},{64,72,80,88,96,104,112,120},{128,136,144,152,1..., dimensions={0} | all-to-all | bytes 1048576 | tf_op jit(solution)/shard_map/all_to_all | solution.py:129
  115.3 1.2 shard_map.81
  116.5 3.4 %all-to-all-start.5 = ((f32[8,32,256]{2,1,0:T(8,128)}), f32[8,32,256]{2,1,0:T(8,128)S(1)}, u32[]{:S(2)}, u32[]{:S(2)}) async-start(f32[8,32,256]{2,1,0:T(8,128)} %shard_map.81), calls=%async_computation.5 | async-start | bytes 524288 | tf_op jit(solution)/shard_map/all_to_all | solution.py:129
  120.0 10.4 %all-to-all-done.5 = f32[8,32,256]{2,1,0:T(8,128)S(1)} async-done(((f32[8,32,256]{2,1,0:T(8,128)}), f32[8,32,256]{2,1,0:T(8,128)S(1)}, u32[]{:S(2)}, u32[]{:S(2)}) %all-to-all-start.5) | async-done | bytes 262176 | tf_op jit(solution)/shard_map/all_to_all | solution.py:129
  (36 shorter events, 4.0 us)
Async XLA Ops:
  0.6 2.1 %copy-start = (f32[1,64,32,256]{3,2,1,0:T(8,128)S(1)}, f32[1,64,32,256]{3,2,1,0:T(8,128)}, u32[]{:S(2)}) copy-start(f32[1,64,32,256]{3,2,1,0:T(8,128)} %param.6) | copy-start | bytes 6291460
  4.7 7.2 %copy-start.3 = (f32[1,2,32,256]{3,2,1,0:T(8,128)S(1)}, f32[1,2,32,256]{3,2,1,0:T(8,128)}, u32[]{:S(2)}) copy-start(f32[1,2,32,256]{3,2,1,0:T(8,128)} %param.7) | copy-start | bytes 196612
  4.7 37.6 %all-to-all-start = ((f32[64,32,256]{2,1,0:T(8,128)}), f32[64,32,256]{2,1,0:T(8,128)}, u32[]{:S(2)}, u32[]{:S(2)}) async-start(f32[64,32,256]{2,1,0:T(8,128)} %gather_fusion), calls=%async_computation | async-start | bytes 4194304 | tf_op jit(solution)/shard_map/all_to_all | solution.py:129
  11.9 8.8 %collective-permute-start = (f32[2,32,256]{2,1,0:T(8,128)S(1)}, f32[2,32,256]{2,1,0:T(8,128)S(1)}, u32[]{:S(2)}, u32[]{:S(2)}) collective-permute-start(f32[2,32,256]{2,1,0:T(8,128)S(1)} %bitcast.17), channel_id=1, source_target_pairs={{0,1},{1,0},{2,3},{3,2},{4,5},{5,4},{6,7},{7,6},{8,9},{9,8},{10,11... | collective-permute-start | bytes 196616 | tf_op jit(solution)/shard_map/ppermute | solution.py:120
  20.7 15.1 %collective-permute-start.1 = (f32[2,64,256]{2,1,0:T(8,128)S(1)}, f32[2,64,256]{2,1,0:T(8,128)S(1)}, u32[]{:S(2)}, u32[]{:S(2)}) collective-permute-start(f32[2,64,256]{2,1,0:T(8,128)S(1)} %pad_maximum_fusion), channel_id=1, source_target_pairs={{0,2},{2,4},{4,6},{6,0},{1,3},{3,5},{5,7},{7,1},{8,10},{10,12},{12... | collective-permute-start | bytes 393224 | tf_op jit(solution)/shard_map/ppermute | solution.py:123
  28.7 9.4 %collective-permute-start.2 = (f32[2,64,256]{2,1,0:T(8,128)S(1)}, f32[2,64,256]{2,1,0:T(8,128)S(1)}, u32[]{:S(2)}, u32[]{:S(2)}) collective-permute-start(f32[2,64,256]{2,1,0:T(8,128)S(1)} %pad_maximum_fusion), channel_id=1, source_target_pairs={{0,4},{2,6},{4,0},{6,2},{1,5},{3,7},{5,1},{7,3},{8,12},{10,14},{12... | collective-permute-start | bytes 393224 | tf_op jit(solution)/shard_map/ppermute | solution.py:123
  31.8 8.3 %collective-permute-start.3 = (f32[2,64,256]{2,1,0:T(8,128)S(1)}, f32[2,64,256]{2,1,0:T(8,128)S(1)}, u32[]{:S(2)}, u32[]{:S(2)}) collective-permute-start(f32[2,64,256]{2,1,0:T(8,128)S(1)} %pad_maximum_fusion), channel_id=1, source_target_pairs={{0,6},{2,0},{4,2},{6,4},{1,7},{3,1},{5,3},{7,5},{8,14},{10,8},{12,... | collective-permute-start | bytes 393224 | tf_op jit(solution)/shard_map/ppermute | solution.py:123
  44.1 52.2 %copy-start.2 = (f32[1,2,32,256]{3,2,1,0:T(8,128)S(1)}, f32[1,2,32,256]{3,2,1,0:T(8,128)}, u32[]{:S(2)}) copy-start(f32[1,2,32,256]{3,2,1,0:T(8,128)} %param.9) | copy-start | bytes 196612
  82.7 13.6 %all-to-all-start.3 = ((f32[16,32,256]{2,1,0:T(8,128)}), f32[16,32,256]{2,1,0:T(8,128)S(1)}, u32[]{:S(2)}, u32[]{:S(2)}) async-start(f32[16,32,256]{2,1,0:T(8,128)} %shard_map.79), calls=%async_computation.3 | async-start | bytes 1048576 | tf_op jit(solution)/shard_map/all_to_all | solution.py:129
  96.3 1.0 copy-start.1
  116.5 13.8 %all-to-all-start.5 = ((f32[8,32,256]{2,1,0:T(8,128)}), f32[8,32,256]{2,1,0:T(8,128)S(1)}, u32[]{:S(2)}, u32[]{:S(2)}) async-start(f32[8,32,256]{2,1,0:T(8,128)} %shard_map.81), calls=%async_computation.5 | async-start | bytes 524288 | tf_op jit(solution)/shard_map/all_to_all | solution.py:129

commit v4 on v3

v4 whole, which is shorter than its diff:
```python
import jax
import jax.numpy as jnp
from jax import lax
from jax.experimental import pallas as pl
from jax.experimental.pallas import tpu as pltpu
from jax.sharding import Mesh, PartitionSpec as P

BETA = 0.9
EPS = 1e-06
AXES = ("z", "y", "x", "c")
HIGHEST = lax.Precision.HIGHEST


def device(z, y, x, c, sizes):
    return ((z * sizes[1] + y) * sizes[2] + x) * sizes[3] + c


def lines(sizes, along):
    groups = []
    for x in range(sizes[2]):
        for c in range(sizes[3]):
            for fixed in range(sizes[0]):
                if along[c] == "y":
                    groups.append([device(fixed, i, x, c, sizes) for i in range(sizes[1])])
                else:
                    groups.append([device(i, fixed, x, c, sizes) for i in range(sizes[0])])
    return groups


VMEM = pl.BlockSpec(memory_space=pltpu.VMEM)
SMEM = pl.BlockSpec(memory_space=pltpu.SMEM)


ANY = pl.BlockSpec(memory_space=pl.ANY)
TWO, THREE, OWN, BACK, SOURCE, COUNT, TABLE = 0, 16, 24, 26, 34, 35, 36


def local_call(body, outs, ins, args, out_specs=None, scratch=()):
    return pl.pallas_call(
        body,
        out_shape=outs,
        in_specs=ins,
        out_specs=jax.tree.map(lambda _: VMEM, outs) if out_specs is None else out_specs,
        scratch_shapes=scratch,
        compiler_params=pltpu.CompilerParams(vmem_limit_bytes=24 * 2**20),
    )(*args)


def key_of(owner, flip, side):
    turned = (owner & (side - 1)) * side + owner // side
    return jnp.where(flip, turned, owner)


def sort_blocks(place_ref, owner_ref, slot_ref, start_ref, side):
    nb = owner_ref.shape[0]
    flip = place_ref[2] == 1
    for k in range(side * side):
        start_ref[k] = 0
    for b in range(nb):
        key = key_of(owner_ref[b], flip, side)
        slot_ref[b] = start_ref[key]
        start_ref[key] = slot_ref[b] + 1
    total = jnp.int32(0)
    for k in range(side * side):
        held = start_ref[k]
        start_ref[k] = total
        total = total + held


def deal(parts, place, block_owner, side):
    nb = parts.shape[0]

    def body(place_ref, owner_ref, parts_ref, out_ref, slot_ref, start_ref, sem):
        flip = place_ref[2] == 1
        sort_blocks(place_ref, owner_ref, slot_ref, start_ref, side)
        for b in range(nb):
            rank = start_ref[key_of(owner_ref[b], flip, side)] + slot_ref[b]
            to = (rank & (side - 1)) * (nb // side) + rank // side
            pltpu.make_async_copy(parts_ref.at[b], out_ref.at[to], sem).start()
        pltpu.make_async_copy(parts_ref, out_ref, sem).wait()

    scratch = [pltpu.SMEM((nb,), jnp.int32), pltpu.SMEM((side * side,), jnp.int32), pltpu.SemaphoreType.DMA(())]
    out = jax.ShapeDtypeStruct(parts.shape, parts.dtype)
    return local_call(body, out, [SMEM, SMEM, ANY], (place, block_owner, parts), ANY, scratch)


def tables(place, block_owner, owner_counts, side, slots):
    nb = block_owner.shape[0]

    def body(place_ref, owner_ref, count_ref, out_ref, slot_ref, start_ref, key_at_ref):
        z, y, flip = place_ref[0], place_ref[1], place_ref[2] == 1
        u, w = jnp.where(flip, z, y), jnp.where(flip, y, z)
        sort_blocks(place_ref, owner_ref, slot_ref, start_ref, side)
        for b in range(nb):
            key = key_of(owner_ref[b], flip, side)
            key_at_ref[start_ref[key] + slot_ref[b]] = key

        def first(line):
            return jnp.maximum(start_ref[line * side] - u + side - 1, 0) // side

        for line in range(side):
            for s in range(slots):
                out_ref[TWO + line * slots + s] = jnp.minimum(first(line) + s, nb // side - 1)
        here = key_at_ref[jnp.minimum(first(w) * side + u, nb - 1)] & (side - 1)
        for i in range(side):
            out_ref[THREE + i] = jnp.where(here == i, 0, 1)
        for s in range(slots):
            out_ref[OWN + s] = (start_ref[w * side + u] + s) & (side - 1)
        for i in range(side):
            b = jnp.where(flip, u * side + i, i * side + u)
            key = key_of(owner_ref[b], flip, side)
            out_ref[BACK + i] = (key & (side - 1)) * slots + slot_ref[b]
        out_ref[SOURCE] = key_of(owner_ref[z * side + y], flip, side) // side
        out_ref[COUNT] = count_ref[0]

    scratch = [pltpu.SMEM((nb,), jnp.int32), pltpu.SMEM((side * side,), jnp.int32), pltpu.SMEM((nb,), jnp.int32)]
    out = jax.ShapeDtypeStruct((TABLE,), jnp.int32)
    return local_call(body, out, [SMEM, SMEM, SMEM], (place, block_owner, owner_counts), SMEM, scratch)


def sum_and_pick(got, table, base, count, sources):
    each = got.shape[0] // sources

    def body(table_ref, got_ref, out_ref, held_ref, total_ref, sems):
        def fetch(s):
            part = pl.ds(s * each, each)
            return pltpu.make_async_copy(got_ref.at[part], held_ref.at[part], sems.at[s])

        for s in range(sources):
            fetch(s).start()
        for s in range(sources):
            fetch(s).wait()
            for i in range(each):
                block = held_ref[s * each + i]
                total_ref[i] = block if s == 0 else total_ref[i] + block
        for i in range(count):
            out_ref[i] = total_ref[table_ref[base + i]]

    out = jax.ShapeDtypeStruct((count, *got.shape[1:]), got.dtype)
    scratch = [
        pltpu.VMEM(got.shape, got.dtype),
        pltpu.VMEM((each, *got.shape[1:]), got.dtype),
        pltpu.SemaphoreType.DMA((sources,)),
    ]
    return local_call(body, out, [SMEM, ANY], (table, got), None, scratch)


def sum_and_pick_here(got, table, base, count, sources):
    each = got.shape[0] // sources

    def body(table_ref, got_ref, out_ref):
        for i in range(count):
            at = table_ref[base + i]
            total = got_ref[at]
            for s in range(1, sources):
                total = total + got_ref[s * each + at]
            out_ref[i] = total

    out = jax.ShapeDtypeStruct((count, *got.shape[1:]), got.dtype)
    return local_call(body, out, [SMEM, VMEM], (table, got))


def pick_and_repeat(got, table, base, count, times):
    def body(table_ref, got_ref, out_ref):
        for i in range(count):
            block = got_ref[table_ref[base + i]]
            for t in range(times):
                out_ref[t * count + i] = block

    out = jax.ShapeDtypeStruct((times * count, *got.shape[1:]), got.dtype)
    return local_call(body, out, [SMEM, VMEM], (table, got))


def step(got, factors, moment, table, times):
    slots, rows, order = moment.shape
    reps = order // rows

    def body(table_ref, got_ref, factor_ref, moment_ref, moment_out_ref, send_ref):
        held = table_ref[COUNT]
        for s in range(slots):
            whole = jnp.concatenate([got_ref[r * slots + s] for r in range(reps)], axis=0)
            right_part = jnp.dot(
                whole, factor_ref[slots + s], precision=HIGHEST, preferred_element_type=jnp.float32
            )
            precond = jnp.dot(
                factor_ref[s], right_part, precision=HIGHEST, preferred_element_type=jnp.float32
            )
            entries = order * order
            grad_mean = jnp.sum(whole * whole, keepdims=True) / entries
            pre_mean = jnp.sum(precond * precond, keepdims=True) / entries
            graft = jnp.sqrt(grad_mean) / jnp.sqrt(pre_mean + EPS)
            direction = graft * precond[:rows]
            before = moment_ref[s]
            fresh = BETA * before + direction
            update = BETA * fresh + direction
            moment_out_ref[s] = jnp.where(s < held, fresh, before)
            for t in range(times):
                send_ref[t * slots + s] = update

    outs = (
        jax.ShapeDtypeStruct(moment.shape, moment.dtype),
        jax.ShapeDtypeStruct((times * slots, rows, order), moment.dtype),
    )
    return local_call(
        body, outs, [SMEM, VMEM, VMEM, VMEM], (table, got, factors, moment)
    )


def make(sizes):
    side = sizes[0]
    reps = sizes[2] * sizes[3]
    first_lines = lines(sizes, ("y", "z"))
    second_lines = lines(sizes, ("z", "y"))

    rep_lines = [
        [device(z, y, x, c, sizes) for x in range(sizes[2]) for c in range(sizes[3])]
        for z in range(sizes[0])
        for y in range(sizes[1])
    ]

    def gather_any_order(rows):
        other = lax.ppermute(rows, "c", [(0, 1), (1, 0)])
        chip = jnp.concatenate([rows, other], axis=1)
        away = [
            lax.ppermute(chip, "x", [(i, (i + k) % sizes[2]) for i in range(sizes[2])])
            for k in range(1, sizes[2])
        ]
        return jnp.concatenate([chip, *away], axis=1)

    def exchange(blocks, groups):
        return lax.all_to_all(blocks, AXES, 0, 0, tiled=True, axis_index_groups=groups)

    def on_device(grads, left_root, right_root, momentum, block_owner, owner_counts):
        slots = left_root.shape[1]
        place = jnp.stack([lax.axis_index(a) for a in ("z", "y", "c")]).astype(jnp.int32)
        got = exchange(deal(grads[0], place, block_owner, side), first_lines)
        table = tables(place, block_owner, owner_counts, side, slots)
        factors = jnp.concatenate([gather_any_order(left_root[0]), right_root[0]], axis=0)
        got, factors, table = lax.optimization_barrier((got, factors, table))
        got = exchange(sum_and_pick(got, table, TWO, side * slots, side), second_lines)
        got = exchange(sum_and_pick_here(got, table, THREE, side, side), first_lines)
        got = exchange(pick_and_repeat(got, table, OWN, slots, reps), rep_lines)
        new_moment, send = step(got, factors, momentum[0], table, side)
        got = exchange(send, first_lines)
        got = exchange(pick_and_repeat(got, table, BACK, side, 1), second_lines)
        update = pick_and_repeat(got, table, SOURCE, 1, 1)
        return (update, new_moment[None])

    return on_device


def solution(mesh):
    sizes = (8, 8, 4, 2)
    fine = Mesh(mesh.devices.reshape(sizes), AXES)
    dp, rep = ("z", "y"), ("x", "c")
    in_specs = (
        P(dp, None, rep, None),
        P(dp, None, rep, None),
        P(dp, None, None, None),
        P(dp, None, rep, None),
        P(),
        P(dp),
    )
    out_specs = (P(dp, rep, None), P(dp, None, rep, None))
    return jax.shard_map(
        make(sizes), mesh=fine, in_specs=in_specs, out_specs=out_specs, check_vma=False
    )
```

time: 132 us -> 129 us (0.977)
  blocking collectives: 52.2 us -> 78.5 us
  waiting for transfers between devices: 25 us -> 11 us
  starting transfers between devices: 30.5 us -> 22.4 us
  between operations: 6.73 us -> 1.45 us
  Pallas kernels: 7.34 us -> 11.5 us
  local copies, waits for them, and re-layouts: 6.42 us -> 2.31 us
  other arithmetic: 2.72 us -> 1.2 us
    all_to_all x3 -> x5, blocking collectives: 52.2 us -> 78.5 us  [exchange(): lax.all_to_all(blocks, AXES, 0, 0, tiled=True, axis_index_groups=groups)]
    all_to_all x3 -> x1, waiting for transfers between devices: 20.8 us -> 5.56 us  [exchange(): lax.all_to_all(blocks, AXES, 0, 0, tiled=True, axis_index_groups=groups)]
    all_to_all x3 -> x1, starting transfers between devices: 15.4 us -> 7.24 us  [exchange(): lax.all_to_all(blocks, AXES, 0, 0, tiled=True, axis_index_groups=groups)]
    pallas_call x5 -> x8, Pallas kernels: 7.34 us -> 11.5 us  [local_call(): pl.pallas_call(body, out_shape=outs, in_specs=ins, out_specs=jax.tree.map...]
    gather x2 -> x0, local copies, waits for them, and re-layouts: 2.63 us -> none  [pick(): return blocks.at[index].get(mode='promise_in_bounds')]
    dynamic_slice x4 -> x0, local copies, waits for them, and re-layouts: 2.38 us -> none  [the longest x1 0.62 us: on_device(): update = lax.dynamic_index_in_dim(got, source, 0, True)]
    reduce_sum x4 -> x0, other arithmetic: 1.91 us -> none  [the longest x1 1.45 us: on_device(): my_start = jnp.sum((key < w * side + u).astype(jnp.int32))]
  transfers between devices with their start and end apart: 7 -> 5, of which waited for: 5 -> 4; matrix products, arithmetic and copies ran while one was open for 3% -> 1% of each run, Pallas kernels for 0% -> 2%
where the time goes in v4:
time: 129 us; the launch traced here: 128 us
  blocking collectives  78.5 us (61%)
  starting transfers between devices  22.4 us (17%)
  Pallas kernels  11.5 us (9%)
  waiting for transfers between devices  11 us (9%)
  local copies, waits for them, and re-layouts  2.31 us (2%)
  between operations  1.45 us (1%)
    all_to_all x5, blocking collectives, exchange(): lax.all_to_all(blocks, AXES, 0, 0, tiled=True, axis_index_groups=groups)  78.5 us
    pallas_call x8, Pallas kernels, local_call(): pl.pallas_call(body, out_shape=outs, in_specs=ins, out_specs=jax.tree.map...  11.5 us
    ppermute x3, starting transfers between devices, gather_any_order(): lax.ppermute(chip, 'x', [(i, (i + k) % sizes[2]) for i in range(sizes[2])])  10.5 us
    all_to_all x1, starting transfers between devices, exchange(): lax.all_to_all(blocks, AXES, 0, 0, tiled=True, axis_index_groups=groups)  7.24 us
    all_to_all x1, waiting for transfers between devices, exchange(): lax.all_to_all(blocks, AXES, 0, 0, tiled=True, axis_index_groups=groups)  5.56 us
    ppermute x1, starting transfers between devices, gather_any_order(): other = lax.ppermute(rows, 'c', [(0, 1), (1, 0)])  4.69 us
    ppermute x3, waiting for transfers between devices, gather_any_order(): lax.ppermute(chip, 'x', [(i, (i + k) % sizes[2]) for i in range(sizes[2])])  4.53 us
  transfers between devices with their start and end apart: 5, of which 4 were waited for; matrix products, arithmetic and copies ran while one was open for 1% of the time, Pallas kernels for 2%

profile of v4, /device:TPU:2, one launch (start us, length us, event | category | flops | bytes accessed | tf_op | source)
XLA Modules:
  0.0 128.4 jit_solution(11754622757398810120)
XLA Ops:
  0.7 1.6 %copy-done = f32[1,64,32,256]{3,2,1,0:T(8,128)S(1)} copy-done((f32[1,64,32,256]{3,2,1,0:T(8,128)S(1)}, f32[1,64,32,256]{3,2,1,0:T(8,128)}, u32[]{:S(2)}) %copy-start) | copy-done | bytes 2097176
  2.3 0.7 copy-done.2
  3.0 2.5 %shard_map.77 = f32[64,32,256]{2,1,0:T(8,128)} custom-call(s32[3]{0:T(128)S(1)} %pad_add_fusion.place_ref, s32[64]{0:T(128)S(1)} %copy-done.2, f32[64,32,256]{2,1,0:T(8,128)S(1)} %bitcast.9), custom_call_target="tpu_custom_call" | custom-call | tf_op jit(solution)/shard_map/pallas_call | solution.py:39
  5.5 7.2 %all-to-all-start = ((f32[64,32,256]{2,1,0:T(8,128)}), f32[64,32,256]{2,1,0:T(8,128)S(1)}, u32[]{:S(2)}, u32[]{:S(2)}) async-start(f32[64,32,256]{2,1,0:T(8,128)} %shard_map.77), calls=%async_computation | async-start | bytes 4194304 | tf_op jit(solution)/shard_map/all_to_all | solution.py:231
  12.8 4.7 %collective-permute-start = (f32[2,32,256]{2,1,0:T(8,128)S(1)}, f32[2,32,256]{2,1,0:T(8,128)S(1)}, u32[]{:S(2)}, u32[]{:S(2)}) collective-permute-start(f32[2,32,256]{2,1,0:T(8,128)S(1)} %bitcast.12), channel_id=1, source_target_pairs={{0,1},{1,0},{2,3},{3,2},{4,5},{5,4},{6,7},{7,6},{8,9},{9,8},{10,11... | collective-permute-start | bytes 196616 | tf_op jit(solution)/shard_map/ppermute | solution.py:222
  17.5 0.9 collective-permute-done
  18.3 3.4 %collective-permute-start.1 = (f32[2,64,256]{2,1,0:T(8,128)S(1)}, f32[2,64,256]{2,1,0:T(8,128)S(1)}, u32[]{:S(2)}, u32[]{:S(2)}) collective-permute-start(f32[2,64,256]{2,1,0:T(8,128)S(1)} %pad_maximum_fusion.1), channel_id=1, source_target_pairs={{0,2},{2,4},{4,6},{6,0},{1,3},{3,5},{5,7},{7,1},{8,10},{10,12},{12... | collective-permute-start | bytes 393224 | tf_op jit(solution)/shard_map/ppermute | solution.py:225
  22.4 2.2 %shard_map.78.table_ref = s32[36]{0:T(128)S(1)} custom-call(s32[3]{0:T(128)S(1)} %pad_add_fusion.place_ref, s32[64]{0:T(128)S(1)} %copy-done.3, s32[1]{0:T(128)S(6)} %copy.12.count_ref), custom_call_target="tpu_custom_call" | custom-call | tf_op jit(solution)/shard_map/pallas_call | solution.py:39
  24.7 3.0 %collective-permute-start.2 = (f32[2,64,256]{2,1,0:T(8,128)S(1)}, f32[2,64,256]{2,1,0:T(8,128)S(1)}, u32[]{:S(2)}, u32[]{:S(2)}) collective-permute-start(f32[2,64,256]{2,1,0:T(8,128)S(1)} %pad_maximum_fusion.1), channel_id=1, source_target_pairs={{0,4},{2,6},{4,0},{6,2},{1,5},{3,7},{5,1},{7,3},{8,12},{10,14},{12... | collective-permute-start | bytes 393224 | tf_op jit(solution)/shard_map/ppermute | solution.py:225
  27.7 4.1 %collective-permute-start.3 = (f32[2,64,256]{2,1,0:T(8,128)S(1)}, f32[2,64,256]{2,1,0:T(8,128)S(1)}, u32[]{:S(2)}, u32[]{:S(2)}) collective-permute-start(f32[2,64,256]{2,1,0:T(8,128)S(1)} %pad_maximum_fusion.1), channel_id=1, source_target_pairs={{0,6},{2,0},{4,2},{6,4},{1,7},{3,1},{5,3},{7,5},{8,14},{10,8},{12,... | collective-permute-start | bytes 393224 | tf_op jit(solution)/shard_map/ppermute | solution.py:225
  31.8 2.6 %collective-permute-done.2 = f32[2,64,256]{2,1,0:T(8,128)S(1)} collective-permute-done((f32[2,64,256]{2,1,0:T(8,128)S(1)}, f32[2,64,256]{2,1,0:T(8,128)S(1)}, u32[]{:S(2)}, u32[]{:S(2)}) %collective-permute-start.2) | collective-permute-done | bytes 131104 | tf_op jit(solution)/shard_map/ppermute | solution.py:225
  34.4 1.9 %collective-permute-done.3 = f32[2,64,256]{2,1,0:T(8,128)S(1)} collective-permute-done((f32[2,64,256]{2,1,0:T(8,128)S(1)}, f32[2,64,256]{2,1,0:T(8,128)S(1)}, u32[]{:S(2)}, u32[]{:S(2)}) %collective-permute-start.3) | collective-permute-done | bytes 131104 | tf_op jit(solution)/shard_map/ppermute | solution.py:225
  36.3 1.1 pad_maximum_fusion.factor_ref
  37.5 5.6 %all-to-all-done.got_ref = f32[64,32,256]{2,1,0:T(8,128)S(1)} async-done(((f32[64,32,256]{2,1,0:T(8,128)}), f32[64,32,256]{2,1,0:T(8,128)S(1)}, u32[]{:S(2)}, u32[]{:S(2)}) %all-to-all-start) | async-done | bytes 2097184 | tf_op jit(solution)/shard_map/all_to_all | solution.py:231
  43.0 1.0 shard_map.79
  44.1 23.5 %all_to_all.30.got_ref = f32[16,32,256]{2,1,0:T(8,128)S(1)} all-to-all(f32[16,32,256]{2,1,0:T(8,128)S(1)} %shard_map.79), channel_id=1, replica_groups={{0,64,128,192,256,320,384,448},{8,72,136,200,264,328,392,456},{16,80,14..., dimensions={0} | all-to-all | bytes 1048576 | tf_op jit(solution)/shard_map/all_to_all | solution.py:231
  67.6 0.6 shard_map.80
  68.3 12.9 %all_to_all.31.got_ref = f32[8,32,256]{2,1,0:T(8,128)S(1)} all-to-all(f32[8,32,256]{2,1,0:T(8,128)S(1)} %shard_map.80), channel_id=1, replica_groups={{0,8,16,24,32,40,48,56},{64,72,80,88,96,104,112,120},{128,136,144,152,1..., dimensions={0} | all-to-all | bytes 524288 | tf_op jit(solution)/shard_map/all_to_all | solution.py:231
  81.1 0.6 shard_map.81
  81.7 13.6 %all_to_all.32.got_ref = f32[16,32,256]{2,1,0:T(8,128)S(1)} all-to-all(f32[16,32,256]{2,1,0:T(8,128)S(1)} %shard_map.81), channel_id=1, replica_groups={{0,1,2,3,4,5,6,7},{8,9,10,11,12,13,14,15},{16,17,18,19,20,21,22,23},{24..., dimensions={0} | all-to-all | bytes 1048576 | tf_op jit(solution)/shard_map/all_to_all | solution.py:231
  95.3 2.9 %shard_map.82 = (f32[2,32,256]{2,1,0:T(8,128)}, f32[16,32,256]{2,1,0:T(8,128)S(1)}) custom-call(s32[36]{0:T(128)S(1)} %shard_map.78.table_ref, f32[16,32,256]{2,1,0:T(8,128)S(1)} %all_to_all.32.got_ref, f32[4,256,256]{2,1,0:T(8,128)S(1)} %pad_maximum_fusion.factor_ref, f32[2,32,256]{2,1,0:T(8,128)S(1)} %bitcast.10), custom_call_target="tpu_custom_call" | custom-call | tf_op jit(solution)/shard_map/pallas_call | solution.py:39
  98.1 15.7 %all_to_all.33.got_ref = f32[16,32,256]{2,1,0:T(8,128)S(1)} all-to-all(f32[16,32,256]{2,1,0:T(8,128)S(1)} %get-tuple-element.10), channel_id=1, replica_groups={{0,8,16,24,32,40,48,56},{64,72,80,88,96,104,112,120},{128,136,144,152,1..., dimensions={0} | all-to-all | bytes 1048576 | tf_op jit(solution)/shard_map/all_to_all | solution.py:231
  114.4 12.9 %all_to_all.34.got_ref = f32[8,32,256]{2,1,0:T(8,128)S(1)} all-to-all(f32[8,32,256]{2,1,0:T(8,128)S(1)} %shard_map.83), channel_id=1, replica_groups={{0,64,128,192,256,320,384,448},{8,72,136,200,264,328,392,456},{16,80,14..., dimensions={0} | all-to-all | bytes 524288 | tf_op jit(solution)/shard_map/all_to_all | solution.py:231
  127.3 1.2 shard_map.84
  (17 shorter events, 0.7 us)
Async XLA Ops:
  0.7 1.6 %copy-start = (f32[1,64,32,256]{3,2,1,0:T(8,128)S(1)}, f32[1,64,32,256]{3,2,1,0:T(8,128)}, u32[]{:S(2)}) copy-start(f32[1,64,32,256]{3,2,1,0:T(8,128)} %param.6) | copy-start | bytes 6291460
  2.3 0.7 copy-start.2
  5.5 7.3 %copy-start.4 = (f32[1,2,32,256]{3,2,1,0:T(8,128)S(1)}, f32[1,2,32,256]{3,2,1,0:T(8,128)}, u32[]{:S(2)}) copy-start(f32[1,2,32,256]{3,2,1,0:T(8,128)} %param.7) | copy-start | bytes 196612
  5.5 16.9 %copy-start.3 = (s32[64]{0:T(128)S(1)}, s32[64]{0:T(128)}, u32[]{:S(2)}) copy-start(s32[64]{0:T(128)} %owner_ref.3) | copy-start | bytes 772
  5.5 37.5 %all-to-all-start = ((f32[64,32,256]{2,1,0:T(8,128)}), f32[64,32,256]{2,1,0:T(8,128)S(1)}, u32[]{:S(2)}, u32[]{:S(2)}) async-start(f32[64,32,256]{2,1,0:T(8,128)} %shard_map.77), calls=%async_computation | async-start | bytes 4194304 | tf_op jit(solution)/shard_map/all_to_all | solution.py:231
  12.8 5.6 %collective-permute-start = (f32[2,32,256]{2,1,0:T(8,128)S(1)}, f32[2,32,256]{2,1,0:T(8,128)S(1)}, u32[]{:S(2)}, u32[]{:S(2)}) collective-permute-start(f32[2,32,256]{2,1,0:T(8,128)S(1)} %bitcast.12), channel_id=1, source_target_pairs={{0,1},{1,0},{2,3},{3,2},{4,5},{5,4},{6,7},{7,6},{8,9},{9,8},{10,11... | collective-permute-start | bytes 196616 | tf_op jit(solution)/shard_map/ppermute | solution.py:222
  18.3 13.4 %collective-permute-start.1 = (f32[2,64,256]{2,1,0:T(8,128)S(1)}, f32[2,64,256]{2,1,0:T(8,128)S(1)}, u32[]{:S(2)}, u32[]{:S(2)}) collective-permute-start(f32[2,64,256]{2,1,0:T(8,128)S(1)} %pad_maximum_fusion.1), channel_id=1, source_target_pairs={{0,2},{2,4},{4,6},{6,0},{1,3},{3,5},{5,7},{7,1},{8,10},{10,12},{12... | collective-permute-start | bytes 393224 | tf_op jit(solution)/shard_map/ppermute | solution.py:225
  24.7 9.8 %collective-permute-start.2 = (f32[2,64,256]{2,1,0:T(8,128)S(1)}, f32[2,64,256]{2,1,0:T(8,128)S(1)}, u32[]{:S(2)}, u32[]{:S(2)}) collective-permute-start(f32[2,64,256]{2,1,0:T(8,128)S(1)} %pad_maximum_fusion.1), channel_id=1, source_target_pairs={{0,4},{2,6},{4,0},{6,2},{1,5},{3,7},{5,1},{7,3},{8,12},{10,14},{12... | collective-permute-start | bytes 393224 | tf_op jit(solution)/shard_map/ppermute | solution.py:225
  27.7 8.7 %collective-permute-start.3 = (f32[2,64,256]{2,1,0:T(8,128)S(1)}, f32[2,64,256]{2,1,0:T(8,128)S(1)}, u32[]{:S(2)}, u32[]{:S(2)}) collective-permute-start(f32[2,64,256]{2,1,0:T(8,128)S(1)} %pad_maximum_fusion.1), channel_id=1, source_target_pairs={{0,6},{2,0},{4,2},{6,4},{1,7},{3,1},{5,3},{7,5},{8,14},{10,8},{12,... | collective-permute-start | bytes 393224 | tf_op jit(solution)/shard_map/ppermute | solution.py:225
  44.1 51.2 %copy-start.1 = (f32[1,2,32,256]{3,2,1,0:T(8,128)S(1)}, f32[1,2,32,256]{3,2,1,0:T(8,128)}, u32[]{:S(2)}) copy-start(f32[1,2,32,256]{3,2,1,0:T(8,128)} %param.9) | copy-start | bytes 196612

commit v5 on v4

--- a/solution.py
+++ b/solution.py
@@ -8,7 +8,6 @@
 BETA = 0.9
 EPS = 1e-06
 AXES = ("z", "y", "x", "c")
-HIGHEST = lax.Precision.HIGHEST
 
 
 def device(z, y, x, c, sizes):
@@ -32,17 +31,17 @@
 
 
 ANY = pl.BlockSpec(memory_space=pl.ANY)
-TWO, THREE, OWN, BACK, SOURCE, COUNT, TABLE = 0, 16, 24, 26, 34, 35, 36
-
-
-def local_call(body, outs, ins, args, out_specs=None, scratch=()):
+TWO, THREE, OWN, BACK, SOURCE, COUNT, CORE, TABLE = 0, 16, 24, 26, 34, 35, 36, 37
+
+
+def local_call(body, outs, ins, args, out_specs=None, scratch=(), limit=24):
     return pl.pallas_call(
         body,
         out_shape=outs,
         in_specs=ins,
         out_specs=jax.tree.map(lambda _: VMEM, outs) if out_specs is None else out_specs,
         scratch_shapes=scratch,
-        compiler_params=pltpu.CompilerParams(vmem_limit_bytes=24 * 2**20),
+        compiler_params=pltpu.CompilerParams(vmem_limit_bytes=limit * 2**20),
     )(*args)
 
 
@@ -81,7 +80,7 @@
 
     scratch = [pltpu.SMEM((nb,), jnp.int32), pltpu.SMEM((side * side,), jnp.int32), pltpu.SemaphoreType.DMA(())]
     out = jax.ShapeDtypeStruct(parts.shape, parts.dtype)
-    return local_call(body, out, [SMEM, SMEM, ANY], (place, block_owner, parts), ANY, scratch)
+    return local_call(body, out, [SMEM, SMEM, ANY], (place, block_owner, parts), ANY, scratch, 60)
 
 
 def tables(place, block_owner, owner_counts, side, slots):
@@ -112,6 +111,7 @@
             out_ref[BACK + i] = (key & (side - 1)) * slots + slot_ref[b]
         out_ref[SOURCE] = key_of(owner_ref[z * side + y], flip, side) // side
         out_ref[COUNT] = count_ref[0]
+        out_ref[CORE] = place_ref[2]
 
     scratch = [pltpu.SMEM((nb,), jnp.int32), pltpu.SMEM((side * side,), jnp.int32), pltpu.SMEM((nb,), jnp.int32)]
     out = jax.ShapeDtypeStruct((TABLE,), jnp.int32)
@@ -171,20 +171,34 @@
     return local_call(body, out, [SMEM, VMEM], (table, got))
 
 
-def step(got, factors, moment, table, times):
+def halves(a):
+    high = a.astype(jnp.bfloat16)
+    return high, (a - high.astype(jnp.float32)).astype(jnp.bfloat16)
+
+
+def product(a, b):
+    (ah, al), (bh, bl) = halves(a), halves(b)
+
+    def dot(p, q):
+        return jnp.dot(p, q, preferred_element_type=jnp.float32)
+
+    return dot(ah, bh) + (dot(ah, bl) + dot(al, bh))
+
+
+def step(own, other, factors, moment, table, times):
     slots, rows, order = moment.shape
-    reps = order // rows
-
-    def body(table_ref, got_ref, factor_ref, moment_ref, moment_out_ref, send_ref):
-        held = table_ref[COUNT]
+    chips = own.shape[0] // slots
+
+    def body(table_ref, own_ref, other_ref, factor_ref, moment_ref, moment_out_ref, send_ref, whole_ref):
+        held, core = table_ref[COUNT], table_ref[CORE]
         for s in range(slots):
-            whole = jnp.concatenate([got_ref[r * slots + s] for r in range(reps)], axis=0)
-            right_part = jnp.dot(
-                whole, factor_ref[slots + s], precision=HIGHEST, preferred_element_type=jnp.float32
-            )
-            precond = jnp.dot(
-                factor_ref[s], right_part, precision=HIGHEST, preferred_element_type=jnp.float32
-            )
+            for x in range(chips):
+                whole_ref[s, 2 * x + core] = own_ref[x * slots + s]
+                whole_ref[s, 2 * x + 1 - core] = other_ref[x * slots + s]
+        for s in range(slots):
+            whole = whole_ref[s].reshape(order, order)
+            right_part = product(whole, factor_ref[slots + s])
+            precond = product(factor_ref[s], right_part)
             entries = order * order
             grad_mean = jnp.sum(whole * whole, keepdims=True) / entries
             pre_mean = jnp.sum(precond * precond, keepdims=True) / entries
@@ -201,21 +215,22 @@
         jax.ShapeDtypeStruct(moment.shape, moment.dtype),
         jax.ShapeDtypeStruct((times * slots, rows, order), moment.dtype),
     )
+    scratch = [pltpu.VMEM((slots, order // rows, rows, order), moment.dtype)]
     return local_call(
-        body, outs, [SMEM, VMEM, VMEM, VMEM], (table, got, factors, moment)
+        body, outs, [SMEM, VMEM, VMEM, VMEM, VMEM], (table, own, other, factors, moment), None, scratch
     )
 
 
 def make(sizes):
     side = sizes[0]
-    reps = sizes[2] * sizes[3]
     first_lines = lines(sizes, ("y", "z"))
     second_lines = lines(sizes, ("z", "y"))
 
-    rep_lines = [
-        [device(z, y, x, c, sizes) for x in range(sizes[2]) for c in range(sizes[3])]
+    chip_lines = [
+        [device(z, y, x, c, sizes) for x in range(sizes[2])]
         for z in range(sizes[0])
         for y in range(sizes[1])
+        for c in range(sizes[3])
     ]
 
     def gather_any_order(rows):
@@ -236,14 +251,17 @@
         got = exchange(deal(grads[0], place, block_owner, side), first_lines)
         table = tables(place, block_owner, owner_counts, side, slots)
         factors = jnp.concatenate([gather_any_order(left_root[0]), right_root[0]], axis=0)
-        got, factors, table = lax.optimization_barrier((got, factors, table))
+        source = table[SOURCE].astype(jnp.uint32)
+        got, factors, table, source = lax.optimization_barrier((got, factors, table, source))
         got = exchange(sum_and_pick(got, table, TWO, side * slots, side), second_lines)
         got = exchange(sum_and_pick_here(got, table, THREE, side, side), first_lines)
-        got = exchange(pick_and_repeat(got, table, OWN, slots, reps), rep_lines)
-        new_moment, send = step(got, factors, momentum[0], table, side)
+        own = exchange(pick_and_repeat(got, table, OWN, slots, sizes[2]), chip_lines)
+        other = lax.ppermute(own, "c", [(0, 1), (1, 0)])
+        new_moment, send = step(own, other, factors, momentum[0], table, side)
         got = exchange(send, first_lines)
         got = exchange(pick_and_repeat(got, table, BACK, side, 1), second_lines)
-        update = pick_and_repeat(got, table, SOURCE, 1, 1)
+        zero = jnp.uint32(0)
+        update = lax.dynamic_slice(got, (source, zero, zero), (1, *got.shape[1:]))
         return (update, new_moment[None])
 
     return on_device

time: 129 us -> 189 us (1.47)
  Pallas kernels: 11.5 us -> 73.1 us
  blocking collectives: 78.5 us -> 74.8 us
  starting transfers between devices: 22.4 us -> 24.3 us
    pallas_call x8 -> x7, Pallas kernels: 11.5 us -> 73.1 us  [local_call(): pl.pallas_call(body, out_shape=outs, in_specs=ins, out_specs=jax.tree.map...]
    all_to_all x5, blocking collectives: 78.5 us -> 74.8 us  [exchange(): lax.all_to_all(blocks, AXES, 0, 0, tiled=True, axis_index_groups=groups)]
    unnamed x14 -> x12, local copies, waits for them, and re-layouts: 2.3 us -> 0.06 us
    ppermute x0 -> x1, starting transfers between devices: none -> 1.91 us  [on_device(): other = lax.ppermute(own, 'c', [(0, 1), (1, 0)])]
  transfers between devices with their start and end apart: 5 -> 6, of which waited for: 4 -> 5; matrix products, arithmetic and copies ran while one was open for 1% -> 1% of each run, Pallas kernels for 2% -> 1%
where the time goes in v5:
time: 189 us
  blocking collectives  74.8 us (40%)
  Pallas kernels  73.1 us (39%)
  starting transfers between devices  24.3 us (13%)
  waiting for transfers between devices  11.2 us (6%)
  between operations  2.13 us (1%)
    all_to_all x5, blocking collectives, exchange(): lax.all_to_all(blocks, AXES, 0, 0, tiled=True, axis_index_groups=groups)  74.8 us
    pallas_call x7, Pallas kernels, local_call(): pl.pallas_call(body, out_shape=outs, in_specs=ins, out_specs=jax.tree.map...  73.1 us
    ppermute x3, starting transfers between devices, gather_any_order(): lax.ppermute(chip, 'x', [(i, (i + k) % sizes[2]) for i in range(sizes[2])])  10.5 us
    all_to_all x1, starting transfers between devices, exchange(): lax.all_to_all(blocks, AXES, 0, 0, tiled=True, axis_index_groups=groups)  7.24 us
    ppermute x1, starting transfers between devices, gather_any_order(): other = lax.ppermute(rows, 'c', [(0, 1), (1, 0)])  4.68 us
    ppermute x3, waiting for transfers between devices, gather_any_order(): lax.ppermute(chip, 'x', [(i, (i + k) % sizes[2]) for i in range(sizes[2])])  4.53 us
    all_to_all x1, waiting for transfers between devices, exchange(): lax.all_to_all(blocks, AXES, 0, 0, tiled=True, axis_index_groups=groups)  4.32 us
  transfers between devices with their start and end apart: 6, of which 5 were waited for; matrix products, arithmetic and copies ran while one was open for 1% of the time, Pallas kernels for 1%

profile of v5, /device:TPU:2, one launch (start us, length us, event | category | flops | bytes accessed | tf_op | source)
XLA Modules:
  0.0 188.6 jit_solution(5213705773199151957)
XLA Ops:
  0.6 0.7 pad_add_fusion.place_ref
  1.3 65.8 %shard_map.77 = f32[64,32,256]{2,1,0:T(8,128)} custom-call(s32[3]{0:T(128)} %pad_add_fusion.place_ref, s32[64]{0:T(128)} %owner_ref.3, f32[64,32,256]{2,1,0:T(8,128)} %bitcast.11), custom_call_target="tpu_custom_call" | custom-call | tf_op jit(solution)/shard_map/pallas_call | solution.py:38
  67.2 7.2 %all-to-all-start = ((f32[64,32,256]{2,1,0:T(8,128)}), f32[64,32,256]{2,1,0:T(8,128)S(1)}, u32[]{:S(2)}, u32[]{:S(2)}) async-start(f32[64,32,256]{2,1,0:T(8,128)} %shard_map.77), calls=%async_computation | async-start | bytes 4194304 | tf_op jit(solution)/shard_map/all_to_all | solution.py:246
  74.4 4.7 %collective-permute-start = (f32[2,32,256]{2,1,0:T(8,128)S(1)}, f32[2,32,256]{2,1,0:T(8,128)S(1)}, u32[]{:S(2)}, u32[]{:S(2)}) collective-permute-start(f32[2,32,256]{2,1,0:T(8,128)S(1)} %bitcast.13), channel_id=1, source_target_pairs={{0,1},{1,0},{2,3},{3,2},{4,5},{5,4},{6,7},{7,6},{8,9},{9,8},{10,11... | collective-permute-start | bytes 196616 | tf_op jit(solution)/shard_map/ppermute | solution.py:237
  79.1 0.9 collective-permute-done
  80.0 3.4 %collective-permute-start.1 = (f32[2,64,256]{2,1,0:T(8,128)S(1)}, f32[2,64,256]{2,1,0:T(8,128)S(1)}, u32[]{:S(2)}, u32[]{:S(2)}) collective-permute-start(f32[2,64,256]{2,1,0:T(8,128)S(1)} %pad_maximum_fusion.1), channel_id=1, source_target_pairs={{0,2},{2,4},{4,6},{6,0},{1,3},{3,5},{5,7},{7,1},{8,10},{10,12},{12... | collective-permute-start | bytes 393224 | tf_op jit(solution)/shard_map/ppermute | solution.py:240
  84.1 2.2 %shard_map.78.table_ref = s32[37]{0:T(128)S(1)} custom-call(s32[3]{0:T(128)S(1)} %copy-done.1, s32[64]{0:T(128)S(1)} %copy-done.2, s32[1]{0:T(128)S(6)} %copy.12.count_ref), custom_call_target="tpu_custom_call" | custom-call | tf_op jit(solution)/shard_map/pallas_call | solution.py:38
  87.5 3.0 %collective-permute-start.2 = (f32[2,64,256]{2,1,0:T(8,128)S(1)}, f32[2,64,256]{2,1,0:T(8,128)S(1)}, u32[]{:S(2)}, u32[]{:S(2)}) collective-permute-start(f32[2,64,256]{2,1,0:T(8,128)S(1)} %pad_maximum_fusion.1), channel_id=1, source_target_pairs={{0,4},{2,6},{4,0},{6,2},{1,5},{3,7},{5,1},{7,3},{8,12},{10,14},{12... | collective-permute-start | bytes 393224 | tf_op jit(solution)/shard_map/ppermute | solution.py:240
  90.6 4.1 %collective-permute-start.3 = (f32[2,64,256]{2,1,0:T(8,128)S(1)}, f32[2,64,256]{2,1,0:T(8,128)S(1)}, u32[]{:S(2)}, u32[]{:S(2)}) collective-permute-start(f32[2,64,256]{2,1,0:T(8,128)S(1)} %pad_maximum_fusion.1), channel_id=1, source_target_pairs={{0,6},{2,0},{4,2},{6,4},{1,7},{3,1},{5,3},{7,5},{8,14},{10,8},{12,... | collective-permute-start | bytes 393224 | tf_op jit(solution)/shard_map/ppermute | solution.py:240
  94.7 2.6 %collective-permute-done.2 = f32[2,64,256]{2,1,0:T(8,128)S(1)} collective-permute-done((f32[2,64,256]{2,1,0:T(8,128)S(1)}, f32[2,64,256]{2,1,0:T(8,128)S(1)}, u32[]{:S(2)}, u32[]{:S(2)}) %collective-permute-start.2) | collective-permute-done | bytes 131104 | tf_op jit(solution)/shard_map/ppermute | solution.py:240
  97.3 1.9 %collective-permute-done.3 = f32[2,64,256]{2,1,0:T(8,128)S(1)} collective-permute-done((f32[2,64,256]{2,1,0:T(8,128)S(1)}, f32[2,64,256]{2,1,0:T(8,128)S(1)}, u32[]{:S(2)}, u32[]{:S(2)}) %collective-permute-start.3) | collective-permute-done | bytes 131104 | tf_op jit(solution)/shard_map/ppermute | solution.py:240
  99.2 1.1 pad_maximum_fusion.factor_ref
  100.4 4.3 %all-to-all-done.got_ref = f32[64,32,256]{2,1,0:T(8,128)S(1)} async-done(((f32[64,32,256]{2,1,0:T(8,128)}), f32[64,32,256]{2,1,0:T(8,128)S(1)}, u32[]{:S(2)}, u32[]{:S(2)}) %all-to-all-start) | async-done | bytes 2097184 | tf_op jit(solution)/shard_map/all_to_all | solution.py:246
  104.7 1.0 shard_map.79
  105.7 23.5 %all_to_all.30.got_ref = f32[16,32,256]{2,1,0:T(8,128)S(1)} all-to-all(f32[16,32,256]{2,1,0:T(8,128)S(1)} %shard_map.79), channel_id=1, replica_groups={{0,64,128,192,256,320,384,448},{8,72,136,200,264,328,392,456},{16,80,14..., dimensions={0} | all-to-all | bytes 1048576 | tf_op jit(solution)/shard_map/all_to_all | solution.py:246
  129.3 0.6 shard_map.80
  129.9 12.9 %all_to_all.31.got_ref = f32[8,32,256]{2,1,0:T(8,128)S(1)} all-to-all(f32[8,32,256]{2,1,0:T(8,128)S(1)} %shard_map.80), channel_id=1, replica_groups={{0,8,16,24,32,40,48,56},{64,72,80,88,96,104,112,120},{128,136,144,152,1..., dimensions={0} | all-to-all | bytes 524288 | tf_op jit(solution)/shard_map/all_to_all | solution.py:246
  143.4 9.8 %all_to_all.32.own_ref = f32[8,32,256]{2,1,0:T(8,128)S(1)} all-to-all(f32[8,32,256]{2,1,0:T(8,128)S(1)} %shard_map.81), channel_id=1, replica_groups={{0,2,4,6},{1,3,5,7},{8,10,12,14},{9,11,13,15},{16,18,20,22},{17,19,21,2..., dimensions={0} | all-to-all | bytes 524288 | tf_op jit(solution)/shard_map/all_to_all | solution.py:246
  153.2 1.9 %collective-permute-start.4 = (f32[8,32,256]{2,1,0:T(8,128)S(1)}, f32[8,32,256]{2,1,0:T(8,128)S(1)}, u32[]{:S(2)}, u32[]{:S(2)}) collective-permute-start(f32[8,32,256]{2,1,0:T(8,128)S(1)} %all_to_all.32.own_ref), channel_id=1, source_target_pairs={{0,1},{1,0},{2,3},{3,2},{4,5},{5,4},{6,7},{7,6},{8,9},{9,8},{10,11... | collective-permute-start | bytes 786440 | tf_op jit(solution)/shard_map/ppermute | solution.py:259
  155.1 1.5 collective-permute-done.4.other_ref
  156.6 2.2 %shard_map.82 = (f32[2,32,256]{2,1,0:T(8,128)}, f32[16,32,256]{2,1,0:T(8,128)S(1)}) custom-call(s32[37]{0:T(128)S(1)} %shard_map.78.table_ref, f32[8,32,256]{2,1,0:T(8,128)S(1)} %all_to_all.32.own_ref, f32[8,32,256]{2,1,0:T(8,128)S(1)} %collective-permute-done.4.other_ref, f32[4,256,256]{2,1,0:T(8,128)S(1)} %pad_maximum_fusion.factor_ref, ...), custom_call_target="tpu_custom_call" | custom-call | tf_op jit(solution)/shard_map/pallas_call | solution.py:38
  158.9 15.7 %all_to_all.33.got_ref = f32[16,32,256]{2,1,0:T(8,128)S(1)} all-to-all(f32[16,32,256]{2,1,0:T(8,128)S(1)} %get-tuple-element.11), channel_id=1, replica_groups={{0,8,16,24,32,40,48,56},{64,72,80,88,96,104,112,120},{128,136,144,152,1..., dimensions={0} | all-to-all | bytes 1048576 | tf_op jit(solution)/shard_map/all_to_all | solution.py:246
  175.1 12.9 %all_to_all.34 = f32[8,32,256]{2,1,0:T(8,128)S(1)} all-to-all(f32[8,32,256]{2,1,0:T(8,128)S(1)} %shard_map.83), channel_id=1, replica_groups={{0,64,128,192,256,320,384,448},{8,72,136,200,264,328,392,456},{16,80,14..., dimensions={0} | all-to-all | bytes 524288 | tf_op jit(solution)/shard_map/all_to_all | solution.py:246
  188.0 0.6 constant_dynamic-slice_fusion
  (18 shorter events, 1.8 us)
Async XLA Ops:
  67.1 7.3 %copy-start.3 = (f32[1,2,32,256]{3,2,1,0:T(8,128)S(1)}, f32[1,2,32,256]{3,2,1,0:T(8,128)}, u32[]{:S(2)}) copy-start(f32[1,2,32,256]{3,2,1,0:T(8,128)} %param.7) | copy-start | bytes 196612
  67.1 16.9 %copy-start.1 = (s32[3]{0:T(128)S(1)}, s32[3]{0:T(128)}, u32[]{:S(2)}) copy-start(s32[3]{0:T(128)} %pad_add_fusion.place_ref) | copy-start | bytes 40
  67.2 16.9 %copy-start.2 = (s32[64]{0:T(128)S(1)}, s32[64]{0:T(128)}, u32[]{:S(2)}) copy-start(s32[64]{0:T(128)} %owner_ref.3) | copy-start | bytes 772
  67.2 37.5 %all-to-all-start = ((f32[64,32,256]{2,1,0:T(8,128)}), f32[64,32,256]{2,1,0:T(8,128)S(1)}, u32[]{:S(2)}, u32[]{:S(2)}) async-start(f32[64,32,256]{2,1,0:T(8,128)} %shard_map.77), calls=%async_computation | async-start | bytes 4194304 | tf_op jit(solution)/shard_map/all_to_all | solution.py:246
  74.4 5.6 %collective-permute-start = (f32[2,32,256]{2,1,0:T(8,128)S(1)}, f32[2,32,256]{2,1,0:T(8,128)S(1)}, u32[]{:S(2)}, u32[]{:S(2)}) collective-permute-start(f32[2,32,256]{2,1,0:T(8,128)S(1)} %bitcast.13), channel_id=1, source_target_pairs={{0,1},{1,0},{2,3},{3,2},{4,5},{5,4},{6,7},{7,6},{8,9},{9,8},{10,11... | collective-permute-start | bytes 196616 | tf_op jit(solution)/shard_map/ppermute | solution.py:237
  80.0 14.7 %collective-permute-start.1 = (f32[2,64,256]{2,1,0:T(8,128)S(1)}, f32[2,64,256]{2,1,0:T(8,128)S(1)}, u32[]{:S(2)}, u32[]{:S(2)}) collective-permute-start(f32[2,64,256]{2,1,0:T(8,128)S(1)} %pad_maximum_fusion.1), channel_id=1, source_target_pairs={{0,2},{2,4},{4,6},{6,0},{1,3},{3,5},{5,7},{7,1},{8,10},{10,12},{12... | collective-permute-start | bytes 393224 | tf_op jit(solution)/shard_map/ppermute | solution.py:240
  87.5 9.8 %collective-permute-start.2 = (f32[2,64,256]{2,1,0:T(8,128)S(1)}, f32[2,64,256]{2,1,0:T(8,128)S(1)}, u32[]{:S(2)}, u32[]{:S(2)}) collective-permute-start(f32[2,64,256]{2,1,0:T(8,128)S(1)} %pad_maximum_fusion.1), channel_id=1, source_target_pairs={{0,4},{2,6},{4,0},{6,2},{1,5},{3,7},{5,1},{7,3},{8,12},{10,14},{12... | collective-permute-start | bytes 393224 | tf_op jit(solution)/shard_map/ppermute | solution.py:240
  90.6 8.7 %collective-permute-start.3 = (f32[2,64,256]{2,1,0:T(8,128)S(1)}, f32[2,64,256]{2,1,0:T(8,128)S(1)}, u32[]{:S(2)}, u32[]{:S(2)}) collective-permute-start(f32[2,64,256]{2,1,0:T(8,128)S(1)} %pad_maximum_fusion.1), channel_id=1, source_target_pairs={{0,6},{2,0},{4,2},{6,4},{1,7},{3,1},{5,3},{7,5},{8,14},{10,8},{12,... | collective-permute-start | bytes 393224 | tf_op jit(solution)/shard_map/ppermute | solution.py:240
  105.7 50.9 %copy-start = (f32[1,2,32,256]{3,2,1,0:T(8,128)S(1)}, f32[1,2,32,256]{3,2,1,0:T(8,128)}, u32[]{:S(2)}) copy-start(f32[1,2,32,256]{3,2,1,0:T(8,128)} %param.9) | copy-start | bytes 196612
  153.2 3.4 %collective-permute-start.4 = (f32[8,32,256]{2,1,0:T(8,128)S(1)}, f32[8,32,256]{2,1,0:T(8,128)S(1)}, u32[]{:S(2)}, u32[]{:S(2)}) collective-permute-start(f32[8,32,256]{2,1,0:T(8,128)S(1)} %all_to_all.32.own_ref), channel_id=1, source_target_pairs={{0,1},{1,0},{2,3},{3,2},{4,5},{5,4},{6,7},{7,6},{8,9},{9,8},{10,11... | collective-permute-start | bytes 786440 | tf_op jit(solution)/shard_map/ppermute | solution.py:259

commit v6 on v5

--- a/solution.py
+++ b/solution.py
@@ -50,9 +50,8 @@
     return jnp.where(flip, turned, owner)
 
 
-def sort_blocks(place_ref, owner_ref, slot_ref, start_ref, side):
+def sort_blocks(flip, owner_ref, slot_ref, start_ref, side):
     nb = owner_ref.shape[0]
-    flip = place_ref[2] == 1
     for k in range(side * side):
         start_ref[k] = 0
     for b in range(nb):
@@ -66,30 +65,40 @@
         total = total + held
 
 
-def deal(parts, place, block_owner, side):
+def deal(parts, block_owner, side):
     nb = parts.shape[0]
 
-    def body(place_ref, owner_ref, parts_ref, out_ref, slot_ref, start_ref, sem):
-        flip = place_ref[2] == 1
-        sort_blocks(place_ref, owner_ref, slot_ref, start_ref, side)
+    def body(owner_ref, parts_ref, out_ref, held_ref, slot_ref, start_ref, in_sem, out_sem):
+        fetch = pltpu.make_async_copy(parts_ref, held_ref, in_sem)
+        fetch.start()
+        flip = lax.axis_index("c") == 1
+        sort_blocks(flip, owner_ref, slot_ref, start_ref, side)
+        fetch.wait()
         for b in range(nb):
             rank = start_ref[key_of(owner_ref[b], flip, side)] + slot_ref[b]
             to = (rank & (side - 1)) * (nb // side) + rank // side
-            pltpu.make_async_copy(parts_ref.at[b], out_ref.at[to], sem).start()
-        pltpu.make_async_copy(parts_ref, out_ref, sem).wait()
-
-    scratch = [pltpu.SMEM((nb,), jnp.int32), pltpu.SMEM((side * side,), jnp.int32), pltpu.SemaphoreType.DMA(())]
+            pltpu.make_async_copy(held_ref.at[b], out_ref.at[to], out_sem).start()
+        pltpu.make_async_copy(held_ref, out_ref, out_sem).wait()
+
+    scratch = [
+        pltpu.VMEM(parts.shape, parts.dtype),
+        pltpu.SMEM((nb,), jnp.int32),
+        pltpu.SMEM((side * side,), jnp.int32),
+        pltpu.SemaphoreType.DMA(()),
+        pltpu.SemaphoreType.DMA(()),
+    ]
     out = jax.ShapeDtypeStruct(parts.shape, parts.dtype)
-    return local_call(body, out, [SMEM, SMEM, ANY], (place, block_owner, parts), ANY, scratch, 60)
-
-
-def tables(place, block_owner, owner_counts, side, slots):
+    return local_call(body, out, [SMEM, ANY], (block_owner, parts), ANY, scratch, 60)
+
+
+def tables(block_owner, owner_counts, side, slots):
     nb = block_owner.shape[0]
 
-    def body(place_ref, owner_ref, count_ref, out_ref, slot_ref, start_ref, key_at_ref):
-        z, y, flip = place_ref[0], place_ref[1], place_ref[2] == 1
+    def body(owner_ref, count_ref, out_ref, slot_ref, start_ref, key_at_ref):
+        z, y, core = lax.axis_index("z"), lax.axis_index("y"), lax.axis_index("c")
+        flip = core == 1
         u, w = jnp.where(flip, z, y), jnp.where(flip, y, z)
-        sort_blocks(place_ref, owner_ref, slot_ref, start_ref, side)
+        sort_blocks(flip, owner_ref, slot_ref, start_ref, side)
         for b in range(nb):
             key = key_of(owner_ref[b], flip, side)
             key_at_ref[start_ref[key] + slot_ref[b]] = key
@@ -111,11 +120,11 @@
             out_ref[BACK + i] = (key & (side - 1)) * slots + slot_ref[b]
         out_ref[SOURCE] = key_of(owner_ref[z * side + y], flip, side) // side
         out_ref[COUNT] = count_ref[0]
-        out_ref[CORE] = place_ref[2]
+        out_ref[CORE] = core
 
     scratch = [pltpu.SMEM((nb,), jnp.int32), pltpu.SMEM((side * side,), jnp.int32), pltpu.SMEM((nb,), jnp.int32)]
     out = jax.ShapeDtypeStruct((TABLE,), jnp.int32)
-    return local_call(body, out, [SMEM, SMEM, SMEM], (place, block_owner, owner_counts), SMEM, scratch)
+    return local_call(body, out, [SMEM, SMEM], (block_owner, owner_counts), SMEM, scratch)
 
 
 def sum_and_pick(got, table, base, count, sources):
@@ -247,9 +256,8 @@
 
     def on_device(grads, left_root, right_root, momentum, block_owner, owner_counts):
         slots = left_root.shape[1]
-        place = jnp.stack([lax.axis_index(a) for a in ("z", "y", "c")]).astype(jnp.int32)
-        got = exchange(deal(grads[0], place, block_owner, side), first_lines)
-        table = tables(place, block_owner, owner_counts, side, slots)
+        got = exchange(deal(grads[0], block_owner, side), first_lines)
+        table = tables(block_owner, owner_counts, side, slots)
         factors = jnp.concatenate([gather_any_order(left_root[0]), right_root[0]], axis=0)
         source = table[SOURCE].astype(jnp.uint32)
         got, factors, table, source = lax.optimization_barrier((got, factors, table, source))

time: 189 us -> 126 us (0.67)
  Pallas kernels: 73.1 us -> 10.9 us
    pallas_call x7, Pallas kernels: 73.1 us -> 10.9 us  [local_call(): pl.pallas_call(body, out_shape=outs, in_specs=ins, out_specs=jax.tree.map...]
  transfers between devices with their start and end apart: 6 -> 6, of which waited for: 5 -> 5; matrix products, arithmetic and copies ran while one was open for 1% -> 1% of each run, Pallas kernels for 1% -> 2%
where the time goes in v6:
time: 126 us
  blocking collectives  74.8 us (59%)
  starting transfers between devices  24.3 us (19%)
  waiting for transfers between devices  11.3 us (9%)
  Pallas kernels  10.9 us (9%)
  between operations  2.1 us (2%)
  local copies, waits for them, and re-layouts  1.26 us (1%)
    all_to_all x5, blocking collectives, exchange(): lax.all_to_all(blocks, AXES, 0, 0, tiled=True, axis_index_groups=groups)  74.8 us
    pallas_call x7, Pallas kernels, local_call(): pl.pallas_call(body, out_shape=outs, in_specs=ins, out_specs=jax.tree.map...  10.9 us
    ppermute x3, starting transfers between devices, gather_any_order(): lax.ppermute(chip, 'x', [(i, (i + k) % sizes[2]) for i in range(sizes[2])])  10.5 us
    all_to_all x1, starting transfers between devices, exchange(): lax.all_to_all(blocks, AXES, 0, 0, tiled=True, axis_index_groups=groups)  7.24 us
    ppermute x1, starting transfers between devices, gather_any_order(): other = lax.ppermute(rows, 'c', [(0, 1), (1, 0)])  4.63 us
    ppermute x3, waiting for transfers between devices, gather_any_order(): lax.ppermute(chip, 'x', [(i, (i + k) % sizes[2]) for i in range(sizes[2])])  4.53 us
    all_to_all x1, waiting for transfers between devices, exchange(): lax.all_to_all(blocks, AXES, 0, 0, tiled=True, axis_index_groups=groups)  4.35 us
  transfers between devices with their start and end apart: 6, of which 5 were waited for; matrix products, arithmetic and copies ran while one was open for 1% of the time, Pallas kernels for 2%

profile of v6, /device:TPU:2, one launch (start us, length us, event | category | flops | bytes accessed | tf_op | source)
XLA Modules:
  0.0 125.8 jit_solution(449079720602904948)
XLA Ops:
  0.6 3.6 %shard_map.77 = f32[64,32,256]{2,1,0:T(8,128)} custom-call(s32[64]{0:T(128)} %owner_ref.3, f32[64,32,256]{2,1,0:T(8,128)} %bitcast.8), custom_call_target="tpu_custom_call" | custom-call | tf_op jit(solution)/shard_map/pallas_call | solution.py:38
  4.3 7.2 %all-to-all-start = ((f32[64,32,256]{2,1,0:T(8,128)}), f32[64,32,256]{2,1,0:T(8,128)S(1)}, u32[]{:S(2)}, u32[]{:S(2)}) async-start(f32[64,32,256]{2,1,0:T(8,128)} %shard_map.77), calls=%async_computation | async-start | bytes 4194304 | tf_op jit(solution)/shard_map/all_to_all | solution.py:255
  11.5 4.6 %collective-permute-start = (f32[2,32,256]{2,1,0:T(8,128)S(1)}, f32[2,32,256]{2,1,0:T(8,128)S(1)}, u32[]{:S(2)}, u32[]{:S(2)}) collective-permute-start(f32[2,32,256]{2,1,0:T(8,128)S(1)} %bitcast.10), channel_id=1, source_target_pairs={{0,1},{1,0},{2,3},{3,2},{4,5},{5,4},{6,7},{7,6},{8,9},{9,8},{10,11... | collective-permute-start | bytes 196616 | tf_op jit(solution)/shard_map/ppermute | solution.py:246
  16.2 0.9 collective-permute-done
  17.1 3.4 %collective-permute-start.1 = (f32[2,64,256]{2,1,0:T(8,128)S(1)}, f32[2,64,256]{2,1,0:T(8,128)S(1)}, u32[]{:S(2)}, u32[]{:S(2)}) collective-permute-start(f32[2,64,256]{2,1,0:T(8,128)S(1)} %pad_maximum_fusion.1), channel_id=1, source_target_pairs={{0,2},{2,4},{4,6},{6,0},{1,3},{3,5},{5,7},{7,1},{8,10},{10,12},{12... | collective-permute-start | bytes 393224 | tf_op jit(solution)/shard_map/ppermute | solution.py:249
  21.1 2.2 %shard_map.78.table_ref = s32[37]{0:T(128)S(1)} custom-call(s32[64]{0:T(128)S(1)} %copy-done.1, s32[1]{0:T(128)S(6)} %copy.12.count_ref), custom_call_target="tpu_custom_call" | custom-call | tf_op jit(solution)/shard_map/pallas_call | solution.py:38
  23.4 0.6 slice.3
  24.6 3.0 %collective-permute-start.2 = (f32[2,64,256]{2,1,0:T(8,128)S(1)}, f32[2,64,256]{2,1,0:T(8,128)S(1)}, u32[]{:S(2)}, u32[]{:S(2)}) collective-permute-start(f32[2,64,256]{2,1,0:T(8,128)S(1)} %pad_maximum_fusion.1), channel_id=1, source_target_pairs={{0,4},{2,6},{4,0},{6,2},{1,5},{3,7},{5,1},{7,3},{8,12},{10,14},{12... | collective-permute-start | bytes 393224 | tf_op jit(solution)/shard_map/ppermute | solution.py:249
  27.6 4.1 %collective-permute-start.3 = (f32[2,64,256]{2,1,0:T(8,128)S(1)}, f32[2,64,256]{2,1,0:T(8,128)S(1)}, u32[]{:S(2)}, u32[]{:S(2)}) collective-permute-start(f32[2,64,256]{2,1,0:T(8,128)S(1)} %pad_maximum_fusion.1), channel_id=1, source_target_pairs={{0,6},{2,0},{4,2},{6,4},{1,7},{3,1},{5,3},{7,5},{8,14},{10,8},{12,... | collective-permute-start | bytes 393224 | tf_op jit(solution)/shard_map/ppermute | solution.py:249
  31.8 2.6 %collective-permute-done.2 = f32[2,64,256]{2,1,0:T(8,128)S(1)} collective-permute-done((f32[2,64,256]{2,1,0:T(8,128)S(1)}, f32[2,64,256]{2,1,0:T(8,128)S(1)}, u32[]{:S(2)}, u32[]{:S(2)}) %collective-permute-start.2) | collective-permute-done | bytes 131104 | tf_op jit(solution)/shard_map/ppermute | solution.py:249
  34.4 1.9 %collective-permute-done.3 = f32[2,64,256]{2,1,0:T(8,128)S(1)} collective-permute-done((f32[2,64,256]{2,1,0:T(8,128)S(1)}, f32[2,64,256]{2,1,0:T(8,128)S(1)}, u32[]{:S(2)}, u32[]{:S(2)}) %collective-permute-start.3) | collective-permute-done | bytes 131104 | tf_op jit(solution)/shard_map/ppermute | solution.py:249
  36.3 1.1 pad_maximum_fusion.factor_ref
  37.5 4.4 %all-to-all-done.got_ref = f32[64,32,256]{2,1,0:T(8,128)S(1)} async-done(((f32[64,32,256]{2,1,0:T(8,128)}), f32[64,32,256]{2,1,0:T(8,128)S(1)}, u32[]{:S(2)}, u32[]{:S(2)}) %all-to-all-start) | async-done | bytes 2097184 | tf_op jit(solution)/shard_map/all_to_all | solution.py:255
  41.8 1.0 shard_map.79
  42.9 23.5 %all_to_all.30.got_ref = f32[16,32,256]{2,1,0:T(8,128)S(1)} all-to-all(f32[16,32,256]{2,1,0:T(8,128)S(1)} %shard_map.79), channel_id=1, replica_groups={{0,64,128,192,256,320,384,448},{8,72,136,200,264,328,392,456},{16,80,14..., dimensions={0} | all-to-all | bytes 1048576 | tf_op jit(solution)/shard_map/all_to_all | solution.py:255
  66.4 0.6 shard_map.80
  67.0 12.9 %all_to_all.31.got_ref = f32[8,32,256]{2,1,0:T(8,128)S(1)} all-to-all(f32[8,32,256]{2,1,0:T(8,128)S(1)} %shard_map.80), channel_id=1, replica_groups={{0,8,16,24,32,40,48,56},{64,72,80,88,96,104,112,120},{128,136,144,152,1..., dimensions={0} | all-to-all | bytes 524288 | tf_op jit(solution)/shard_map/all_to_all | solution.py:255
  80.5 9.8 %all_to_all.32.own_ref = f32[8,32,256]{2,1,0:T(8,128)S(1)} all-to-all(f32[8,32,256]{2,1,0:T(8,128)S(1)} %shard_map.81), channel_id=1, replica_groups={{0,2,4,6},{1,3,5,7},{8,10,12,14},{9,11,13,15},{16,18,20,22},{17,19,21,2..., dimensions={0} | all-to-all | bytes 524288 | tf_op jit(solution)/shard_map/all_to_all | solution.py:255
  90.3 1.9 %collective-permute-start.4 = (f32[8,32,256]{2,1,0:T(8,128)S(1)}, f32[8,32,256]{2,1,0:T(8,128)S(1)}, u32[]{:S(2)}, u32[]{:S(2)}) collective-permute-start(f32[8,32,256]{2,1,0:T(8,128)S(1)} %all_to_all.32.own_ref), channel_id=1, source_target_pairs={{0,1},{1,0},{2,3},{3,2},{4,5},{5,4},{6,7},{7,6},{8,9},{9,8},{10,11... | collective-permute-start | bytes 786440 | tf_op jit(solution)/shard_map/ppermute | solution.py:267
  92.3 1.5 %collective-permute-done.4.other_ref = f32[8,32,256]{2,1,0:T(8,128)S(1)} collective-permute-done((f32[8,32,256]{2,1,0:T(8,128)S(1)}, f32[8,32,256]{2,1,0:T(8,128)S(1)}, u32[]{:S(2)}, u32[]{:S(2)}) %collective-permute-start.4) | collective-permute-done | bytes 262176 | tf_op jit(solution)/shard_map/ppermute | solution.py:267
  93.8 2.2 %shard_map.82 = (f32[2,32,256]{2,1,0:T(8,128)}, f32[16,32,256]{2,1,0:T(8,128)S(1)}) custom-call(s32[37]{0:T(128)S(1)} %shard_map.78.table_ref, f32[8,32,256]{2,1,0:T(8,128)S(1)} %all_to_all.32.own_ref, f32[8,32,256]{2,1,0:T(8,128)S(1)} %collective-permute-done.4.other_ref, f32[4,256,256]{2,1,0:T(8,128)S(1)} %pad_maximum_fusion.factor_ref, ...), custom_call_target="tpu_custom_call" | custom-call | tf_op jit(solution)/shard_map/pallas_call | solution.py:38
  96.0 15.7 %all_to_all.33.got_ref = f32[16,32,256]{2,1,0:T(8,128)S(1)} all-to-all(f32[16,32,256]{2,1,0:T(8,128)S(1)} %get-tuple-element.11), channel_id=1, replica_groups={{0,8,16,24,32,40,48,56},{64,72,80,88,96,104,112,120},{128,136,144,152,1..., dimensions={0} | all-to-all | bytes 1048576 | tf_op jit(solution)/shard_map/all_to_all | solution.py:255
  112.3 12.9 %all_to_all.34 = f32[8,32,256]{2,1,0:T(8,128)S(1)} all-to-all(f32[8,32,256]{2,1,0:T(8,128)S(1)} %shard_map.83), channel_id=1, replica_groups={{0,64,128,192,256,320,384,448},{8,72,136,200,264,328,392,456},{16,80,14..., dimensions={0} | all-to-all | bytes 524288 | tf_op jit(solution)/shard_map/all_to_all | solution.py:255
  125.1 0.6 constant_dynamic-slice_fusion
  (15 shorter events, 1.2 us)
Async XLA Ops:
  4.3 7.3 %copy-start.2 = (f32[1,2,32,256]{3,2,1,0:T(8,128)S(1)}, f32[1,2,32,256]{3,2,1,0:T(8,128)}, u32[]{:S(2)}) copy-start(f32[1,2,32,256]{3,2,1,0:T(8,128)} %param.7) | copy-start | bytes 196612
  4.3 16.9 %copy-start.1 = (s32[64]{0:T(128)S(1)}, s32[64]{0:T(128)}, u32[]{:S(2)}) copy-start(s32[64]{0:T(128)} %owner_ref.3) | copy-start | bytes 772
  4.3 37.5 %all-to-all-start = ((f32[64,32,256]{2,1,0:T(8,128)}), f32[64,32,256]{2,1,0:T(8,128)S(1)}, u32[]{:S(2)}, u32[]{:S(2)}) async-start(f32[64,32,256]{2,1,0:T(8,128)} %shard_map.77), calls=%async_computation | async-start | bytes 4194304 | tf_op jit(solution)/shard_map/all_to_all | solution.py:255
  11.5 5.5 %collective-permute-start = (f32[2,32,256]{2,1,0:T(8,128)S(1)}, f32[2,32,256]{2,1,0:T(8,128)S(1)}, u32[]{:S(2)}, u32[]{:S(2)}) collective-permute-start(f32[2,32,256]{2,1,0:T(8,128)S(1)} %bitcast.10), channel_id=1, source_target_pairs={{0,1},{1,0},{2,3},{3,2},{4,5},{5,4},{6,7},{7,6},{8,9},{9,8},{10,11... | collective-permute-start | bytes 196616 | tf_op jit(solution)/shard_map/ppermute | solution.py:246
  17.1 14.7 %collective-permute-start.1 = (f32[2,64,256]{2,1,0:T(8,128)S(1)}, f32[2,64,256]{2,1,0:T(8,128)S(1)}, u32[]{:S(2)}, u32[]{:S(2)}) collective-permute-start(f32[2,64,256]{2,1,0:T(8,128)S(1)} %pad_maximum_fusion.1), channel_id=1, source_target_pairs={{0,2},{2,4},{4,6},{6,0},{1,3},{3,5},{5,7},{7,1},{8,10},{10,12},{12... | collective-permute-start | bytes 393224 | tf_op jit(solution)/shard_map/ppermute | solution.py:249
  24.6 9.8 %collective-permute-start.2 = (f32[2,64,256]{2,1,0:T(8,128)S(1)}, f32[2,64,256]{2,1,0:T(8,128)S(1)}, u32[]{:S(2)}, u32[]{:S(2)}) collective-permute-start(f32[2,64,256]{2,1,0:T(8,128)S(1)} %pad_maximum_fusion.1), channel_id=1, source_target_pairs={{0,4},{2,6},{4,0},{6,2},{1,5},{3,7},{5,1},{7,3},{8,12},{10,14},{12... | collective-permute-start | bytes 393224 | tf_op jit(solution)/shard_map/ppermute | solution.py:249
  27.6 8.7 %collective-permute-start.3 = (f32[2,64,256]{2,1,0:T(8,128)S(1)}, f32[2,64,256]{2,1,0:T(8,128)S(1)}, u32[]{:S(2)}, u32[]{:S(2)}) collective-permute-start(f32[2,64,256]{2,1,0:T(8,128)S(1)} %pad_maximum_fusion.1), channel_id=1, source_target_pairs={{0,6},{2,0},{4,2},{6,4},{1,7},{3,1},{5,3},{7,5},{8,14},{10,8},{12,... | collective-permute-start | bytes 393224 | tf_op jit(solution)/shard_map/ppermute | solution.py:249
  42.8 50.9 %copy-start = (f32[1,2,32,256]{3,2,1,0:T(8,128)S(1)}, f32[1,2,32,256]{3,2,1,0:T(8,128)}, u32[]{:S(2)}) copy-start(f32[1,2,32,256]{3,2,1,0:T(8,128)} %param.9) | copy-start | bytes 196612
  90.3 3.4 %collective-permute-start.4 = (f32[8,32,256]{2,1,0:T(8,128)S(1)}, f32[8,32,256]{2,1,0:T(8,128)S(1)}, u32[]{:S(2)}, u32[]{:S(2)}) collective-permute-start(f32[8,32,256]{2,1,0:T(8,128)S(1)} %all_to_all.32.own_ref), channel_id=1, source_target_pairs={{0,1},{1,0},{2,3},{3,2},{4,5},{5,4},{6,7},{7,6},{8,9},{9,8},{10,11... | collective-permute-start | bytes 786440 | tf_op jit(solution)/shard_map/ppermute | solution.py:267

commit v7 on v6

--- a/solution.py
+++ b/solution.py
@@ -31,7 +31,7 @@
 
 
 ANY = pl.BlockSpec(memory_space=pl.ANY)
-TWO, THREE, OWN, BACK, SOURCE, COUNT, CORE, TABLE = 0, 16, 24, 26, 34, 35, 36, 37
+TWO, THREE, OWN, BACK, COUNT, ROWS, SOURCE, TABLE = 0, 16, 24, 26, 34, 35, 36, 37
 
 
 def local_call(body, outs, ins, args, out_specs=None, scratch=(), limit=24):
@@ -68,33 +68,47 @@
 def deal(parts, block_owner, side):
     nb = parts.shape[0]
 
-    def body(owner_ref, parts_ref, out_ref, held_ref, slot_ref, start_ref, in_sem, out_sem):
-        fetch = pltpu.make_async_copy(parts_ref, held_ref, in_sem)
-        fetch.start()
+    group = nb // side
+
+    def body(owner_any_ref, parts_ref, out_ref, held_ref, owner_ref, to_ref, start_ref, in_sems, owner_sem, out_sem):
+        fetches = []
+        for i in range(side):
+            part = pl.ds(i * group, group)
+            fetches.append(pltpu.make_async_copy(parts_ref.at[part], held_ref.at[part], in_sems.at[i]))
+            fetches[i].start()
+        owners = pltpu.make_async_copy(owner_any_ref, owner_ref, owner_sem)
+        owners.start()
+        owners.wait()
         flip = lax.axis_index("c") == 1
-        sort_blocks(flip, owner_ref, slot_ref, start_ref, side)
-        fetch.wait()
+        sort_blocks(flip, owner_ref, to_ref, start_ref, side)
         for b in range(nb):
-            rank = start_ref[key_of(owner_ref[b], flip, side)] + slot_ref[b]
-            to = (rank & (side - 1)) * (nb // side) + rank // side
-            pltpu.make_async_copy(held_ref.at[b], out_ref.at[to], out_sem).start()
+            rank = start_ref[key_of(owner_ref[b], flip, side)] + to_ref[b]
+            to_ref[b] = (rank & (side - 1)) * group + rank // side
+        for i in range(side):
+            fetches[i].wait()
+            for b in range(i * group, (i + 1) * group):
+                pltpu.make_async_copy(held_ref.at[b], out_ref.at[to_ref[b]], out_sem).start()
         pltpu.make_async_copy(held_ref, out_ref, out_sem).wait()
 
     scratch = [
         pltpu.VMEM(parts.shape, parts.dtype),
         pltpu.SMEM((nb,), jnp.int32),
+        pltpu.SMEM((nb,), jnp.int32),
         pltpu.SMEM((side * side,), jnp.int32),
+        pltpu.SemaphoreType.DMA((side,)),
         pltpu.SemaphoreType.DMA(()),
         pltpu.SemaphoreType.DMA(()),
     ]
     out = jax.ShapeDtypeStruct(parts.shape, parts.dtype)
-    return local_call(body, out, [SMEM, ANY], (block_owner, parts), ANY, scratch, 60)
-
-
-def tables(block_owner, owner_counts, side, slots):
+    return local_call(body, out, [ANY, ANY], (block_owner, parts), ANY, scratch, 60)
+
+
+def tables(block_owner, owner_counts, rights, side, slots):
     nb = block_owner.shape[0]
 
-    def body(owner_ref, count_ref, out_ref, slot_ref, start_ref, key_at_ref):
+    def body(owner_ref, count_ref, right_ref, out_ref, staged_ref, slot_ref, start_ref, key_at_ref, sem):
+        fetch = pltpu.make_async_copy(right_ref, staged_ref, sem)
+        fetch.start()
         z, y, core = lax.axis_index("z"), lax.axis_index("y"), lax.axis_index("c")
         flip = core == 1
         u, w = jnp.where(flip, z, y), jnp.where(flip, y, z)
@@ -120,11 +134,22 @@
             out_ref[BACK + i] = (key & (side - 1)) * slots + slot_ref[b]
         out_ref[SOURCE] = key_of(owner_ref[z * side + y], flip, side) // side
         out_ref[COUNT] = count_ref[0]
-        out_ref[CORE] = core
-
-    scratch = [pltpu.SMEM((nb,), jnp.int32), pltpu.SMEM((side * side,), jnp.int32), pltpu.SMEM((nb,), jnp.int32)]
-    out = jax.ShapeDtypeStruct((TABLE,), jnp.int32)
-    return local_call(body, out, [SMEM, SMEM], (block_owner, owner_counts), SMEM, scratch)
+        out_ref[ROWS] = lax.axis_index("x") * 2 + core
+        fetch.wait()
+
+    scratch = [
+        pltpu.SMEM((nb,), jnp.int32),
+        pltpu.SMEM((side * side,), jnp.int32),
+        pltpu.SMEM((nb,), jnp.int32),
+        pltpu.SemaphoreType.DMA(()),
+    ]
+    outs = (
+        jax.ShapeDtypeStruct((TABLE,), jnp.int32),
+        jax.ShapeDtypeStruct(rights.shape, rights.dtype),
+    )
+    return local_call(
+        body, outs, [SMEM, SMEM, ANY], (block_owner, owner_counts, rights), (SMEM, VMEM), scratch
+    )
 
 
 def sum_and_pick(got, table, base, count, sources):
@@ -194,25 +219,22 @@
     return dot(ah, bh) + (dot(ah, bl) + dot(al, bh))
 
 
-def step(own, other, factors, moment, table, times):
+def step(whole, lefts, rights, moment, table, times):
     slots, rows, order = moment.shape
-    chips = own.shape[0] // slots
-
-    def body(table_ref, own_ref, other_ref, factor_ref, moment_ref, moment_out_ref, send_ref, whole_ref):
-        held, core = table_ref[COUNT], table_ref[CORE]
+
+    def body(table_ref, whole_ref, left_ref, right_ref, moment_ref, moment_out_ref, send_ref, pre_ref):
+        held = table_ref[COUNT]
+        mine = pl.ds(pl.multiple_of(table_ref[ROWS] * rows, rows), rows)
         for s in range(slots):
-            for x in range(chips):
-                whole_ref[s, 2 * x + core] = own_ref[x * slots + s]
-                whole_ref[s, 2 * x + 1 - core] = other_ref[x * slots + s]
-        for s in range(slots):
-            whole = whole_ref[s].reshape(order, order)
-            right_part = product(whole, factor_ref[slots + s])
-            precond = product(factor_ref[s], right_part)
+            gradient = whole_ref[s]
+            right_part = product(gradient, right_ref[s])
+            precond = product(left_ref[s], right_part)
+            pre_ref[s] = precond
             entries = order * order
-            grad_mean = jnp.sum(whole * whole, keepdims=True) / entries
+            grad_mean = jnp.sum(gradient * gradient, keepdims=True) / entries
             pre_mean = jnp.sum(precond * precond, keepdims=True) / entries
             graft = jnp.sqrt(grad_mean) / jnp.sqrt(pre_mean + EPS)
-            direction = graft * precond[:rows]
+            direction = graft * pre_ref[s, mine]
             before = moment_ref[s]
             fresh = BETA * before + direction
             update = BETA * fresh + direction
@@ -224,9 +246,9 @@
         jax.ShapeDtypeStruct(moment.shape, moment.dtype),
         jax.ShapeDtypeStruct((times * slots, rows, order), moment.dtype),
     )
-    scratch = [pltpu.VMEM((slots, order // rows, rows, order), moment.dtype)]
+    scratch = [pltpu.VMEM((slots, order, order), moment.dtype)]
     return local_call(
-        body, outs, [SMEM, VMEM, VMEM, VMEM, VMEM], (table, own, other, factors, moment), None, scratch
+        body, outs, [SMEM, VMEM, VMEM, VMEM, VMEM], (table, whole, lefts, rights, moment), None, scratch
     )
 
 
@@ -235,37 +257,22 @@
     first_lines = lines(sizes, ("y", "z"))
     second_lines = lines(sizes, ("z", "y"))
 
-    chip_lines = [
-        [device(z, y, x, c, sizes) for x in range(sizes[2])]
-        for z in range(sizes[0])
-        for y in range(sizes[1])
-        for c in range(sizes[3])
-    ]
-
-    def gather_any_order(rows):
-        other = lax.ppermute(rows, "c", [(0, 1), (1, 0)])
-        chip = jnp.concatenate([rows, other], axis=1)
-        away = [
-            lax.ppermute(chip, "x", [(i, (i + k) % sizes[2]) for i in range(sizes[2])])
-            for k in range(1, sizes[2])
-        ]
-        return jnp.concatenate([chip, *away], axis=1)
-
     def exchange(blocks, groups):
         return lax.all_to_all(blocks, AXES, 0, 0, tiled=True, axis_index_groups=groups)
 
     def on_device(grads, left_root, right_root, momentum, block_owner, owner_counts):
         slots = left_root.shape[1]
         got = exchange(deal(grads[0], block_owner, side), first_lines)
-        table = tables(block_owner, owner_counts, side, slots)
-        factors = jnp.concatenate([gather_any_order(left_root[0]), right_root[0]], axis=0)
+        table, rights = tables(block_owner, owner_counts, right_root[0], side, slots)
         source = table[SOURCE].astype(jnp.uint32)
-        got, factors, table, source = lax.optimization_barrier((got, factors, table, source))
+        lefts = lax.all_gather(left_root[0], ("x", "c"), axis=1, tiled=True)
+        early = (lefts, rights, table, source)
+        got, (lefts, rights, table, source) = lax.optimization_barrier((got, early))
         got = exchange(sum_and_pick(got, table, TWO, side * slots, side), second_lines)
         got = exchange(sum_and_pick_here(got, table, THREE, side, side), first_lines)
-        own = exchange(pick_and_repeat(got, table, OWN, slots, sizes[2]), chip_lines)
-        other = lax.ppermute(own, "c", [(0, 1), (1, 0)])
-        new_moment, send = step(own, other, factors, momentum[0], table, side)
+        gradient = pick_and_repeat(got, table, OWN, slots, 1)
+        whole = lax.all_gather(gradient, ("x", "c"), axis=1, tiled=True)
+        new_moment, send = step(whole, lefts, rights, momentum[0], table, side)
         got = exchange(send, first_lines)
         got = exchange(pick_and_repeat(got, table, BACK, side, 1), second_lines)
         zero = jnp.uint32(0)

time: 126 us -> 126 us (level)
  blocking collectives: 74.8 us -> 92 us
  starting transfers between devices: 24.3 us -> 7.24 us
    all_gather x0 -> x2, blocking collectives: none -> 27 us  [the longest x1 13.9 us: on_device(): lefts = lax.all_gather(left_root[0], ('x', 'c'), axis=1, tiled=True)]
    ppermute x5 -> x0, starting transfers between devices: 17 us -> none  [the longest x3 10.5 us: gather_any_order(): lax.ppermute(chip, 'x', [(i, (i + k) % sizes[2]) for i in range(sizes[2])])]
    all_to_all x5 -> x4, blocking collectives: 74.8 us -> 65 us  [exchange(): lax.all_to_all(blocks, AXES, 0, 0, tiled=True, axis_index_groups=groups)]
    all_to_all x1, waiting for transfers between devices: 4.35 us -> 12.2 us  [exchange(): lax.all_to_all(blocks, AXES, 0, 0, tiled=True, axis_index_groups=groups)]
    ppermute x5 -> x0, waiting for transfers between devices: 6.91 us -> none  [the longest x3 4.53 us: gather_any_order(): lax.ppermute(chip, 'x', [(i, (i + k) % sizes[2]) for i in range(sizes[2])])]
  transfers between devices with their start and end apart: 6 -> 1, of which waited for: 5 -> 1; matrix products, arithmetic and copies ran while one was open for 1% -> 0% of each run, Pallas kernels for 2% -> 2%
where the time goes in v7:
time: 126 us
  blocking collectives  92 us (73%)
  waiting for transfers between devices  12.2 us (10%)
  Pallas kernels  11 us (9%)
  starting transfers between devices  7.24 us (6%)
  between operations  2.04 us (2%)
    all_to_all x4, blocking collectives, exchange(): lax.all_to_all(blocks, AXES, 0, 0, tiled=True, axis_index_groups=groups)  65 us
    all_gather x1, blocking collectives, on_device(): lefts = lax.all_gather(left_root[0], ('x', 'c'), axis=1, tiled=True)  13.9 us
    all_gather x1, blocking collectives, on_device(): whole = lax.all_gather(gradient, ('x', 'c'), axis=1, tiled=True)  13.2 us
    all_to_all x1, waiting for transfers between devices, exchange(): lax.all_to_all(blocks, AXES, 0, 0, tiled=True, axis_index_groups=groups)  12.2 us
    pallas_call x7, Pallas kernels, local_call(): pl.pallas_call(body, out_shape=outs, in_specs=ins, out_specs=jax.tree.map...  11 us
    all_to_all x1, starting transfers between devices, exchange(): lax.all_to_all(blocks, AXES, 0, 0, tiled=True, axis_index_groups=groups)  7.24 us
  transfers between devices with their start and end apart: 1, of which 1 were waited for; matrix products, arithmetic and copies ran while one was open for 0% of the time, Pallas kernels for 2%

profile of v7, /device:TPU:2, one launch (start us, length us, event | category | flops | bytes accessed | tf_op | source)
XLA Modules:
  0.0 125.7 jit_solution(9304623637984946061)
XLA Ops:
  0.6 3.7 %shard_map.77 = f32[64,32,256]{2,1,0:T(8,128)} custom-call(s32[64]{0:T(128)} %owner_ref.1, f32[64,32,256]{2,1,0:T(8,128)} %bitcast.9), custom_call_target="tpu_custom_call" | custom-call | tf_op jit(solution)/shard_map/pallas_call | solution.py:38
  4.3 0.0 copy-start
  4.3 0.0 copy-start.2
  4.4 0.0 copy-start.3
  4.4 7.2 %all-to-all-start = ((f32[64,32,256]{2,1,0:T(8,128)}), f32[64,32,256]{2,1,0:T(8,128)S(1)}, u32[]{:S(2)}, u32[]{:S(2)}) async-start(f32[64,32,256]{2,1,0:T(8,128)} %shard_map.77), calls=%async_computation | async-start | bytes 4194304 | tf_op jit(solution)/shard_map/all_to_all | solution.py:261
  12.3 0.0 copy-done
  12.3 0.0 copy-done.2
  12.3 2.3 %shard_map.78 = (s32[37]{0:T(128)S(1)}, f32[2,256,256]{2,1,0:T(8,128)S(1)}) custom-call(s32[64]{0:T(128)S(1)} %copy-done.2, s32[1]{0:T(128)S(6)} %copy.8.count_ref, f32[2,256,256]{2,1,0:T(8,128)S(1)} %bitcast.7), custom_call_target="tpu_custom_call" | custom-call | tf_op jit(solution)/shard_map/pallas_call | solution.py:38
  14.6 0.6 slice.3
  15.8 13.9 %all-gather = f32[1,2,256,256]{3,2,1,0:T(8,128)S(1)} all-gather(f32[1,2,32,256]{3,2,1,0:T(8,128)S(1)} %copy-done.3), channel_id=2, replica_groups=mesh['z'=8,'y'=8,'x'=4,'c'=2] {'x','c'}, dimensions={2}, use_global_device_ids=true | all-gather | bytes 589824 | tf_op jit(solution)/shard_map/all_gather | solution.py:268
  29.7 12.2 %all-to-all-done.got_ref = f32[64,32,256]{2,1,0:T(8,128)S(1)} async-done(((f32[64,32,256]{2,1,0:T(8,128)}), f32[64,32,256]{2,1,0:T(8,128)S(1)}, u32[]{:S(2)}, u32[]{:S(2)}) %all-to-all-start) | async-done | bytes 2097184 | tf_op jit(solution)/shard_map/all_to_all | solution.py:261
  41.9 1.0 shard_map.79
  42.9 0.0 copy-start.1
  42.9 23.5 %all_to_all.25.got_ref = f32[16,32,256]{2,1,0:T(8,128)S(1)} all-to-all(f32[16,32,256]{2,1,0:T(8,128)S(1)} %shard_map.79), channel_id=1, replica_groups={{0,64,128,192,256,320,384,448},{8,72,136,200,264,328,392,456},{16,80,14..., dimensions={0} | all-to-all | bytes 1048576 | tf_op jit(solution)/shard_map/all_to_all | solution.py:261
  66.5 0.6 shard_map.80
  67.1 12.9 %all_to_all.26.got_ref = f32[8,32,256]{2,1,0:T(8,128)S(1)} all-to-all(f32[8,32,256]{2,1,0:T(8,128)S(1)} %shard_map.80), channel_id=1, replica_groups={{0,8,16,24,32,40,48,56},{64,72,80,88,96,104,112,120},{128,136,144,152,1..., dimensions={0} | all-to-all | bytes 524288 | tf_op jit(solution)/shard_map/all_to_all | solution.py:261
  80.0 0.5 shard_map.81
  80.6 13.2 %all_gather.7.whole_ref = f32[2,256,256]{2,1,0:T(8,128)S(1)} all-gather(f32[2,32,256]{2,1,0:T(8,128)S(1)} %shard_map.81), channel_id=1, replica_groups=mesh['z'=8,'y'=8,'x'=4,'c'=2] {'x','c'}, dimensions={1}, use_global_device_ids=true | all-gather | bytes 589824 | tf_op jit(solution)/shard_map/all_gather | solution.py:274
  93.7 0.0 copy-done.1
  93.7 2.2 %shard_map.82 = (f32[2,32,256]{2,1,0:T(8,128)}, f32[16,32,256]{2,1,0:T(8,128)S(1)}) custom-call(s32[37]{0:T(128)S(1)} %get-tuple-element.13.table_ref, f32[2,256,256]{2,1,0:T(8,128)S(1)} %all_gather.7.whole_ref, f32[2,256,256]{2,1,0:T(8,128)S(1)} %bitcast.6, f32[2,256,256]{2,1,0:T(8,128)S(1)} %get-tuple-element.16.right_ref, f32[2,32,256]{2,1,0:T(8,128)S(1)} %bitcast.8), custom_call_target="tpu_custom_call" | custom-call | tf_op jit(solution)/shard_map/pallas_call | solution.py:38
  96.0 15.7 %all_to_all.27.got_ref = f32[16,32,256]{2,1,0:T(8,128)S(1)} all-to-all(f32[16,32,256]{2,1,0:T(8,128)S(1)} %get-tuple-element.17), channel_id=1, replica_groups={{0,8,16,24,32,40,48,56},{64,72,80,88,96,104,112,120},{128,136,144,152,1..., dimensions={0} | all-to-all | bytes 1048576 | tf_op jit(solution)/shard_map/all_to_all | solution.py:261
  111.6 0.6 shard_map.83
  112.2 12.9 %all_to_all.28 = f32[8,32,256]{2,1,0:T(8,128)S(1)} all-to-all(f32[8,32,256]{2,1,0:T(8,128)S(1)} %shard_map.83), channel_id=1, replica_groups={{0,64,128,192,256,320,384,448},{8,72,136,200,264,328,392,456},{16,80,14..., dimensions={0} | all-to-all | bytes 524288 | tf_op jit(solution)/shard_map/all_to_all | solution.py:261
  125.1 0.6 constant_dynamic-slice_fusion
  (1 shorter events, 0.0 us)
Async XLA Ops:
  4.3 7.9 %copy-start = (f32[1,2,256,256]{3,2,1,0:T(8,128)S(1)}, f32[1,2,256,256]{3,2,1,0:T(8,128)}, u32[]{:S(2)}) copy-start(f32[1,2,256,256]{3,2,1,0:T(8,128)} %param.8) | copy-start | bytes 1572868
  4.3 7.9 %copy-start.2 = (s32[64]{0:T(128)S(1)}, s32[64]{0:T(128)}, u32[]{:S(2)}) copy-start(s32[64]{0:T(128)} %owner_ref.1) | copy-start | bytes 772
  4.4 11.4 %copy-start.3 = (f32[1,2,32,256]{3,2,1,0:T(8,128)S(1)}, f32[1,2,32,256]{3,2,1,0:T(8,128)}, u32[]{:S(2)}) copy-start(f32[1,2,32,256]{3,2,1,0:T(8,128)} %param.7) | copy-start | bytes 196612
  4.4 37.5 %all-to-all-start = ((f32[64,32,256]{2,1,0:T(8,128)}), f32[64,32,256]{2,1,0:T(8,128)S(1)}, u32[]{:S(2)}, u32[]{:S(2)}) async-start(f32[64,32,256]{2,1,0:T(8,128)} %shard_map.77), calls=%async_computation | async-start | bytes 4194304 | tf_op jit(solution)/shard_map/all_to_all | solution.py:261
  42.9 50.8 %copy-start.1 = (f32[1,2,32,256]{3,2,1,0:T(8,128)S(1)}, f32[1,2,32,256]{3,2,1,0:T(8,128)}, u32[]{:S(2)}) copy-start(f32[1,2,32,256]{3,2,1,0:T(8,128)} %param.9) | copy-start | bytes 196612

commit v8 on v7

--- a/solution.py
+++ b/solution.py
@@ -205,18 +205,8 @@
     return local_call(body, out, [SMEM, VMEM], (table, got))
 
 
-def halves(a):
-    high = a.astype(jnp.bfloat16)
-    return high, (a - high.astype(jnp.float32)).astype(jnp.bfloat16)
-
-
 def product(a, b):
-    (ah, al), (bh, bl) = halves(a), halves(b)
-
-    def dot(p, q):
-        return jnp.dot(p, q, preferred_element_type=jnp.float32)
-
-    return dot(ah, bh) + (dot(ah, bl) + dot(al, bh))
+    return jnp.dot(a, b, precision=lax.Precision.HIGHEST, preferred_element_type=jnp.float32)
 
 
 def step(whole, lefts, rights, moment, table, times):

time: 126 us -> 127 us (level)
  no operation moved by 1% of the time
where the time goes in v8:
time: 127 us; the launch traced here: 126 us
  blocking collectives  92 us (72%)
  waiting for transfers between devices  12.2 us (10%)
  Pallas kernels  11.6 us (9%)
  starting transfers between devices  7.24 us (6%)
  between operations  2.04 us (2%)
    all_to_all x4, blocking collectives, exchange(): lax.all_to_all(blocks, AXES, 0, 0, tiled=True, axis_index_groups=groups)  65 us
    all_gather x1, blocking collectives, on_device(): lefts = lax.all_gather(left_root[0], ('x', 'c'), axis=1, tiled=True)  13.9 us
    all_gather x1, blocking collectives, on_device(): whole = lax.all_gather(gradient, ('x', 'c'), axis=1, tiled=True)  13.2 us
    all_to_all x1, waiting for transfers between devices, exchange(): lax.all_to_all(blocks, AXES, 0, 0, tiled=True, axis_index_groups=groups)  12.2 us
    pallas_call x7, Pallas kernels, local_call(): pl.pallas_call(body, out_shape=outs, in_specs=ins, out_specs=jax.tree.map...  11.6 us
    all_to_all x1, starting transfers between devices, exchange(): lax.all_to_all(blocks, AXES, 0, 0, tiled=True, axis_index_groups=groups)  7.24 us
  transfers between devices with their start and end apart: 1, of which 1 were waited for; matrix products, arithmetic and copies ran while one was open for 0% of the time, Pallas kernels for 2%

profile of v8, /device:TPU:2, one launch (start us, length us, event | category | flops | bytes accessed | tf_op | source)
XLA Modules:
  0.0 126.3 jit_solution(11412922088540992981)
XLA Ops:
  0.6 3.7 %shard_map.77 = f32[64,32,256]{2,1,0:T(8,128)} custom-call(s32[64]{0:T(128)} %owner_ref.1, f32[64,32,256]{2,1,0:T(8,128)} %bitcast.9), custom_call_target="tpu_custom_call" | custom-call | tf_op jit(solution)/shard_map/pallas_call | solution.py:38
  4.3 0.0 copy-start
  4.3 0.0 copy-start.2
  4.3 0.0 copy-start.3
  4.4 7.2 %all-to-all-start = ((f32[64,32,256]{2,1,0:T(8,128)}), f32[64,32,256]{2,1,0:T(8,128)S(1)}, u32[]{:S(2)}, u32[]{:S(2)}) async-start(f32[64,32,256]{2,1,0:T(8,128)} %shard_map.77), calls=%async_computation | async-start | bytes 4194304 | tf_op jit(solution)/shard_map/all_to_all | solution.py:251
  12.3 0.0 copy-done
  12.3 0.0 copy-done.2
  12.3 2.3 %shard_map.78 = (s32[37]{0:T(128)S(1)}, f32[2,256,256]{2,1,0:T(8,128)S(1)}) custom-call(s32[64]{0:T(128)S(1)} %copy-done.2, s32[1]{0:T(128)S(6)} %copy.8.count_ref, f32[2,256,256]{2,1,0:T(8,128)S(1)} %bitcast.7), custom_call_target="tpu_custom_call" | custom-call | tf_op jit(solution)/shard_map/pallas_call | solution.py:38
  14.6 0.6 slice.3
  15.8 13.9 %all-gather = f32[1,2,256,256]{3,2,1,0:T(8,128)S(1)} all-gather(f32[1,2,32,256]{3,2,1,0:T(8,128)S(1)} %copy-done.3), channel_id=2, replica_groups=mesh['z'=8,'y'=8,'x'=4,'c'=2] {'x','c'}, dimensions={2}, use_global_device_ids=true | all-gather | bytes 589824 | tf_op jit(solution)/shard_map/all_gather | solution.py:258
  29.7 12.2 %all-to-all-done.got_ref = f32[64,32,256]{2,1,0:T(8,128)S(1)} async-done(((f32[64,32,256]{2,1,0:T(8,128)}), f32[64,32,256]{2,1,0:T(8,128)S(1)}, u32[]{:S(2)}, u32[]{:S(2)}) %all-to-all-start) | async-done | bytes 2097184 | tf_op jit(solution)/shard_map/all_to_all | solution.py:251
  41.9 1.0 shard_map.79
  42.9 0.0 copy-start.1
  42.9 23.5 %all_to_all.25.got_ref = f32[16,32,256]{2,1,0:T(8,128)S(1)} all-to-all(f32[16,32,256]{2,1,0:T(8,128)S(1)} %shard_map.79), channel_id=1, replica_groups={{0,64,128,192,256,320,384,448},{8,72,136,200,264,328,392,456},{16,80,14..., dimensions={0} | all-to-all | bytes 1048576 | tf_op jit(solution)/shard_map/all_to_all | solution.py:251
  66.5 0.6 shard_map.80
  67.1 12.9 %all_to_all.26.got_ref = f32[8,32,256]{2,1,0:T(8,128)S(1)} all-to-all(f32[8,32,256]{2,1,0:T(8,128)S(1)} %shard_map.80), channel_id=1, replica_groups={{0,8,16,24,32,40,48,56},{64,72,80,88,96,104,112,120},{128,136,144,152,1..., dimensions={0} | all-to-all | bytes 524288 | tf_op jit(solution)/shard_map/all_to_all | solution.py:251
  80.0 0.5 shard_map.81
  80.5 13.2 %all_gather.7.whole_ref = f32[2,256,256]{2,1,0:T(8,128)S(1)} all-gather(f32[2,32,256]{2,1,0:T(8,128)S(1)} %shard_map.81), channel_id=1, replica_groups=mesh['z'=8,'y'=8,'x'=4,'c'=2] {'x','c'}, dimensions={1}, use_global_device_ids=true | all-gather | bytes 589824 | tf_op jit(solution)/shard_map/all_gather | solution.py:264
  93.7 0.0 copy-done.1
  93.7 2.9 %shard_map.82 = (f32[2,32,256]{2,1,0:T(8,128)}, f32[16,32,256]{2,1,0:T(8,128)S(1)}) custom-call(s32[37]{0:T(128)S(1)} %get-tuple-element.13.table_ref, f32[2,256,256]{2,1,0:T(8,128)S(1)} %all_gather.7.whole_ref, f32[2,256,256]{2,1,0:T(8,128)S(1)} %bitcast.6, f32[2,256,256]{2,1,0:T(8,128)S(1)} %get-tuple-element.16.right_ref, f32[2,32,256]{2,1,0:T(8,128)S(1)} %bitcast.8), custom_call_target="tpu_custom_call" | custom-call | tf_op jit(solution)/shard_map/pallas_call | solution.py:38
  96.6 15.7 %all_to_all.27.got_ref = f32[16,32,256]{2,1,0:T(8,128)S(1)} all-to-all(f32[16,32,256]{2,1,0:T(8,128)S(1)} %get-tuple-element.17), channel_id=1, replica_groups={{0,8,16,24,32,40,48,56},{64,72,80,88,96,104,112,120},{128,136,144,152,1..., dimensions={0} | all-to-all | bytes 1048576 | tf_op jit(solution)/shard_map/all_to_all | solution.py:251
  112.3 0.6 shard_map.83
  112.8 12.9 %all_to_all.28 = f32[8,32,256]{2,1,0:T(8,128)S(1)} all-to-all(f32[8,32,256]{2,1,0:T(8,128)S(1)} %shard_map.83), channel_id=1, replica_groups={{0,64,128,192,256,320,384,448},{8,72,136,200,264,328,392,456},{16,80,14..., dimensions={0} | all-to-all | bytes 524288 | tf_op jit(solution)/shard_map/all_to_all | solution.py:251
  125.7 0.6 constant_dynamic-slice_fusion
  (1 shorter events, 0.0 us)
Async XLA Ops:
  4.3 7.9 %copy-start = (f32[1,2,256,256]{3,2,1,0:T(8,128)S(1)}, f32[1,2,256,256]{3,2,1,0:T(8,128)}, u32[]{:S(2)}) copy-start(f32[1,2,256,256]{3,2,1,0:T(8,128)} %param.8) | copy-start | bytes 1572868
  4.3 7.9 %copy-start.2 = (s32[64]{0:T(128)S(1)}, s32[64]{0:T(128)}, u32[]{:S(2)}) copy-start(s32[64]{0:T(128)} %owner_ref.1) | copy-start | bytes 772
  4.3 11.4 %copy-start.3 = (f32[1,2,32,256]{3,2,1,0:T(8,128)S(1)}, f32[1,2,32,256]{3,2,1,0:T(8,128)}, u32[]{:S(2)}) copy-start(f32[1,2,32,256]{3,2,1,0:T(8,128)} %param.7) | copy-start | bytes 196612
  4.4 37.5 %all-to-all-start = ((f32[64,32,256]{2,1,0:T(8,128)}), f32[64,32,256]{2,1,0:T(8,128)S(1)}, u32[]{:S(2)}, u32[]{:S(2)}) async-start(f32[64,32,256]{2,1,0:T(8,128)} %shard_map.77), calls=%async_computation | async-start | bytes 4194304 | tf_op jit(solution)/shard_map/all_to_all | solution.py:251
  42.9 50.8 %copy-start.1 = (f32[1,2,32,256]{3,2,1,0:T(8,128)S(1)}, f32[1,2,32,256]{3,2,1,0:T(8,128)}, u32[]{:S(2)}) copy-start(f32[1,2,32,256]{3,2,1,0:T(8,128)} %param.9) | copy-start | bytes 196612

commit v9 on v8

--- a/solution.py
+++ b/solution.py
@@ -46,18 +46,21 @@
 
 
 def key_of(owner, flip, side):
-    turned = (owner & (side - 1)) * side + owner // side
+    bits = side.bit_length() - 1
+    turned = ((owner & (side - 1)) << bits) | (owner >> bits)
     return jnp.where(flip, turned, owner)
 
 
-def sort_blocks(flip, owner_ref, slot_ref, start_ref, side):
+def sort_blocks(flip, owner_ref, key_ref, slot_ref, start_ref, side):
     nb = owner_ref.shape[0]
     for k in range(side * side):
         start_ref[k] = 0
     for b in range(nb):
         key = key_of(owner_ref[b], flip, side)
-        slot_ref[b] = start_ref[key]
-        start_ref[key] = slot_ref[b] + 1
+        slot = start_ref[key]
+        key_ref[b] = key
+        slot_ref[b] = slot
+        start_ref[key] = slot + 1
     total = jnp.int32(0)
     for k in range(side * side):
         held = start_ref[k]
@@ -70,7 +73,7 @@
 
     group = nb // side
 
-    def body(owner_any_ref, parts_ref, out_ref, held_ref, owner_ref, to_ref, start_ref, in_sems, owner_sem, out_sem):
+    def body(owner_any_ref, parts_ref, out_ref, held_ref, owner_ref, key_ref, to_ref, start_ref, in_sems, owner_sem, out_sem):
         fetches = []
         for i in range(side):
             part = pl.ds(i * group, group)
@@ -80,10 +83,11 @@
         owners.start()
         owners.wait()
         flip = lax.axis_index("c") == 1
-        sort_blocks(flip, owner_ref, to_ref, start_ref, side)
+        sort_blocks(flip, owner_ref, key_ref, to_ref, start_ref, side)
+        bits = side.bit_length() - 1
         for b in range(nb):
-            rank = start_ref[key_of(owner_ref[b], flip, side)] + to_ref[b]
-            to_ref[b] = (rank & (side - 1)) * group + rank // side
+            rank = start_ref[key_ref[b]] + to_ref[b]
+            to_ref[b] = (rank & (side - 1)) * group + (rank >> bits)
         for i in range(side):
             fetches[i].wait()
             for b in range(i * group, (i + 1) * group):
@@ -92,6 +96,7 @@
 
     scratch = [
         pltpu.VMEM(parts.shape, parts.dtype),
+        pltpu.SMEM((nb,), jnp.int32),
         pltpu.SMEM((nb,), jnp.int32),
         pltpu.SMEM((nb,), jnp.int32),
         pltpu.SMEM((side * side,), jnp.int32),
@@ -106,19 +111,19 @@
 def tables(block_owner, owner_counts, rights, side, slots):
     nb = block_owner.shape[0]
 
-    def body(owner_ref, count_ref, right_ref, out_ref, staged_ref, slot_ref, start_ref, key_at_ref, sem):
+    def body(owner_ref, count_ref, right_ref, out_ref, staged_ref, key_ref, slot_ref, start_ref, key_at_ref, sem):
         fetch = pltpu.make_async_copy(right_ref, staged_ref, sem)
         fetch.start()
         z, y, core = lax.axis_index("z"), lax.axis_index("y"), lax.axis_index("c")
         flip = core == 1
         u, w = jnp.where(flip, z, y), jnp.where(flip, y, z)
-        sort_blocks(flip, owner_ref, slot_ref, start_ref, side)
+        bits = side.bit_length() - 1
+        sort_blocks(flip, owner_ref, key_ref, slot_ref, start_ref, side)
         for b in range(nb):
-            key = key_of(owner_ref[b], flip, side)
-            key_at_ref[start_ref[key] + slot_ref[b]] = key
+            key_at_ref[start_ref[key_ref[b]] + slot_ref[b]] = key_ref[b]
 
         def first(line):
-            return jnp.maximum(start_ref[line * side] - u + side - 1, 0) // side
+            return jnp.maximum(start_ref[line * side] - u + side - 1, 0) >> bits
 
         for line in range(side):
             for s in range(slots):
@@ -130,14 +135,14 @@
             out_ref[OWN + s] = (start_ref[w * side + u] + s) & (side - 1)
         for i in range(side):
             b = jnp.where(flip, u * side + i, i * side + u)
-            key = key_of(owner_ref[b], flip, side)
-            out_ref[BACK + i] = (key & (side - 1)) * slots + slot_ref[b]
-        out_ref[SOURCE] = key_of(owner_ref[z * side + y], flip, side) // side
+            out_ref[BACK + i] = (key_ref[b] & (side - 1)) * slots + slot_ref[b]
+        out_ref[SOURCE] = key_ref[z * side + y] >> bits
         out_ref[COUNT] = count_ref[0]
         out_ref[ROWS] = lax.axis_index("x") * 2 + core
         fetch.wait()
 
     scratch = [
+        pltpu.SMEM((nb,), jnp.int32),
         pltpu.SMEM((nb,), jnp.int32),
         pltpu.SMEM((side * side,), jnp.int32),
         pltpu.SMEM((nb,), jnp.int32),

time: 127 us -> 126 us (level)
  Pallas kernels: 11.6 us -> 10.1 us
    pallas_call x7, Pallas kernels: 11.6 us -> 10.1 us  [local_call(): pl.pallas_call(body, out_shape=outs, in_specs=ins, out_specs=jax.tree.map...]
  transfers between devices with their start and end apart: 1 -> 1, of which waited for: 1 -> 1; matrix products, arithmetic and copies ran while one was open for 0% -> 0% of each run, Pallas kernels for 2% -> 1%
where the time goes in v9:
time: 126 us; the launch traced here: 125 us
  blocking collectives  92 us (73%)
  waiting for transfers between devices  12.8 us (10%)
  Pallas kernels  10.1 us (8%)
  starting transfers between devices  7.24 us (6%)
  between operations  2.04 us (2%)
    all_to_all x4, blocking collectives, exchange(): lax.all_to_all(blocks, AXES, 0, 0, tiled=True, axis_index_groups=groups)  65 us
    all_gather x1, blocking collectives, on_device(): lefts = lax.all_gather(left_root[0], ('x', 'c'), axis=1, tiled=True)  13.9 us
    all_gather x1, blocking collectives, on_device(): whole = lax.all_gather(gradient, ('x', 'c'), axis=1, tiled=True)  13.2 us
    all_to_all x1, waiting for transfers between devices, exchange(): lax.all_to_all(blocks, AXES, 0, 0, tiled=True, axis_index_groups=groups)  12.8 us
    pallas_call x7, Pallas kernels, local_call(): pl.pallas_call(body, out_shape=outs, in_specs=ins, out_specs=jax.tree.map...  10.1 us
    all_to_all x1, starting transfers between devices, exchange(): lax.all_to_all(blocks, AXES, 0, 0, tiled=True, axis_index_groups=groups)  7.24 us
  transfers between devices with their start and end apart: 1, of which 1 were waited for; matrix products, arithmetic and copies ran while one was open for 0% of the time, Pallas kernels for 1%

profile of v9, /device:TPU:2, one launch (start us, length us, event | category | flops | bytes accessed | tf_op | source)
XLA Modules:
  0.0 125.4 jit_solution(6399629142041808455)
XLA Ops:
  0.6 2.7 %shard_map.77 = f32[64,32,256]{2,1,0:T(8,128)} custom-call(s32[64]{0:T(128)} %owner_ref.1, f32[64,32,256]{2,1,0:T(8,128)} %bitcast.9), custom_call_target="tpu_custom_call" | custom-call | tf_op jit(solution)/shard_map/pallas_call | solution.py:38
  3.4 0.0 copy-start
  3.4 0.0 copy-start.2
  3.4 0.0 copy-start.3
  3.4 7.2 %all-to-all-start = ((f32[64,32,256]{2,1,0:T(8,128)}), f32[64,32,256]{2,1,0:T(8,128)S(1)}, u32[]{:S(2)}, u32[]{:S(2)}) async-start(f32[64,32,256]{2,1,0:T(8,128)} %shard_map.77), calls=%async_computation | async-start | bytes 4194304 | tf_op jit(solution)/shard_map/all_to_all | solution.py:256
  11.3 0.0 copy-done
  11.3 0.0 copy-done.2
  11.3 1.7 %shard_map.78 = (s32[37]{0:T(128)S(1)}, f32[2,256,256]{2,1,0:T(8,128)S(1)}) custom-call(s32[64]{0:T(128)S(1)} %copy-done.2, s32[1]{0:T(128)S(6)} %copy.8.count_ref, f32[2,256,256]{2,1,0:T(8,128)S(1)} %bitcast.7), custom_call_target="tpu_custom_call" | custom-call | tf_op jit(solution)/shard_map/pallas_call | solution.py:38
  13.1 0.6 slice.3
  14.3 0.0 copy-done.3
  14.3 13.9 %all-gather = f32[1,2,256,256]{3,2,1,0:T(8,128)S(1)} all-gather(f32[1,2,32,256]{3,2,1,0:T(8,128)S(1)} %copy-done.3), channel_id=2, replica_groups=mesh['z'=8,'y'=8,'x'=4,'c'=2] {'x','c'}, dimensions={2}, use_global_device_ids=true | all-gather | bytes 589824 | tf_op jit(solution)/shard_map/all_gather | solution.py:263
  28.2 12.8 %all-to-all-done.got_ref = f32[64,32,256]{2,1,0:T(8,128)S(1)} async-done(((f32[64,32,256]{2,1,0:T(8,128)}), f32[64,32,256]{2,1,0:T(8,128)S(1)}, u32[]{:S(2)}, u32[]{:S(2)}) %all-to-all-start) | async-done | bytes 2097184 | tf_op jit(solution)/shard_map/all_to_all | solution.py:256
  40.9 1.0 shard_map.79
  42.0 0.0 copy-start.1
  42.0 23.5 %all_to_all.25.got_ref = f32[16,32,256]{2,1,0:T(8,128)S(1)} all-to-all(f32[16,32,256]{2,1,0:T(8,128)S(1)} %shard_map.79), channel_id=1, replica_groups={{0,64,128,192,256,320,384,448},{8,72,136,200,264,328,392,456},{16,80,14..., dimensions={0} | all-to-all | bytes 1048576 | tf_op jit(solution)/shard_map/all_to_all | solution.py:256
  65.5 0.6 shard_map.80
  66.2 12.9 %all_to_all.26.got_ref = f32[8,32,256]{2,1,0:T(8,128)S(1)} all-to-all(f32[8,32,256]{2,1,0:T(8,128)S(1)} %shard_map.80), channel_id=1, replica_groups={{0,8,16,24,32,40,48,56},{64,72,80,88,96,104,112,120},{128,136,144,152,1..., dimensions={0} | all-to-all | bytes 524288 | tf_op jit(solution)/shard_map/all_to_all | solution.py:256
  79.0 0.5 shard_map.81
  79.6 13.2 %all_gather.7.whole_ref = f32[2,256,256]{2,1,0:T(8,128)S(1)} all-gather(f32[2,32,256]{2,1,0:T(8,128)S(1)} %shard_map.81), channel_id=1, replica_groups=mesh['z'=8,'y'=8,'x'=4,'c'=2] {'x','c'}, dimensions={1}, use_global_device_ids=true | all-gather | bytes 589824 | tf_op jit(solution)/shard_map/all_gather | solution.py:269
  92.8 2.9 %shard_map.82 = (f32[2,32,256]{2,1,0:T(8,128)}, f32[16,32,256]{2,1,0:T(8,128)S(1)}) custom-call(s32[37]{0:T(128)S(1)} %get-tuple-element.13.table_ref, f32[2,256,256]{2,1,0:T(8,128)S(1)} %all_gather.7.whole_ref, f32[2,256,256]{2,1,0:T(8,128)S(1)} %bitcast.6, f32[2,256,256]{2,1,0:T(8,128)S(1)} %get-tuple-element.16.right_ref, f32[2,32,256]{2,1,0:T(8,128)S(1)} %bitcast.8), custom_call_target="tpu_custom_call" | custom-call | tf_op jit(solution)/shard_map/pallas_call | solution.py:38
  95.6 15.7 %all_to_all.27.got_ref = f32[16,32,256]{2,1,0:T(8,128)S(1)} all-to-all(f32[16,32,256]{2,1,0:T(8,128)S(1)} %get-tuple-element.17), channel_id=1, replica_groups={{0,8,16,24,32,40,48,56},{64,72,80,88,96,104,112,120},{128,136,144,152,1..., dimensions={0} | all-to-all | bytes 1048576 | tf_op jit(solution)/shard_map/all_to_all | solution.py:256
  111.3 0.6 shard_map.83
  111.9 12.9 %all_to_all.28 = f32[8,32,256]{2,1,0:T(8,128)S(1)} all-to-all(f32[8,32,256]{2,1,0:T(8,128)S(1)} %shard_map.83), channel_id=1, replica_groups={{0,64,128,192,256,320,384,448},{8,72,136,200,264,328,392,456},{16,80,14..., dimensions={0} | all-to-all | bytes 524288 | tf_op jit(solution)/shard_map/all_to_all | solution.py:256
  124.8 0.6 constant_dynamic-slice_fusion
  (1 shorter events, 0.0 us)
Async XLA Ops:
  3.4 7.9 %copy-start = (f32[1,2,256,256]{3,2,1,0:T(8,128)S(1)}, f32[1,2,256,256]{3,2,1,0:T(8,128)}, u32[]{:S(2)}) copy-start(f32[1,2,256,256]{3,2,1,0:T(8,128)} %param.8) | copy-start | bytes 1572868
  3.4 7.9 %copy-start.2 = (s32[64]{0:T(128)S(1)}, s32[64]{0:T(128)}, u32[]{:S(2)}) copy-start(s32[64]{0:T(128)} %owner_ref.1) | copy-start | bytes 772
  3.4 10.9 %copy-start.3 = (f32[1,2,32,256]{3,2,1,0:T(8,128)S(1)}, f32[1,2,32,256]{3,2,1,0:T(8,128)}, u32[]{:S(2)}) copy-start(f32[1,2,32,256]{3,2,1,0:T(8,128)} %param.7) | copy-start | bytes 196612
  3.4 37.5 %all-to-all-start = ((f32[64,32,256]{2,1,0:T(8,128)}), f32[64,32,256]{2,1,0:T(8,128)S(1)}, u32[]{:S(2)}, u32[]{:S(2)}) async-start(f32[64,32,256]{2,1,0:T(8,128)} %shard_map.77), calls=%async_computation | async-start | bytes 4194304 | tf_op jit(solution)/shard_map/all_to_all | solution.py:256
  42.0 50.8 %copy-start.1 = (f32[1,2,32,256]{3,2,1,0:T(8,128)S(1)}, f32[1,2,32,256]{3,2,1,0:T(8,128)}, u32[]{:S(2)}) copy-start(f32[1,2,32,256]{3,2,1,0:T(8,128)} %param.9) | copy-start | bytes 196612

commit v10 on v9

--- a/solution.py
+++ b/solution.py
@@ -214,19 +214,43 @@
     return jnp.dot(a, b, precision=lax.Precision.HIGHEST, preferred_element_type=jnp.float32)
 
 
-def step(whole, lefts, rights, moment, table, times):
+def right_half(own, rights):
+    slots, order = rights.shape[0], rights.shape[2]
+    chips, rows = own.shape[0] // slots, own.shape[1]
+
+    def body(own_ref, right_ref, out_ref):
+        for s in range(slots):
+            half = jnp.concatenate([own_ref[x * slots + s] for x in range(chips)], axis=0)
+            out_ref[s] = product(half, right_ref[s]).reshape(chips, rows, order)
+
+    return pl.pallas_call(
+        body,
+        out_shape=jax.ShapeDtypeStruct((slots, chips, rows, order), own.dtype),
+        in_specs=[VMEM, VMEM],
+        out_specs=VMEM,
+        cost_estimate=pl.CostEstimate(flops=2 * slots * chips * rows * order * order * 6, bytes_accessed=2**20, transcendentals=0),
+        compiler_params=pltpu.CompilerParams(vmem_limit_bytes=24 * 2**20),
+    )(own, rights)
+
+
+def step(own, ready, other, lefts, rights, moment, table, times):
     slots, rows, order = moment.shape
-
-    def body(table_ref, whole_ref, left_ref, right_ref, moment_ref, moment_out_ref, send_ref, pre_ref):
-        held = table_ref[COUNT]
+    chips = own.shape[0] // slots
+
+    def body(table_ref, own_ref, ready_ref, other_ref, left_ref, right_ref, moment_ref, moment_out_ref, send_ref, pre_ref, right_part_ref):
+        held, core = table_ref[COUNT], table_ref[ROWS] & 1
         mine = pl.ds(pl.multiple_of(table_ref[ROWS] * rows, rows), rows)
         for s in range(slots):
-            gradient = whole_ref[s]
-            right_part = product(gradient, right_ref[s])
-            precond = product(left_ref[s], right_part)
+            here = jnp.concatenate([own_ref[x * slots + s] for x in range(chips)], axis=0)
+            there = jnp.concatenate([other_ref[x * slots + s] for x in range(chips)], axis=0)
+            rest = product(there, right_ref[s]).reshape(chips, rows, order)
+            for x in range(chips):
+                right_part_ref[s, 2 * x + core] = ready_ref[s, x]
+                right_part_ref[s, 2 * x + 1 - core] = rest[x]
+            precond = product(left_ref[s], right_part_ref[s].reshape(order, order))
             pre_ref[s] = precond
             entries = order * order
-            grad_mean = jnp.sum(gradient * gradient, keepdims=True) / entries
+            grad_mean = jnp.sum(here * here + there * there, keepdims=True) / entries
             pre_mean = jnp.sum(precond * precond, keepdims=True) / entries
             graft = jnp.sqrt(grad_mean) / jnp.sqrt(pre_mean + EPS)
             direction = graft * pre_ref[s, mine]
@@ -241,16 +265,25 @@
         jax.ShapeDtypeStruct(moment.shape, moment.dtype),
         jax.ShapeDtypeStruct((times * slots, rows, order), moment.dtype),
     )
-    scratch = [pltpu.VMEM((slots, order, order), moment.dtype)]
-    return local_call(
-        body, outs, [SMEM, VMEM, VMEM, VMEM, VMEM], (table, whole, lefts, rights, moment), None, scratch
-    )
+    scratch = [
+        pltpu.VMEM((slots, order, order), moment.dtype),
+        pltpu.VMEM((slots, order // rows, rows, order), moment.dtype),
+    ]
+    ins = [SMEM] + [VMEM] * 6
+    return local_call(body, outs, ins, (table, own, ready, other, lefts, rights, moment), None, scratch)
 
 
 def make(sizes):
     side = sizes[0]
     first_lines = lines(sizes, ("y", "z"))
     second_lines = lines(sizes, ("z", "y"))
+
+    chip_lines = [
+        [device(z, y, x, c, sizes) for x in range(sizes[2])]
+        for z in range(sizes[0])
+        for y in range(sizes[1])
+        for c in range(sizes[3])
+    ]
 
     def exchange(blocks, groups):
         return lax.all_to_all(blocks, AXES, 0, 0, tiled=True, axis_index_groups=groups)
@@ -265,9 +298,10 @@
         got, (lefts, rights, table, source) = lax.optimization_barrier((got, early))
         got = exchange(sum_and_pick(got, table, TWO, side * slots, side), second_lines)
         got = exchange(sum_and_pick_here(got, table, THREE, side, side), first_lines)
-        gradient = pick_and_repeat(got, table, OWN, slots, 1)
-        whole = lax.all_gather(gradient, ("x", "c"), axis=1, tiled=True)
-        new_moment, send = step(whole, lefts, rights, momentum[0], table, side)
+        own = exchange(pick_and_repeat(got, table, OWN, slots, sizes[2]), chip_lines)
+        other = lax.ppermute(own, "c", [(0, 1), (1, 0)])
+        ready = right_half(own, rights)
+        new_moment, send = step(own, ready, other, lefts, rights, momentum[0], table, side)
         got = exchange(send, first_lines)
         got = exchange(pick_and_repeat(got, table, BACK, side, 1), second_lines)
         zero = jnp.uint32(0)

time: 126 us -> 126 us (level)
  blocking collectives: 92 us -> 88.7 us
  starting transfers between devices: 7.24 us -> 9.15 us
    all_gather x1 -> x0, blocking collectives: 13.2 us -> none  [on_device(): whole = lax.all_gather(gradient, ('x', 'c'), axis=1, tiled=True)]
    all_to_all x4 -> x5, blocking collectives: 65 us -> 74.8 us  [exchange(): lax.all_to_all(blocks, AXES, 0, 0, tiled=True, axis_index_groups=groups)]
    ppermute x0 -> x1, starting transfers between devices: none -> 1.91 us  [on_device(): other = lax.ppermute(own, 'c', [(0, 1), (1, 0)])]
  transfers between devices with their start and end apart: 1 -> 2, of which waited for: 1 -> 2; matrix products, arithmetic and copies ran while one was open for 0% -> 0% of each run, Pallas kernels for 1% -> 2%
where the time goes in v10:
time: 126 us; the launch traced here: 125 us
  blocking collectives  88.7 us (70%)
  waiting for transfers between devices  13.8 us (11%)
  Pallas kernels  10.3 us (8%)
  starting transfers between devices  9.15 us (7%)
  between operations  2.06 us (2%)
    all_to_all x5, blocking collectives, exchange(): lax.all_to_all(blocks, AXES, 0, 0, tiled=True, axis_index_groups=groups)  74.8 us
    all_gather x1, blocking collectives, on_device(): lefts = lax.all_gather(left_root[0], ('x', 'c'), axis=1, tiled=True)  13.9 us
    all_to_all x1, waiting for transfers between devices, exchange(): lax.all_to_all(blocks, AXES, 0, 0, tiled=True, axis_index_groups=groups)  12.8 us
    pallas_call x7, Pallas kernels, local_call(): pl.pallas_call(body, out_shape=outs, in_specs=ins, out_specs=jax.tree.map...  9.9 us
    all_to_all x1, starting transfers between devices, exchange(): lax.all_to_all(blocks, AXES, 0, 0, tiled=True, axis_index_groups=groups)  7.24 us
  transfers between devices with their start and end apart: 2, of which 2 were waited for; matrix products, arithmetic and copies ran while one was open for 0% of the time, Pallas kernels for 2%

profile of v10, /device:TPU:2, one launch (start us, length us, event | category | flops | bytes accessed | tf_op | source)
XLA Modules:
  0.0 125.3 jit_solution(5246343545862470709)
XLA Ops:
  0.6 2.7 %shard_map.77 = f32[64,32,256]{2,1,0:T(8,128)} custom-call(s32[64]{0:T(128)} %owner_ref.1, f32[64,32,256]{2,1,0:T(8,128)} %bitcast.9), custom_call_target="tpu_custom_call" | custom-call | tf_op jit(solution)/shard_map/pallas_call | solution.py:38
  3.4 0.0 copy-start
  3.4 0.0 copy-start.2
  3.4 0.0 copy-start.3
  3.4 7.2 %all-to-all-start = ((f32[64,32,256]{2,1,0:T(8,128)}), f32[64,32,256]{2,1,0:T(8,128)S(1)}, u32[]{:S(2)}, u32[]{:S(2)}) async-start(f32[64,32,256]{2,1,0:T(8,128)} %shard_map.77), calls=%async_computation | async-start | bytes 4194304 | tf_op jit(solution)/shard_map/all_to_all | solution.py:289
  11.3 1.7 %shard_map.78 = (s32[37]{0:T(128)S(1)}, f32[2,256,256]{2,1,0:T(8,128)S(1)}) custom-call(s32[64]{0:T(128)S(1)} %copy-done.2, s32[1]{0:T(128)S(6)} %copy.8.count_ref, f32[2,256,256]{2,1,0:T(8,128)S(1)} %bitcast.7), custom_call_target="tpu_custom_call" | custom-call | tf_op jit(solution)/shard_map/pallas_call | solution.py:38
  13.1 0.6 slice.3
  14.3 13.9 %all-gather = f32[1,2,256,256]{3,2,1,0:T(8,128)S(1)} all-gather(f32[1,2,32,256]{3,2,1,0:T(8,128)S(1)} %copy-done.3), channel_id=2, replica_groups=mesh['z'=8,'y'=8,'x'=4,'c'=2] {'x','c'}, dimensions={2}, use_global_device_ids=true | all-gather | bytes 589824 | tf_op jit(solution)/shard_map/all_gather | solution.py:296
  28.2 12.8 %all-to-all-done.got_ref = f32[64,32,256]{2,1,0:T(8,128)S(1)} async-done(((f32[64,32,256]{2,1,0:T(8,128)}), f32[64,32,256]{2,1,0:T(8,128)S(1)}, u32[]{:S(2)}, u32[]{:S(2)}) %all-to-all-start) | async-done | bytes 2097184 | tf_op jit(solution)/shard_map/all_to_all | solution.py:289
  40.9 1.0 shard_map.79
  42.0 0.0 copy-start.1
  42.0 23.5 %all_to_all.30.got_ref = f32[16,32,256]{2,1,0:T(8,128)S(1)} all-to-all(f32[16,32,256]{2,1,0:T(8,128)S(1)} %shard_map.79), channel_id=1, replica_groups={{0,64,128,192,256,320,384,448},{8,72,136,200,264,328,392,456},{16,80,14..., dimensions={0} | all-to-all | bytes 1048576 | tf_op jit(solution)/shard_map/all_to_all | solution.py:289
  65.5 0.6 shard_map.80
  66.2 12.9 %all_to_all.31.got_ref = f32[8,32,256]{2,1,0:T(8,128)S(1)} all-to-all(f32[8,32,256]{2,1,0:T(8,128)S(1)} %shard_map.80), channel_id=1, replica_groups={{0,8,16,24,32,40,48,56},{64,72,80,88,96,104,112,120},{128,136,144,152,1..., dimensions={0} | all-to-all | bytes 524288 | tf_op jit(solution)/shard_map/all_to_all | solution.py:289
  79.0 0.6 shard_map.81
  79.6 9.8 %all_to_all.32.own_ref = f32[8,32,256]{2,1,0:T(8,128)S(1)} all-to-all(f32[8,32,256]{2,1,0:T(8,128)S(1)} %shard_map.81), channel_id=1, replica_groups={{0,2,4,6},{1,3,5,7},{8,10,12,14},{9,11,13,15},{16,18,20,22},{17,19,21,2..., dimensions={0} | all-to-all | bytes 524288 | tf_op jit(solution)/shard_map/all_to_all | solution.py:289
  89.5 1.9 %collective-permute-start = (f32[8,32,256]{2,1,0:T(8,128)S(1)}, f32[8,32,256]{2,1,0:T(8,128)S(1)}, u32[]{:S(2)}, u32[]{:S(2)}) collective-permute-start(f32[8,32,256]{2,1,0:T(8,128)S(1)} %all_to_all.32.own_ref), channel_id=1, source_target_pairs={{0,1},{1,0},{2,3},{3,2},{4,5},{5,4},{6,7},{7,6},{8,9},{9,8},{10,11... | collective-permute-start | bytes 786440 | tf_op jit(solution)/shard_map/ppermute | solution.py:302
  91.4 0.4 shard_map.82.ready_ref
  91.8 1.0 collective-permute-done.other_ref
  92.9 2.6 %shard_map.83 = (f32[2,32,256]{2,1,0:T(8,128)}, f32[16,32,256]{2,1,0:T(8,128)S(1)}) custom-call(s32[37]{0:T(128)S(1)} %get-tuple-element.13.table_ref, f32[8,32,256]{2,1,0:T(8,128)S(1)} %all_to_all.32.own_ref, f32[2,4,32,256]{3,2,1,0:T(8,128)S(1)} %shard_map.82.ready_ref, f32[8,32,256]{2,1,0:T(8,128)S(1)} %collective-permute-done.other_ref, ...), custom_call_target="tpu_custom_call" | custom-call | tf_op jit(solution)/shard_map/pallas_call | solution.py:38
  95.5 15.7 %all_to_all.33.got_ref = f32[16,32,256]{2,1,0:T(8,128)S(1)} all-to-all(f32[16,32,256]{2,1,0:T(8,128)S(1)} %get-tuple-element.17), channel_id=1, replica_groups={{0,8,16,24,32,40,48,56},{64,72,80,88,96,104,112,120},{128,136,144,152,1..., dimensions={0} | all-to-all | bytes 1048576 | tf_op jit(solution)/shard_map/all_to_all | solution.py:289
  111.2 0.6 shard_map.84
  111.8 12.9 %all_to_all.34 = f32[8,32,256]{2,1,0:T(8,128)S(1)} all-to-all(f32[8,32,256]{2,1,0:T(8,128)S(1)} %shard_map.84), channel_id=1, replica_groups={{0,64,128,192,256,320,384,448},{8,72,136,200,264,328,392,456},{16,80,14..., dimensions={0} | all-to-all | bytes 524288 | tf_op jit(solution)/shard_map/all_to_all | solution.py:289
  124.7 0.6 constant_dynamic-slice_fusion
  (4 shorter events, 0.0 us)
Async XLA Ops:
  3.4 7.9 %copy-start = (f32[1,2,256,256]{3,2,1,0:T(8,128)S(1)}, f32[1,2,256,256]{3,2,1,0:T(8,128)}, u32[]{:S(2)}) copy-start(f32[1,2,256,256]{3,2,1,0:T(8,128)} %param.8) | copy-start | bytes 1572868
  3.4 7.9 %copy-start.2 = (s32[64]{0:T(128)S(1)}, s32[64]{0:T(128)}, u32[]{:S(2)}) copy-start(s32[64]{0:T(128)} %owner_ref.1) | copy-start | bytes 772
  3.4 10.9 %copy-start.3 = (f32[1,2,32,256]{3,2,1,0:T(8,128)S(1)}, f32[1,2,32,256]{3,2,1,0:T(8,128)}, u32[]{:S(2)}) copy-start(f32[1,2,32,256]{3,2,1,0:T(8,128)} %param.7) | copy-start | bytes 196612
  3.4 37.5 %all-to-all-start = ((f32[64,32,256]{2,1,0:T(8,128)}), f32[64,32,256]{2,1,0:T(8,128)S(1)}, u32[]{:S(2)}, u32[]{:S(2)}) async-start(f32[64,32,256]{2,1,0:T(8,128)} %shard_map.77), calls=%async_computation | async-start | bytes 4194304 | tf_op jit(solution)/shard_map/all_to_all | solution.py:289
  42.0 50.9 %copy-start.1 = (f32[1,2,32,256]{3,2,1,0:T(8,128)S(1)}, f32[1,2,32,256]{3,2,1,0:T(8,128)}, u32[]{:S(2)}) copy-start(f32[1,2,32,256]{3,2,1,0:T(8,128)} %param.9) | copy-start | bytes 196612
  89.5 3.4 %collective-permute-start = (f32[8,32,256]{2,1,0:T(8,128)S(1)}, f32[8,32,256]{2,1,0:T(8,128)S(1)}, u32[]{:S(2)}, u32[]{:S(2)}) collective-permute-start(f32[8,32,256]{2,1,0:T(8,128)S(1)} %all_to_all.32.own_ref), channel_id=1, source_target_pairs={{0,1},{1,0},{2,3},{3,2},{4,5},{5,4},{6,7},{7,6},{8,9},{9,8},{10,11... | collective-permute-start | bytes 786440 | tf_op jit(solution)/shard_map/ppermute | solution.py:302

commit v11 on v10

--- a/solution.py
+++ b/solution.py
@@ -210,8 +210,18 @@
     return local_call(body, out, [SMEM, VMEM], (table, got))
 
 
+def halves(a):
+    high = a.astype(jnp.bfloat16)
+    return high, (a - high.astype(jnp.float32)).astype(jnp.bfloat16)
+
+
 def product(a, b):
-    return jnp.dot(a, b, precision=lax.Precision.HIGHEST, preferred_element_type=jnp.float32)
+    (ah, al), (bh, bl) = halves(a), halves(b)
+
+    def dot(p, q):
+        return jnp.dot(p, q, preferred_element_type=jnp.float32)
+
+    return dot(ah, bh) + (dot(ah, bl) + dot(al, bh))
 
 
 def right_half(own, rights):

time: 126 us -> 125 us (level)
  no operation moved by 1% of the time
where the time goes in v11:
time: 125 us
  blocking collectives  88.7 us (71%)
  waiting for transfers between devices  13.9 us (11%)
  Pallas kernels  9.64 us (8%)
  starting transfers between devices  9.15 us (7%)
  between operations  2.06 us (2%)
    all_to_all x5, blocking collectives, exchange(): lax.all_to_all(blocks, AXES, 0, 0, tiled=True, axis_index_groups=groups)  74.8 us
    all_gather x1, blocking collectives, on_device(): lefts = lax.all_gather(left_root[0], ('x', 'c'), axis=1, tiled=True)  13.9 us
    all_to_all x1, waiting for transfers between devices, exchange(): lax.all_to_all(blocks, AXES, 0, 0, tiled=True, axis_index_groups=groups)  12.7 us
    pallas_call x7, Pallas kernels, local_call(): pl.pallas_call(body, out_shape=outs, in_specs=ins, out_specs=jax.tree.map...  9.34 us
    all_to_all x1, starting transfers between devices, exchange(): lax.all_to_all(blocks, AXES, 0, 0, tiled=True, axis_index_groups=groups)  7.24 us
  transfers between devices with their start and end apart: 2, of which 2 were waited for; matrix products, arithmetic and copies ran while one was open for 0% of the time, Pallas kernels for 2%

profile of v11, /device:TPU:2, one launch (start us, length us, event | category | flops | bytes accessed | tf_op | source)
XLA Modules:
  0.0 124.7 jit_solution(4715815322188169083)
XLA Ops:
  0.6 2.7 %shard_map.77 = f32[64,32,256]{2,1,0:T(8,128)} custom-call(s32[64]{0:T(128)} %owner_ref.1, f32[64,32,256]{2,1,0:T(8,128)} %bitcast.9), custom_call_target="tpu_custom_call" | custom-call | tf_op jit(solution)/shard_map/pallas_call | solution.py:38
  3.4 0.0 copy-start
  3.4 0.0 copy-start.2
  3.4 0.0 copy-start.3
  3.4 7.2 %all-to-all-start = ((f32[64,32,256]{2,1,0:T(8,128)}), f32[64,32,256]{2,1,0:T(8,128)S(1)}, u32[]{:S(2)}, u32[]{:S(2)}) async-start(f32[64,32,256]{2,1,0:T(8,128)} %shard_map.77), calls=%async_computation | async-start | bytes 4194304 | tf_op jit(solution)/shard_map/all_to_all | solution.py:299
  11.3 1.7 %shard_map.78 = (s32[37]{0:T(128)S(1)}, f32[2,256,256]{2,1,0:T(8,128)S(1)}) custom-call(s32[64]{0:T(128)S(1)} %copy-done.2, s32[1]{0:T(128)S(6)} %copy.8.count_ref, f32[2,256,256]{2,1,0:T(8,128)S(1)} %bitcast.7), custom_call_target="tpu_custom_call" | custom-call | tf_op jit(solution)/shard_map/pallas_call | solution.py:38
  13.1 0.6 slice.3
  14.3 13.9 %all-gather = f32[1,2,256,256]{3,2,1,0:T(8,128)S(1)} all-gather(f32[1,2,32,256]{3,2,1,0:T(8,128)S(1)} %copy-done.3), channel_id=2, replica_groups=mesh['z'=8,'y'=8,'x'=4,'c'=2] {'x','c'}, dimensions={2}, use_global_device_ids=true | all-gather | bytes 589824 | tf_op jit(solution)/shard_map/all_gather | solution.py:306
  28.2 12.7 %all-to-all-done.got_ref = f32[64,32,256]{2,1,0:T(8,128)S(1)} async-done(((f32[64,32,256]{2,1,0:T(8,128)}), f32[64,32,256]{2,1,0:T(8,128)S(1)}, u32[]{:S(2)}, u32[]{:S(2)}) %all-to-all-start) | async-done | bytes 2097184 | tf_op jit(solution)/shard_map/all_to_all | solution.py:299
  40.9 1.0 shard_map.79
  42.0 0.0 copy-start.1
  42.0 23.5 %all_to_all.30.got_ref = f32[16,32,256]{2,1,0:T(8,128)S(1)} all-to-all(f32[16,32,256]{2,1,0:T(8,128)S(1)} %shard_map.79), channel_id=1, replica_groups={{0,64,128,192,256,320,384,448},{8,72,136,200,264,328,392,456},{16,80,14..., dimensions={0} | all-to-all | bytes 1048576 | tf_op jit(solution)/shard_map/all_to_all | solution.py:299
  65.5 0.6 shard_map.80
  66.2 12.9 %all_to_all.31.got_ref = f32[8,32,256]{2,1,0:T(8,128)S(1)} all-to-all(f32[8,32,256]{2,1,0:T(8,128)S(1)} %shard_map.80), channel_id=1, replica_groups={{0,8,16,24,32,40,48,56},{64,72,80,88,96,104,112,120},{128,136,144,152,1..., dimensions={0} | all-to-all | bytes 524288 | tf_op jit(solution)/shard_map/all_to_all | solution.py:299
  79.0 0.6 shard_map.81
  79.6 9.8 %all_to_all.32.own_ref = f32[8,32,256]{2,1,0:T(8,128)S(1)} all-to-all(f32[8,32,256]{2,1,0:T(8,128)S(1)} %shard_map.81), channel_id=1, replica_groups={{0,2,4,6},{1,3,5,7},{8,10,12,14},{9,11,13,15},{16,18,20,22},{17,19,21,2..., dimensions={0} | all-to-all | bytes 524288 | tf_op jit(solution)/shard_map/all_to_all | solution.py:299
  89.5 1.9 %collective-permute-start = (f32[8,32,256]{2,1,0:T(8,128)S(1)}, f32[8,32,256]{2,1,0:T(8,128)S(1)}, u32[]{:S(2)}, u32[]{:S(2)}) collective-permute-start(f32[8,32,256]{2,1,0:T(8,128)S(1)} %all_to_all.32.own_ref), channel_id=1, source_target_pairs={{0,1},{1,0},{2,3},{3,2},{4,5},{5,4},{6,7},{7,6},{8,9},{9,8},{10,11... | collective-permute-start | bytes 786440 | tf_op jit(solution)/shard_map/ppermute | solution.py:312
  91.4 0.3 shard_map.82.ready_ref
  91.7 1.2 collective-permute-done.other_ref
  92.9 2.1 %shard_map.83 = (f32[2,32,256]{2,1,0:T(8,128)}, f32[16,32,256]{2,1,0:T(8,128)S(1)}) custom-call(s32[37]{0:T(128)S(1)} %get-tuple-element.13.table_ref, f32[8,32,256]{2,1,0:T(8,128)S(1)} %all_to_all.32.own_ref, f32[2,4,32,256]{3,2,1,0:T(8,128)S(1)} %shard_map.82.ready_ref, f32[8,32,256]{2,1,0:T(8,128)S(1)} %collective-permute-done.other_ref, ...), custom_call_target="tpu_custom_call" | custom-call | tf_op jit(solution)/shard_map/pallas_call | solution.py:38
  95.0 15.7 %all_to_all.33.got_ref = f32[16,32,256]{2,1,0:T(8,128)S(1)} all-to-all(f32[16,32,256]{2,1,0:T(8,128)S(1)} %get-tuple-element.17), channel_id=1, replica_groups={{0,8,16,24,32,40,48,56},{64,72,80,88,96,104,112,120},{128,136,144,152,1..., dimensions={0} | all-to-all | bytes 1048576 | tf_op jit(solution)/shard_map/all_to_all | solution.py:299
  110.7 0.6 shard_map.84
  111.2 12.9 %all_to_all.34 = f32[8,32,256]{2,1,0:T(8,128)S(1)} all-to-all(f32[8,32,256]{2,1,0:T(8,128)S(1)} %shard_map.84), channel_id=1, replica_groups={{0,64,128,192,256,320,384,448},{8,72,136,200,264,328,392,456},{16,80,14..., dimensions={0} | all-to-all | bytes 524288 | tf_op jit(solution)/shard_map/all_to_all | solution.py:299
  124.1 0.6 constant_dynamic-slice_fusion
  (4 shorter events, 0.0 us)
Async XLA Ops:
  3.4 7.9 %copy-start = (f32[1,2,256,256]{3,2,1,0:T(8,128)S(1)}, f32[1,2,256,256]{3,2,1,0:T(8,128)}, u32[]{:S(2)}) copy-start(f32[1,2,256,256]{3,2,1,0:T(8,128)} %param.8) | copy-start | bytes 1572868
  3.4 7.9 %copy-start.2 = (s32[64]{0:T(128)S(1)}, s32[64]{0:T(128)}, u32[]{:S(2)}) copy-start(s32[64]{0:T(128)} %owner_ref.1) | copy-start | bytes 772
  3.4 10.9 %copy-start.3 = (f32[1,2,32,256]{3,2,1,0:T(8,128)S(1)}, f32[1,2,32,256]{3,2,1,0:T(8,128)}, u32[]{:S(2)}) copy-start(f32[1,2,32,256]{3,2,1,0:T(8,128)} %param.7) | copy-start | bytes 196612
  3.4 37.5 %all-to-all-start = ((f32[64,32,256]{2,1,0:T(8,128)}), f32[64,32,256]{2,1,0:T(8,128)S(1)}, u32[]{:S(2)}, u32[]{:S(2)}) async-start(f32[64,32,256]{2,1,0:T(8,128)} %shard_map.77), calls=%async_computation | async-start | bytes 4194304 | tf_op jit(solution)/shard_map/all_to_all | solution.py:299
  42.0 50.9 %copy-start.1 = (f32[1,2,32,256]{3,2,1,0:T(8,128)S(1)}, f32[1,2,32,256]{3,2,1,0:T(8,128)}, u32[]{:S(2)}) copy-start(f32[1,2,32,256]{3,2,1,0:T(8,128)} %param.9) | copy-start | bytes 196612
  89.5 3.4 %collective-permute-start = (f32[8,32,256]{2,1,0:T(8,128)S(1)}, f32[8,32,256]{2,1,0:T(8,128)S(1)}, u32[]{:S(2)}, u32[]{:S(2)}) collective-permute-start(f32[8,32,256]{2,1,0:T(8,128)S(1)} %all_to_all.32.own_ref), channel_id=1, source_target_pairs={{0,1},{1,0},{2,3},{3,2},{4,5},{5,4},{6,7},{7,6},{8,9},{9,8},{10,11... | collective-permute-start | bytes 786440 | tf_op jit(solution)/shard_map/ppermute | solution.py:312
